TPU v7x, 32 devices: a whole 2x2x4 slice. The times are simulated.
32 devices in a mesh: aux: 4 (over x, core), orb: 8 (over z, y).
Axes of the slice: x: 2, y: 2, z: 4, core: 2. Of those that a mesh axis runs over, the one named last changes fastest.
Arguments:
- three_center: float32 [16, 8, 128, 1024], P('aux', 'orb'), may hold values from -6 to 6
- tile_lists: int32 [2, 4, 8, 8], P(None, 'aux'), may hold values from -1 to 7, as said below
- occ_density: float32 [2, 1024, 1024], P(None, 'orb', 'aux'), may hold values from -0.1875 to 0.1875
- vir_density: float32 [2, 1024, 1024], P(None, 'orb', 'aux'), may hold values from -0.1875 to 0.1875
Outputs:
- coupled: float32 [2, 16, 8, 1024, 128], P(None, 'aux', 'orb')
Inputs may be any that keep to these rules, and one draw needn't show every extreme that they name: Row m of tile_lists[t, j] names distinct orbital blocks in rising order, block m always among them, and -1 in the remaining places; it names between 2 and 8 blocks, and for every t and j one row names all 8 and another exactly 2.
All inputs are finite; a program needn't handle non-finite values.
Results may differ from a plain program's by a relative error of at most 0.0003.
Values sent between devices are 32-bit elements; how exact they have to be, the bound alone decides.
No kernel may reach another device: no remote copies, remote signals or barrier semaphores. Data moves between devices by JAX's collectives and lax.ppermute only.
A program may use at most 64 MiB of HBM per device.

v0:
```python
import jax
import jax.numpy as jnp
from jax import lax
from jax.sharding import PartitionSpec as P


def listed_mask(tile_lists, part_index, block_index):
    block_table = lax.dynamic_index_in_dim(tile_lists, part_index, 1, keepdims=False)
    listed_row = lax.dynamic_index_in_dim(block_table, block_index, 1, keepdims=False)
    block_count = tile_lists.shape[3]
    block_ids = jnp.arange(block_count, dtype=jnp.int32)
    matches = listed_row[:, :, None] == block_ids[None, None, :]
    return jnp.sum(matches.astype(jnp.float32), axis=1)


def masked_rows(integrals, listed_now):
    aux_count, block_size, orbitals = integrals.shape
    block_count = orbitals // block_size
    viewed = integrals.reshape(aux_count, block_size, block_count, block_size)
    masked = viewed[None] * listed_now[:, None, None, :, None]
    return masked.reshape(listed_now.shape[0], aux_count * block_size, orbitals)


def make_adder(masked, density_rows):
    return jnp.einsum("tar,trl->tal", masked, density_rows, precision=lax.Precision.HIGHEST)


def make_applier(column_data, density_rows):
    return jnp.einsum("tsk,takl->tasl", density_rows, column_data, precision=lax.Precision.HIGHEST)


def outgoing(product, listed_now, aux_count, block_size, block_count, split_count):
    time_count = product.shape[0]
    aux_share = aux_count // split_count
    pruned = product.reshape(time_count, aux_count, block_size, block_count, block_size)
    pruned = pruned * listed_now[:, None, None, :, None]
    split_view = pruned.reshape(
        time_count, split_count, aux_share, block_size, block_count, block_size
    )
    ordered = split_view.transpose(4, 1, 0, 2, 3, 5)
    return ordered.reshape(block_count * split_count, time_count, aux_share, block_size, block_size)


def make_arrange(block_count, split_count):

    def arrange(received):
        unit_count, time_count, item_count, row_count, col_count = received.shape
        grouped = received.reshape(
            block_count, split_count, time_count, item_count, row_count, col_count
        )
        reordered = grouped.transpose(2, 1, 3, 0, 4, 5)
        return reordered.reshape(
            time_count, split_count, item_count, block_count * row_count, col_count
        )

    return arrange


def local(three_center, tile_lists, occ_density, vir_density):
    aux_count = three_center.shape[0]
    block_size = three_center.shape[2]
    orbitals = three_center.shape[3]
    block_count = orbitals // block_size
    owners = lax.axis_size("orb")
    split_count = owners // block_count
    owner_unit = lax.axis_index("orb")
    block_index = owner_unit // split_count
    part_index = owner_unit % split_count
    listed = listed_mask(tile_lists, part_index, block_index)
    integrals = three_center[:, 0]
    arrange = make_arrange(block_count, split_count)
    occ_cols, vir_cols = (
        lax.all_gather(occ_density, "aux", axis=2, tiled=True),
        lax.all_gather(vir_density, "aux", axis=2, tiled=True),
    )
    time_count = occ_cols.shape[0]
    masked = masked_rows(integrals, listed)
    product = make_adder(masked, lax.all_gather(occ_cols, "orb", axis=1, tiled=True))
    sending = outgoing(product, listed, aux_count, block_size, block_count, split_count)
    column_data = arrange(lax.all_to_all(sending, "orb", split_axis=0, concat_axis=0, tiled=True))
    column_data = column_data.reshape(time_count, aux_count, orbitals, block_size)
    coupled = make_applier(column_data, lax.all_gather(vir_cols, "orb", axis=1, tiled=True))
    return coupled[:, :, None]


def solution(mesh):
    in_specs = (
        P("aux", "orb", None, None),
        P(None, "aux", None, None),
        P(None, "orb", "aux"),
        P(None, "orb", "aux"),
    )
    out_specs = P(None, "aux", "orb", None, None)
    return jax.shard_map(local, mesh=mesh, in_specs=in_specs, out_specs=out_specs, check_vma=False)
```

profile of v0, /device:TPU:0, one launch (start us, length us, event | category | flops | bytes accessed | tf_op | source)
XLA Modules:
  0.0 414.8 jit_solution(10929656270472314241)
XLA Ops:
  6.5 0.0 copy-start
  6.5 0.0 copy-start.1
  6.5 0.0 all-gather.5.cloned.1.call-start
  6.5 0.7 all-gather.5.cloned.1.call-update
  7.3 0.0 all-gather.9.cloned.1.call-start
  7.3 0.7 all-gather.9.cloned.1.call-update
  8.0 0.0 all-gather.7.cloned.1.call-start
  8.1 20.3 %all-gather.5.cloned.1.call-done = f32[2,128,1024]{2,1,0:T(8,128)} async-done(((f32[2,128,256]{2,1,0:T(8,128)}), f32[2,128,1024]{2,1,0:T(8,128)}) %all-gather.5.cloned.1.call-update) | async-done | bytes 1048592 | tf_op jit(solution)/shard_map/all_gather | solution.py:73
  28.4 0.0 all-gather.7.cloned.1.call-update
  28.4 0.0 all-gather.11.cloned.1.call-start
  28.4 18.2 %all-gather.9.cloned.1.call-done = f32[2,128,1024]{2,1,0:T(8,128)} async-done(((f32[2,128,256]{2,1,0:T(8,128)}), f32[2,128,1024]{2,1,0:T(8,128)}) %all-gather.9.cloned.1.call-update) | async-done | bytes 1048592 | tf_op jit(solution)/shard_map/all_gather | solution.py:74
  46.7 0.0 all-gather.11.cloned.1.call-update
  46.7 0.0 copy-done
  46.7 0.1 convert_reduce_fusion
  46.8 0.1 copy.11
  46.9 0.1 broadcast_bitcast_fusion
  47.0 126.8 %all-gather.7.cloned.1.call-done = f32[2,1024,1024]{2,1,0:T(8,128)} async-done(((f32[2,128,1024]{2,1,0:T(8,128)}), f32[2,1024,1024]{2,1,0:T(8,128)}) %all-gather.7.cloned.1.call-update) | async-done | bytes 8388624 | tf_op jit(solution)/shard_map/all_gather | solution.py:78
  173.8 0.0 copy-done.1
  173.8 16.0 %fusion.3 = f32[2,512,1024]{2,1,0:T(8,128)S(1)} fusion(f32[2,1024,1024]{2,1,0:T(8,128)} %all-gather.7.cloned.1.call-done, f32[2,1024]{1,0:T(2,128)S(1)} %bitcast.40, f32[512,1024]{1,0:T(8,128)S(1)} %bitcast.39), kind=kOutput, calls=%fused_computation.4 | convolution fusion | flops 12885950464 | bytes 14688256 | tf_op jit(solution)/shard_map/tar,trl->tal/dot_general | solution.py:25
  189.9 1.0 copy.17
  190.9 0.8 fusion.2
  191.7 183.1 %all_to_all.5 = f32[8,2,4,128,128]{4,3,2,1,0:T(8,128)} all-to-all(f32[8,2,4,128,128]{4,3,2,1,0:T(8,128)S(1)} %fusion.2), channel_id=1, replica_groups=mesh['aux'=4,'orb'=8] {'orb'}, dimensions={0} | all-to-all | bytes 8388608 | tf_op jit(solution)/shard_map/all_to_all | solution.py:80
  374.8 5.2 %copy.13 = f32[2,1,4,8,128,128]{4,3,5,2,0,1:T(8,128)} copy(f32[2,1,4,8,128,128]{5,4,2,0,3,1:T(8,128)} %bitcast.37) | data formatting | bytes 8388608 | tf_op jit(solution)/shard_map/transpose | solution.py:51
  380.1 4.9 %reshape_reshape.3 = f32[2,4,1024,128]{2,3,1,0:T(8,128)} reshape(f32[2,1,4,8,128,128]{4,3,5,2,0,1:T(8,128)} %copy.13) | data formatting | bytes 8388608 | tf_op jit(solution)/shard_map/reshape;reshape | solution.py:81
  385.0 0.0 all-gather.11.cloned.1.call-done
  385.0 18.0 %fusion.5 = f32[2,4,1,1024,128]{3,4,1,0,2:T(8,128)} fusion(f32[2,4,1024,128]{2,3,1,0:T(8,128)} %reshape_reshape.3, f32[2,1024,1024]{2,1,0:T(8,128)} %all-gather.11.cloned.1.call-done), kind=kOutput, calls=%fused_computation.6 | convolution fusion | flops 12884901888 | bytes 16777216 | tf_op jit(solution)/shard_map/tsk,takl->tasl/dot_general | solution.py:29
  402.9 5.3 %copy.14 = f32[2,4,1,1024,128]{4,3,2,1,0:T(8,128)} copy(f32[2,4,1,1024,128]{3,4,1,0,2:T(8,128)} %fusion.5) | data formatting | bytes 8388608 | tf_op jit(solution)/shard_map/broadcast_in_dim | solution.py:83
  (2 shorter events, 0.0 us)
Async XLA Ops:
  6.5 40.2 %copy-start = (s32[2,1,8,8]{3,2,1,0:T(8,128)S(1)}, s32[2,1,8,8]{3,2,1,0:T(8,128)}, u32[]{:S(2)}) copy-start(s32[2,1,8,8]{3,2,1,0:T(8,128)} %param.5) | copy-start | bytes 1540
  6.5 167.3 %copy-start.1 = (f32[4,1,128,1024]{3,2,1,0:T(8,128)S(1)}, f32[4,1,128,1024]{3,2,1,0:T(8,128)}, u32[]{:S(2)}) copy-start(f32[4,1,128,1024]{3,2,1,0:T(8,128)} %param.4) | copy-start | bytes 6291460
  6.5 21.8 %all-gather.5.cloned.1.call-start = ((), (), s32[]{:S(2)}) async-start(), calls=%async_computation.1 | async-start | bytes 1310720 | tf_op jit(solution)/shard_map/all_gather | solution.py:73
  7.3 39.4 %all-gather.9.cloned.1.call-start = ((), (), s32[]{:S(2)}) async-start(), calls=%async_computation.3 | async-start | bytes 1310720 | tf_op jit(solution)/shard_map/all_gather | solution.py:74
  8.0 165.8 %all-gather.7.cloned.1.call-start = ((), (), s32[]{:S(2)}) async-start(), calls=%async_computation.2 | async-start | bytes 9437184 | tf_op jit(solution)/shard_map/all_gather | solution.py:78
  28.4 356.6 %all-gather.11.cloned.1.call-start = ((), (), s32[]{:S(2)}) async-start(), calls=%async_computation.4 | async-start | bytes 9437184 | tf_op jit(solution)/shard_map/all_gather | solution.py:82
Sparse Core Ops, SparseCore 0:
  8.9 19.4 all-gather.4
  29.9 16.7 all-gather.8
  48.9 124.9 all-gather.6
  175.9 202.5 all-gather.10
where the time goes:
time: 415 us
  blocking collectives  183 us (44%)
  waiting for transfers between devices  167 us (40%)
  matrix products  34 us (8%)
  local copies, waits for them, and re-layouts  16.7 us (4%)
  between operations  13.2 us (3%)
    all_to_all x1, blocking collectives, local(): lax.all_to_all(sending, 'orb', split_axis=0, concat_axis=0, tiled=True)  183 us
    all_gather x1, waiting for transfers between devices, local(): lax.all_gather(occ_cols, 'orb', axis=1, tiled=True)  127 us
    all_gather x1, waiting for transfers between devices, local(): lax.all_gather(occ_density, 'aux', axis=2, tiled=True)  20.3 us
    all_gather x1, waiting for transfers between devices, local(): lax.all_gather(vir_density, 'aux', axis=2, tiled=True)  18.2 us
    dot_general x1, matrix products, make_applier(): jnp.einsum('tsk,takl->tasl', density_rows, column_data, precision=lax.Pre...  18 us
    dot_general x1, matrix products, make_adder(): jnp.einsum('tar,trl->tal', masked, density_rows, precision=lax.Precision....  16 us
  transfers between devices with their start and end apart: 4, of which 3 were waited for; matrix products, arithmetic and copies ran while one was open for 7% of the time, Pallas kernels for 0%

commit v1 on v0

v1 whole, which is shorter than its diff:
```python
import functools

import jax
import jax.numpy as jnp
from jax import lax
from jax.experimental import pallas as pl
from jax.experimental.pallas import tpu as pltpu
from jax.sharding import PartitionSpec as P

VMEM_BYTES = 56 * 1024 * 1024


def listed_mask(tile_lists, part_index, block_index):
    block_table = lax.dynamic_index_in_dim(tile_lists, part_index, 1, keepdims=False)
    listed_row = lax.dynamic_index_in_dim(block_table, block_index, 1, keepdims=False)
    block_ids = jnp.arange(tile_lists.shape[3], dtype=jnp.int32)
    matches = listed_row[:, :, None] == block_ids[None, None, :]
    return jnp.sum(matches.astype(jnp.float32), axis=1)


def halves(value):
    high = value.astype(jnp.bfloat16)
    return high, (value - high.astype(jnp.float32)).astype(jnp.bfloat16)


def three_products(left_high, left_low, right_high, right_low):
    dot = functools.partial(jnp.dot, preferred_element_type=jnp.float32)
    small = dot(left_low, right_high) + dot(left_high, right_low)
    return dot(left_high, right_high) + small


def exchange(value, aux_bits, orb_bits):
    n_aux, n_orb = lax.axis_size("aux"), lax.axis_size("orb")
    pairs = [
        (a * n_orb + o, (a ^ aux_bits) * n_orb + (o ^ orb_bits))
        for a in range(n_aux)
        for o in range(n_orb)
    ]
    return lax.ppermute(value, ("aux", "orb"), pairs)


def bits_of(size):
    return [1 << at for at in reversed(range(size.bit_length() - 1))]


def gather(value):
    stacked, keys = value[None], [(0, 0)]
    for bit in bits_of(lax.axis_size("orb")):
        stacked = jnp.concatenate([stacked, exchange(stacked, 0, bit)], axis=0)
        keys = keys + [(a, o ^ bit) for a, o in keys]
    gathered = [(stacked, keys)]
    for bit in bits_of(lax.axis_size("aux")):
        gathered = gathered + [
            (exchange(array, bit, 0), [(a ^ bit, o) for a, o in names]) for array, names in gathered
        ]
    return gathered


def place_blocks(position, refs, keys, high_ref, low_ref):
    my_aux, my_orb = position[0], position[1]
    for ref, names in zip(refs, keys):
        rows, cols = ref.shape[1:]
        for at, (aux_bits, orb_bits) in enumerate(names):
            row = pl.multiple_of((my_orb ^ orb_bits) * rows, rows)
            col = pl.multiple_of((my_aux ^ aux_bits) * cols, cols)
            high, low = halves(ref[at])
            high_ref[pl.ds(row, rows), pl.ds(col, cols)] = high
            low_ref[pl.ds(row, rows), pl.ds(col, cols)] = low


def half_kernel(keys, time, split, position, listed, integrals, *rest):
    refs, (out, b_high, b_low, a_high, a_low) = rest[: len(keys)], rest[len(keys) :]
    aux_count, block, orbitals = integrals.shape
    blocks = orbitals // block
    share = aux_count // split
    place_blocks(position, refs, keys, b_high, b_low)
    for n in range(blocks):
        cols = slice(n * block, (n + 1) * block)
        part = integrals[:, :, cols].reshape(aux_count * block, block) * listed[time, n]
        a_high[:, cols], a_low[:, cols] = halves(part)
    width = 2 * block
    for pair in range(blocks // 2):
        cols = slice(pair * width, (pair + 1) * width)
        product = three_products(a_high[...], a_low[...], b_high[:, cols], b_low[:, cols])
        for side in range(2):
            column = pair * 2 + side
            part = product[:, side * block : (side + 1) * block] * listed[time, column]
            part = part.reshape(split, share, block, block)
            for h in range(split):
                out[(column * split + h) ^ position[1]] = part[h]


def half_products(position, listed, integrals, gathered, time, split):
    arrays, keys = [g[0] for g in gathered], [g[1] for g in gathered]
    aux_count, block, orbitals = integrals.shape
    units = orbitals // block * split
    smem = pl.BlockSpec(memory_space=pltpu.SMEM)
    vmem = pl.BlockSpec(memory_space=pltpu.VMEM)
    return pl.pallas_call(
        functools.partial(half_kernel, keys, time, split),
        out_shape=jax.ShapeDtypeStruct((units, aux_count // split, block, block), jnp.float32),
        in_specs=[smem, smem, vmem] + [vmem] * len(arrays),
        out_specs=vmem,
        scratch_shapes=[pltpu.VMEM((orbitals, orbitals), jnp.bfloat16)] * 2
        + [pltpu.VMEM((aux_count * block, orbitals), jnp.bfloat16)] * 2,
        compiler_params=pltpu.CompilerParams(vmem_limit_bytes=VMEM_BYTES),
        cost_estimate=pl.CostEstimate(
            flops=6 * aux_count * block * orbitals * orbitals,
            bytes_accessed=4 * (orbitals * orbitals + 2 * aux_count * block * orbitals),
            transcendentals=0,
        ),
        name="half_products",
    )(position, listed, integrals, *arrays)


def split_kernel(keys, position, *rest):
    refs, (high, low) = rest[: len(keys)], rest[len(keys) :]
    place_blocks(position, refs, keys, high, low)


def split_whole(position, gathered, orbitals):
    arrays, keys = [g[0] for g in gathered], [g[1] for g in gathered]
    smem = pl.BlockSpec(memory_space=pltpu.SMEM)
    vmem = pl.BlockSpec(memory_space=pltpu.VMEM)
    return pl.pallas_call(
        functools.partial(split_kernel, keys),
        out_shape=[jax.ShapeDtypeStruct((orbitals, orbitals), jnp.bfloat16)] * 2,
        in_specs=[smem] + [vmem] * len(arrays),
        out_specs=[vmem] * 2,
        compiler_params=pltpu.CompilerParams(vmem_limit_bytes=VMEM_BYTES),
        cost_estimate=pl.CostEstimate(
            flops=4 * orbitals * orbitals, bytes_accessed=8 * orbitals * orbitals, transcendentals=0
        ),
        name="split_whole",
    )(position, *arrays)


def full_kernel(split, count, position, a_high, a_low, own, *rest):
    received, (out, b_high, b_low) = rest[: count - 1], rest[-3:]
    share, block, _ = own.shape[1:]
    for bits in range(count):
        source = position[1] ^ bits
        row = pl.multiple_of(source // split * block, block)
        for at in range(share):
            value = own[0, at] if bits == 0 else received[bits - 1][at]
            col = pl.multiple_of((source % split * share + at) * block, block)
            high, low = halves(value)
            b_high[pl.ds(row, block), pl.ds(col, block)] = high
            b_low[pl.ds(row, block), pl.ds(col, block)] = low
    orbitals = a_high.shape[0]
    tile = 2 * block
    for start in range(0, orbitals, tile):
        rows = slice(start, start + tile)
        product = three_products(a_high[rows], a_low[rows], b_high[...], b_low[...])
        for at in range(share * split):
            out[0, at, 0, rows] = product[:, at * block : (at + 1) * block]


def full_products(position, vir, own, received, time, times, split, earlier):
    high, low = vir
    orbitals = high.shape[0]
    units, share, block, _ = own.shape
    aux_count = share * split
    smem = pl.BlockSpec(memory_space=pltpu.SMEM)
    vmem = pl.BlockSpec(memory_space=pltpu.VMEM)
    first = pl.BlockSpec((1, share, block, block), lambda i: (0, 0, 0, 0))
    operands = [position, high, low, own, *received]
    in_specs = [smem, vmem, vmem, first] + [vmem] * len(received)
    aliases = {}
    if earlier is not None:
        aliases = {len(operands): 0}
        operands.append(earlier)
        in_specs.append(pl.BlockSpec(memory_space=pl.ANY))
    return pl.pallas_call(
        functools.partial(full_kernel, split, units),
        grid=(1,),
        out_shape=jax.ShapeDtypeStruct((times, aux_count, 1, orbitals, block), jnp.float32),
        in_specs=in_specs,
        out_specs=pl.BlockSpec((1, aux_count, 1, orbitals, block), lambda i: (time, 0, 0, 0, 0)),
        scratch_shapes=[pltpu.VMEM((orbitals, aux_count * block), jnp.bfloat16)] * 2,
        input_output_aliases=aliases,
        compiler_params=pltpu.CompilerParams(vmem_limit_bytes=VMEM_BYTES),
        cost_estimate=pl.CostEstimate(
            flops=6 * aux_count * block * orbitals * orbitals,
            bytes_accessed=4 * (orbitals * orbitals + 2 * aux_count * block * orbitals),
            transcendentals=0,
        ),
        name="full_products",
    )(*operands)


def local(three_center, tile_lists, occ_density, vir_density):
    integrals = three_center[:, 0]
    block, orbitals = three_center.shape[2:]
    owners = lax.axis_size("orb")
    split = owners // (orbitals // block)
    unit = lax.axis_index("orb")
    listed = listed_mask(tile_lists, unit % split, unit // split)
    position = jnp.stack([lax.axis_index("aux"), unit]).astype(jnp.int32)
    times = occ_density.shape[0]
    sent, received = [], []
    for time in range(times):
        gathered = gather(occ_density[time])
        products = half_products(position, listed, integrals, gathered, time, split)
        sent.append(products)
        received.append([exchange(products[bits], 0, bits) for bits in range(1, owners)])
    coupled = None
    for time in range(times):
        vir = split_whole(position, gather(vir_density[time]), orbitals)
        coupled = full_products(
            position, vir, sent[time], received[time], time, times, split, coupled
        )
    return coupled


def solution(mesh):
    in_specs = (
        P("aux", "orb", None, None),
        P(None, "aux", None, None),
        P(None, "orb", "aux"),
        P(None, "orb", "aux"),
    )
    out_specs = P(None, "aux", "orb", None, None)
    return jax.shard_map(local, mesh=mesh, in_specs=in_specs, out_specs=out_specs, check_vma=False)
```

time: 415 us -> 255 us (0.61)
  the two profiles are of different devices: /device:TPU:0 before, /device:TPU:10 now
where the time goes in v1:
time: 255 us
  waiting for transfers between devices  157 us (62%)
  starting transfers between devices  45.8 us (18%)
  Pallas kernels  42.7 us (17%)
  local copies, waits for them, and re-layouts  6.88 us (3%)
  other arithmetic  2.77 us (1%)
    ppermute x38, waiting for transfers between devices, exchange(): return lax.ppermute(value, ('aux', 'orb'), pairs)  157 us
    ppermute x38, starting transfers between devices, exchange(): return lax.ppermute(value, ('aux', 'orb'), pairs)  45.8 us
    pallas_call x2, Pallas kernels, half_products(): pl.pallas_call(functools.partial(half_kernel, keys, time, split), out_sha...  17.1 us
    pallas_call x2, Pallas kernels, full_products(): pl.pallas_call(functools.partial(full_kernel, split, units), grid=(1,), o...  15.9 us
    pallas_call x2, Pallas kernels, split_whole(): pl.pallas_call(functools.partial(split_kernel, keys), out_shape=[jax.Shap...  9.73 us
  transfers between devices with their start and end apart: 38, of which 20 were waited for; matrix products, arithmetic and copies ran while one was open for 3% of the time, Pallas kernels for 14%

profile of v1, /device:TPU:10, one launch (start us, length us, event | category | flops | bytes accessed | tf_op | source)
XLA Modules:
  0.0 255.1 jit_solution(15152300806605651054)
XLA Ops:
  1.0 2.7 %collective-permute-start.25 = (f32[1,128,256]{2,1,0:T(8,128)S(1)}, f32[1,128,256]{2,1,0:T(8,128)S(1)}, u32[]{:S(2)}, u32[]{:S(2)}) collective-permute-start(f32[1,128,256]{2,1,0:T(8,128)S(1)} %get-tuple-element.27), channel_id=1, source_target_pairs={{0,4},{1,5},{2,6},{3,7},{4,0},{5,1},{6,2},{7,3},{8,12},{9,13},{10,... | collective-permute-start | bytes 393224 | tf_op jit(solution)/shard_map/ppermute | solution.py:39
  3.7 5.5 %collective-permute-done.25 = f32[1,128,256]{2,1,0:T(8,128)S(1)} collective-permute-done((f32[1,128,256]{2,1,0:T(8,128)S(1)}, f32[1,128,256]{2,1,0:T(8,128)S(1)}, u32[]{:S(2)}, u32[]{:S(2)}) %collective-permute-start.25) | collective-permute-done | bytes 131104 | tf_op jit(solution)/shard_map/ppermute | solution.py:39
  12.7 5.7 %collective-permute-done.26 = f32[2,128,256]{2,1,0:T(8,128)S(1)} collective-permute-done((f32[2,128,256]{2,1,0:T(8,128)S(1)}, f32[2,128,256]{2,1,0:T(8,128)S(1)}, u32[]{:S(2)}, u32[]{:S(2)}) %collective-permute-start.26) | collective-permute-done | bytes 262176 | tf_op jit(solution)/shard_map/ppermute | solution.py:39
  20.0 5.3 %collective-permute-start.19 = (f32[1,128,256]{2,1,0:T(8,128)S(1)}, f32[1,128,256]{2,1,0:T(8,128)S(1)}, u32[]{:S(2)}, u32[]{:S(2)}) collective-permute-start(f32[1,128,256]{2,1,0:T(8,128)S(1)} %get-tuple-element.29), channel_id=1, source_target_pairs={{0,4},{1,5},{2,6},{3,7},{4,0},{5,1},{6,2},{7,3},{8,12},{9,13},{10,... | collective-permute-start | bytes 393224 | tf_op jit(solution)/shard_map/ppermute | solution.py:39
  25.5 6.3 %collective-permute-done.19 = f32[1,128,256]{2,1,0:T(8,128)S(1)} collective-permute-done((f32[1,128,256]{2,1,0:T(8,128)S(1)}, f32[1,128,256]{2,1,0:T(8,128)S(1)}, u32[]{:S(2)}, u32[]{:S(2)}) %collective-permute-start.19) | collective-permute-done | bytes 131104 | tf_op jit(solution)/shard_map/ppermute | solution.py:39
  31.9 3.2 %collective-permute-start.20 = (f32[2,128,256]{2,1,0:T(8,128)S(1)}, f32[2,128,256]{2,1,0:T(8,128)S(1)}, u32[]{:S(2)}, u32[]{:S(2)}) collective-permute-start(f32[2,128,256]{2,1,0:T(8,128)S(1)} %pad_maximum_fusion.10), channel_id=1, source_target_pairs={{0,2},{1,3},{2,0},{3,1},{4,6},{5,7},{6,4},{7,5},{8,10},{9,11},{10,... | collective-permute-start | bytes 786440 | tf_op jit(solution)/shard_map/ppermute | solution.py:39
  37.9 4.7 %collective-permute-done.20 = f32[2,128,256]{2,1,0:T(8,128)S(1)} collective-permute-done((f32[2,128,256]{2,1,0:T(8,128)S(1)}, f32[2,128,256]{2,1,0:T(8,128)S(1)}, u32[]{:S(2)}, u32[]{:S(2)}) %collective-permute-start.20) | collective-permute-done | bytes 262176 | tf_op jit(solution)/shard_map/ppermute | solution.py:39
  43.1 3.8 %collective-permute-done.1 = f32[2,128,256]{2,1,0:T(8,128)S(1)} collective-permute-done((f32[2,128,256]{2,1,0:T(8,128)S(1)}, f32[2,128,256]{2,1,0:T(8,128)S(1)}, u32[]{:S(2)}, u32[]{:S(2)}) %collective-permute-start.1) | collective-permute-done | bytes 262176 | tf_op jit(solution)/shard_map/ppermute | solution.py:39
  47.5 4.7 %collective-permute-done.8 = f32[4,128,256]{2,1,0:T(8,128)S(1)} collective-permute-done((f32[4,128,256]{2,1,0:T(8,128)S(1)}, f32[4,128,256]{2,1,0:T(8,128)S(1)}, u32[]{:S(2)}, u32[]{:S(2)}) %collective-permute-start.8) | collective-permute-done | bytes 524320 | tf_op jit(solution)/shard_map/ppermute | solution.py:39
  54.8 8.6 %collective-permute-done.21 = f32[4,128,256]{2,1,0:T(8,128)S(1)} collective-permute-done((f32[4,128,256]{2,1,0:T(8,128)S(1)}, f32[4,128,256]{2,1,0:T(8,128)S(1)}, u32[]{:S(2)}, u32[]{:S(2)}) %collective-permute-start.21) | collective-permute-done | bytes 524320 | tf_op jit(solution)/shard_map/ppermute | solution.py:39
  63.5 8.2 %collective-permute-done.2 = f32[4,128,256]{2,1,0:T(8,128)S(1)} collective-permute-done((f32[4,128,256]{2,1,0:T(8,128)S(1)}, f32[4,128,256]{2,1,0:T(8,128)S(1)}, u32[]{:S(2)}, u32[]{:S(2)}) %collective-permute-start.2) | collective-permute-done | bytes 524320 | tf_op jit(solution)/shard_map/ppermute | solution.py:39
  74.9 10.4 %collective-permute-done.9.rest_1_ = f32[8,128,256]{2,1,0:T(8,128)} collective-permute-done((f32[8,128,256]{2,1,0:T(8,128)}, f32[8,128,256]{2,1,0:T(8,128)}, u32[]{:S(2)}, u32[]{:S(2)}) %collective-permute-start.9) | collective-permute-done | bytes 1048608 | tf_op jit(solution)/shard_map/ppermute | solution.py:39
  85.4 22.3 %collective-permute-done.22.rest_1_ = f32[8,128,256]{2,1,0:T(8,128)S(1)} collective-permute-done((f32[8,128,256]{2,1,0:T(8,128)S(1)}, f32[8,128,256]{2,1,0:T(8,128)S(1)}, u32[]{:S(2)}, u32[]{:S(2)}) %collective-permute-start.22) | collective-permute-done | bytes 1048608 | tf_op jit(solution)/shard_map/ppermute | solution.py:39
  108.3 19.4 %collective-permute-done.3.rest_1_ = f32[8,128,256]{2,1,0:T(8,128)} collective-permute-done((f32[8,128,256]{2,1,0:T(8,128)S(1)}, f32[8,128,256]{2,1,0:T(8,128)}, u32[]{:S(2)}, u32[]{:S(2)}) %collective-permute-start.3) | collective-permute-done | bytes 1048608 | tf_op jit(solution)/shard_map/ppermute | solution.py:39
  129.4 8.6 %half_products.3.own = f32[8,4,128,128]{3,2,1,0:T(8,128)} custom-call(s32[2]{0:T(128)} %pad_add_fusion.position, f32[2,8]{1,0:T(2,128)} %convert_reduce_fusion.listed, f32[4,128,1024]{2,1,0:T(8,128)} %bitcast.33, f32[8,128,256]{2,1,0:T(8,128)} %copy-done.8, f32[8,128,256]{2,1,0:T(8,128)} %collective-permute-done.28.rest_1_, f32[8,128,256]{2,1,0:T(8,128)} %copy-done.23, ...), custom_call_target="tpu_custom_call" | custom-call | flops 3221225472 | bytes 8388608 | tf_op jit(solution)/shard_map/half_products/pallas_call | solution.py:99
  141.0 8.6 %half_products.2.own = f32[8,4,128,128]{3,2,1,0:T(8,128)} custom-call(s32[2]{0:T(128)} %pad_add_fusion.position, f32[2,8]{1,0:T(2,128)} %convert_reduce_fusion.listed, f32[4,128,1024]{2,1,0:T(8,128)} %bitcast.34, f32[8,128,256]{2,1,0:T(8,128)} %pad_maximum_fusion.1.rest_0_, f32[8,128,256]{2,1,0:T(8,128)} %collective-permute-done.9.rest_1_, ...), custom_call_target="tpu_custom_call" | custom-call | flops 3221225472 | bytes 8388608 | tf_op jit(solution)/shard_map/half_products/pallas_call | solution.py:99
  152.6 3.2 %collective-permute-start.34 = (f32[4,128,128]{2,1,0:T(8,128)S(1)}, f32[4,128,128]{2,1,0:T(8,128)S(1)}, u32[]{:S(2)}, u32[]{:S(2)}) collective-permute-start(f32[4,128,128]{2,1,0:T(8,128)S(1)} %get-tuple-element.16), channel_id=1, source_target_pairs={{0,4},{1,5},{2,6},{3,7},{4,0},{5,1},{6,2},{7,3},{8,12},{9,13},{10,... | collective-permute-start | bytes 786440 | tf_op jit(solution)/shard_map/ppermute | solution.py:39
  158.0 2.7 %collective-permute-start.36 = (f32[4,128,128]{2,1,0:T(8,128)}, f32[4,128,128]{2,1,0:T(8,128)S(1)}, u32[]{:S(2)}, u32[]{:S(2)}) collective-permute-start(f32[4,128,128]{2,1,0:T(8,128)} %get-tuple-element.14), channel_id=1, source_target_pairs={{0,6},{1,7},{2,4},{3,5},{4,2},{5,3},{6,0},{7,1},{8,14},{9,15},{10,... | collective-permute-start | bytes 786440 | tf_op jit(solution)/shard_map/ppermute | solution.py:39
  160.7 7.6 %collective-permute-done.32.rest_1_ = f32[4,128,128]{2,1,0:T(8,128)S(1)} collective-permute-done((f32[4,128,128]{2,1,0:T(8,128)}, f32[4,128,128]{2,1,0:T(8,128)S(1)}, u32[]{:S(2)}, u32[]{:S(2)}) %collective-permute-start.32) | collective-permute-done | bytes 262176 | tf_op jit(solution)/shard_map/ppermute | solution.py:39
  169.6 2.9 %collective-permute-done.33.rest_2_ = f32[4,128,128]{2,1,0:T(8,128)S(1)} collective-permute-done((f32[4,128,128]{2,1,0:T(8,128)S(1)}, f32[4,128,128]{2,1,0:T(8,128)S(1)}, u32[]{:S(2)}, u32[]{:S(2)}) %collective-permute-start.33) | collective-permute-done | bytes 262176 | tf_op jit(solution)/shard_map/ppermute | solution.py:39
  176.5 4.9 %split_whole.3 = (bf16[1024,1024]{1,0:T(8,128)(2,1)}, bf16[1024,1024]{1,0:T(8,128)(2,1)}) custom-call(s32[2]{0:T(128)} %pad_add_fusion.position, f32[8,128,256]{2,1,0:T(8,128)} %copy-done.1, f32[8,128,256]{2,1,0:T(8,128)} %copy-done.3, f32[8,128,256]{2,1,0:T(8,128)} %copy-done.4, f32[8,128,256]{2,1,0:T(8,128)} %copy-done.6), custom_call_target="tpu_custom_call" | custom-call | flops 4194304 | bytes 8388608 | tf_op jit(solution)/shard_map/split_whole/pallas_call | solution.py:125
  181.5 4.8 %split_whole.2 = (bf16[1024,1024]{1,0:T(8,128)(2,1)}, bf16[1024,1024]{1,0:T(8,128)(2,1)}) custom-call(s32[2]{0:T(128)} %pad_add_fusion.position, f32[8,128,256]{2,1,0:T(8,128)} %copy-done.2, f32[8,128,256]{2,1,0:T(8,128)} %collective-permute-done.3.rest_1_, f32[8,128,256]{2,1,0:T(8,128)} %copy-done.5, f32[8,128,256]{2,1,0:T(8,128)} %copy-done.7), custom_call_target="tpu_custom_call" | custom-call | flops 4194304 | bytes 8388608 | tf_op jit(solution)/shard_map/split_whole/pallas_call | solution.py:125
  186.3 4.6 %collective-permute-done.35.rest_4_ = f32[4,128,128]{2,1,0:T(8,128)S(1)} collective-permute-done((f32[4,128,128]{2,1,0:T(8,128)}, f32[4,128,128]{2,1,0:T(8,128)S(1)}, u32[]{:S(2)}, u32[]{:S(2)}) %collective-permute-start.35) | collective-permute-done | bytes 262176 | tf_op jit(solution)/shard_map/ppermute | solution.py:39
  190.8 2.8 %collective-permute-start.14 = (f32[4,128,128]{2,1,0:T(8,128)S(1)}, f32[4,128,128]{2,1,0:T(8,128)S(1)}, u32[]{:S(2)}, u32[]{:S(2)}) collective-permute-start(f32[4,128,128]{2,1,0:T(8,128)S(1)} %get-tuple-element.24), channel_id=1, source_target_pairs={{0,3},{1,2},{2,1},{3,0},{4,7},{5,6},{6,5},{7,4},{8,11},{9,10},{10,... | collective-permute-start | bytes 786440 | tf_op jit(solution)/shard_map/ppermute | solution.py:39
  193.6 3.3 %collective-permute-done.36.rest_5_ = f32[4,128,128]{2,1,0:T(8,128)S(1)} collective-permute-done((f32[4,128,128]{2,1,0:T(8,128)}, f32[4,128,128]{2,1,0:T(8,128)S(1)}, u32[]{:S(2)}, u32[]{:S(2)}) %collective-permute-start.36) | collective-permute-done | bytes 262176 | tf_op jit(solution)/shard_map/ppermute | solution.py:39
  197.5 14.3 %collective-permute-done.37.rest_6_ = f32[4,128,128]{2,1,0:T(8,128)S(1)} collective-permute-done((f32[4,128,128]{2,1,0:T(8,128)S(1)}, f32[4,128,128]{2,1,0:T(8,128)S(1)}, u32[]{:S(2)}, u32[]{:S(2)}) %collective-permute-start.37) | collective-permute-done | bytes 262176 | tf_op jit(solution)/shard_map/ppermute | solution.py:39
  214.2 8.0 %full_products.2.rest_7_ = f32[2,4,1,1024,128]{4,3,2,1,0:T(8,128)} custom-call(s32[2]{0:T(128)} %pad_add_fusion.position, bf16[1024,1024]{1,0:T(8,128)(2,1)} %get-tuple-element.11.a_high, bf16[1024,1024]{1,0:T(8,128)(2,1)} %get-tuple-element.12.a_low, f32[8,4,128,128]{3,2,1,0:T(8,128)} %half_products.3.own, f32[4,128,128]{2,1,0:T(8,128)} %collective-permute-done.31.rest_0_, ...), custom_call_target="tpu_custom_call" | custom-call | flops 3221225472 | bytes 8388608 | tf_op jit(solution)/shard_map/full_products/pallas_call | solution.py:174
  222.3 7.8 %collective-permute-done.15.rest_3_ = f32[4,128,128]{2,1,0:T(8,128)S(1)} collective-permute-done((f32[4,128,128]{2,1,0:T(8,128)S(1)}, f32[4,128,128]{2,1,0:T(8,128)S(1)}, u32[]{:S(2)}, u32[]{:S(2)}) %collective-permute-start.15) | collective-permute-done | bytes 262176 | tf_op jit(solution)/shard_map/ppermute | solution.py:39
  230.1 5.6 %collective-permute-done.16.rest_4_ = f32[4,128,128]{2,1,0:T(8,128)S(1)} collective-permute-done((f32[4,128,128]{2,1,0:T(8,128)S(1)}, f32[4,128,128]{2,1,0:T(8,128)S(1)}, u32[]{:S(2)}, u32[]{:S(2)}) %collective-permute-start.16) | collective-permute-done | bytes 262176 | tf_op jit(solution)/shard_map/ppermute | solution.py:39
  235.7 6.4 %collective-permute-done.17.rest_5_ = f32[4,128,128]{2,1,0:T(8,128)S(1)} collective-permute-done((f32[4,128,128]{2,1,0:T(8,128)S(1)}, f32[4,128,128]{2,1,0:T(8,128)S(1)}, u32[]{:S(2)}, u32[]{:S(2)}) %collective-permute-start.17) | collective-permute-done | bytes 262176 | tf_op jit(solution)/shard_map/ppermute | solution.py:39
  242.1 4.5 %collective-permute-done.18.rest_6_ = f32[4,128,128]{2,1,0:T(8,128)S(1)} collective-permute-done((f32[4,128,128]{2,1,0:T(8,128)S(1)}, f32[4,128,128]{2,1,0:T(8,128)S(1)}, u32[]{:S(2)}, u32[]{:S(2)}) %collective-permute-start.18) | collective-permute-done | bytes 262176 | tf_op jit(solution)/shard_map/ppermute | solution.py:39
  247.3 7.8 %full_products.3 = f32[2,4,1,1024,128]{4,3,2,1,0:T(8,128)} custom-call(s32[2]{0:T(128)} %pad_add_fusion.position, bf16[1024,1024]{1,0:T(8,128)(2,1)} %get-tuple-element.9.a_high, bf16[1024,1024]{1,0:T(8,128)(2,1)} %get-tuple-element.10.a_low, f32[8,4,128,128]{3,2,1,0:T(8,128)} %half_products.2.own, ...), custom_call_target="tpu_custom_call", output_to_operand_aliasing={{}: (11, {})} | custom-call | flops 3221225472 | bytes 8388608 | tf_op jit(solution)/shard_map/full_products/pallas_call | solution.py:174
  (117 shorter events, 35.6 us)
Async XLA Ops:
  10.6 14.9 %collective-permute-start.6 = (f32[1,128,256]{2,1,0:T(8,128)S(1)}, f32[1,128,256]{2,1,0:T(8,128)S(1)}, u32[]{:S(2)}, u32[]{:S(2)}) collective-permute-start(f32[1,128,256]{2,1,0:T(8,128)S(1)} %get-tuple-element.28), channel_id=1, source_target_pairs={{0,4},{1,5},{2,6},{3,7},{4,0},{5,1},{6,2},{7,3},{8,12},{9,13},{10,... | collective-permute-start | bytes 393224 | tf_op jit(solution)/shard_map/ppermute | solution.py:39
  18.4 18.1 %collective-permute-start.27 = (f32[4,128,256]{2,1,0:T(8,128)S(1)}, f32[4,128,256]{2,1,0:T(8,128)S(1)}, u32[]{:S(2)}, u32[]{:S(2)}) collective-permute-start(f32[4,128,256]{2,1,0:T(8,128)S(1)} %pad_maximum_fusion.7), channel_id=1, source_target_pairs={{0,1},{1,0},{2,3},{3,2},{4,5},{5,4},{6,7},{7,6},{8,9},{9,8},{10,11... | collective-permute-start | bytes 1572872 | tf_op jit(solution)/shard_map/ppermute | solution.py:39
  20.0 11.8 %collective-permute-start.19 = (f32[1,128,256]{2,1,0:T(8,128)S(1)}, f32[1,128,256]{2,1,0:T(8,128)S(1)}, u32[]{:S(2)}, u32[]{:S(2)}) collective-permute-start(f32[1,128,256]{2,1,0:T(8,128)S(1)} %get-tuple-element.29), channel_id=1, source_target_pairs={{0,4},{1,5},{2,6},{3,7},{4,0},{5,1},{6,2},{7,3},{8,12},{9,13},{10,... | collective-permute-start | bytes 393224 | tf_op jit(solution)/shard_map/ppermute | solution.py:39
  36.6 36.7 %collective-permute-start.28 = (f32[8,128,256]{2,1,0:T(8,128)S(1)}, f32[8,128,256]{2,1,0:T(8,128)}, u32[]{:S(2)}, u32[]{:S(2)}) collective-permute-start(f32[8,128,256]{2,1,0:T(8,128)S(1)} %pad_maximum_fusion.3.rest_0_), channel_id=1, source_target_pairs={{0,16},{1,17},{2,18},{3,19},{4,20},{5,21},{6,22},{7,23},{8,24},{9,... | collective-permute-start | bytes 3145736 | tf_op jit(solution)/shard_map/ppermute | solution.py:39
  37.3 14.9 %collective-permute-start.8 = (f32[4,128,256]{2,1,0:T(8,128)S(1)}, f32[4,128,256]{2,1,0:T(8,128)S(1)}, u32[]{:S(2)}, u32[]{:S(2)}) collective-permute-start(f32[4,128,256]{2,1,0:T(8,128)S(1)} %pad_maximum_fusion.5), channel_id=1, source_target_pairs={{0,1},{1,0},{2,3},{3,2},{4,5},{5,4},{6,7},{7,6},{8,9},{9,8},{10,11... | collective-permute-start | bytes 1572872 | tf_op jit(solution)/shard_map/ppermute | solution.py:39
  37.9 36.1 %collective-permute-start.29 = (f32[8,128,256]{2,1,0:T(8,128)S(1)}, f32[8,128,256]{2,1,0:T(8,128)S(1)}, u32[]{:S(2)}, u32[]{:S(2)}) collective-permute-start(f32[8,128,256]{2,1,0:T(8,128)S(1)} %pad_maximum_fusion.3.rest_0_), channel_id=1, source_target_pairs={{0,8},{1,9},{2,10},{3,11},{4,12},{5,13},{6,14},{7,15},{8,0},{9,1},... | collective-permute-start | bytes 3145736 | tf_op jit(solution)/shard_map/ppermute | solution.py:39
  42.5 20.9 %collective-permute-start.21 = (f32[4,128,256]{2,1,0:T(8,128)S(1)}, f32[4,128,256]{2,1,0:T(8,128)S(1)}, u32[]{:S(2)}, u32[]{:S(2)}) collective-permute-start(f32[4,128,256]{2,1,0:T(8,128)S(1)} %pad_maximum_fusion.6), channel_id=1, source_target_pairs={{0,1},{1,0},{2,3},{3,2},{4,5},{5,4},{6,7},{7,6},{8,9},{9,8},{10,11... | collective-permute-start | bytes 1572872 | tf_op jit(solution)/shard_map/ppermute | solution.py:39
  46.9 24.8 %collective-permute-start.2 = (f32[4,128,256]{2,1,0:T(8,128)S(1)}, f32[4,128,256]{2,1,0:T(8,128)S(1)}, u32[]{:S(2)}, u32[]{:S(2)}) collective-permute-start(f32[4,128,256]{2,1,0:T(8,128)S(1)} %pad_maximum_fusion.4), channel_id=1, source_target_pairs={{0,1},{1,0},{2,3},{3,2},{4,5},{5,4},{6,7},{7,6},{8,9},{9,8},{10,11... | collective-permute-start | bytes 1572872 | tf_op jit(solution)/shard_map/ppermute | solution.py:39
  53.3 32.1 %collective-permute-start.9 = (f32[8,128,256]{2,1,0:T(8,128)}, f32[8,128,256]{2,1,0:T(8,128)}, u32[]{:S(2)}, u32[]{:S(2)}) collective-permute-start(f32[8,128,256]{2,1,0:T(8,128)} %pad_maximum_fusion.1.rest_0_), channel_id=1, source_target_pairs={{0,16},{1,17},{2,18},{3,19},{4,20},{5,21},{6,22},{7,23},{8,24},{9,... | collective-permute-start | bytes 3145736 | tf_op jit(solution)/shard_map/ppermute | solution.py:39
  63.4 44.3 %collective-permute-start.10 = (f32[8,128,256]{2,1,0:T(8,128)}, f32[8,128,256]{2,1,0:T(8,128)}, u32[]{:S(2)}, u32[]{:S(2)}) collective-permute-start(f32[8,128,256]{2,1,0:T(8,128)} %pad_maximum_fusion.1.rest_0_), channel_id=1, source_target_pairs={{0,8},{1,9},{2,10},{3,11},{4,12},{5,13},{6,14},{7,15},{8,0},{9,1},... | collective-permute-start | bytes 3145736 | tf_op jit(solution)/shard_map/ppermute | solution.py:39
  71.8 36.0 %collective-permute-start.22 = (f32[8,128,256]{2,1,0:T(8,128)S(1)}, f32[8,128,256]{2,1,0:T(8,128)S(1)}, u32[]{:S(2)}, u32[]{:S(2)}) collective-permute-start(f32[8,128,256]{2,1,0:T(8,128)S(1)} %pad_maximum_fusion.2.rest_0_), channel_id=1, source_target_pairs={{0,16},{1,17},{2,18},{3,19},{4,20},{5,21},{6,22},{7,23},{8,24},{9,... | collective-permute-start | bytes 3145736 | tf_op jit(solution)/shard_map/ppermute | solution.py:39
  73.3 54.3 %collective-permute-start.3 = (f32[8,128,256]{2,1,0:T(8,128)S(1)}, f32[8,128,256]{2,1,0:T(8,128)}, u32[]{:S(2)}, u32[]{:S(2)}) collective-permute-start(f32[8,128,256]{2,1,0:T(8,128)S(1)} %pad_maximum_fusion.rest_0_), channel_id=1, source_target_pairs={{0,16},{1,17},{2,18},{3,19},{4,20},{5,21},{6,22},{7,23},{8,24},{9,... | collective-permute-start | bytes 3145736 | tf_op jit(solution)/shard_map/ppermute | solution.py:39
  74.9 54.0 %collective-permute-start.30 = (f32[8,128,256]{2,1,0:T(8,128)}, f32[8,128,256]{2,1,0:T(8,128)}, u32[]{:S(2)}, u32[]{:S(2)}) collective-permute-start(f32[8,128,256]{2,1,0:T(8,128)} %collective-permute-done.28.rest_1_), channel_id=1, source_target_pairs={{0,8},{1,9},{2,10},{3,11},{4,12},{5,13},{6,14},{7,15},{8,0},{9,1},... | collective-permute-start | bytes 3145736 | tf_op jit(solution)/shard_map/ppermute | solution.py:39
  85.4 55.1 %collective-permute-start.11 = (f32[8,128,256]{2,1,0:T(8,128)}, f32[8,128,256]{2,1,0:T(8,128)}, u32[]{:S(2)}, u32[]{:S(2)}) collective-permute-start(f32[8,128,256]{2,1,0:T(8,128)} %collective-permute-done.9.rest_1_), channel_id=1, source_target_pairs={{0,8},{1,9},{2,10},{3,11},{4,12},{5,13},{6,14},{7,15},{8,0},{9,1},... | collective-permute-start | bytes 3145736 | tf_op jit(solution)/shard_map/ppermute | solution.py:39
  107.7 41.8 %collective-permute-start.23 = (f32[8,128,256]{2,1,0:T(8,128)S(1)}, f32[8,128,256]{2,1,0:T(8,128)S(1)}, u32[]{:S(2)}, u32[]{:S(2)}) collective-permute-start(f32[8,128,256]{2,1,0:T(8,128)S(1)} %pad_maximum_fusion.2.rest_0_), channel_id=1, source_target_pairs={{0,8},{1,9},{2,10},{3,11},{4,12},{5,13},{6,14},{7,15},{8,0},{9,1},... | collective-permute-start | bytes 3145736 | tf_op jit(solution)/shard_map/ppermute | solution.py:39
  107.8 43.4 %collective-permute-start.4 = (f32[8,128,256]{2,1,0:T(8,128)S(1)}, f32[8,128,256]{2,1,0:T(8,128)S(1)}, u32[]{:S(2)}, u32[]{:S(2)}) collective-permute-start(f32[8,128,256]{2,1,0:T(8,128)S(1)} %pad_maximum_fusion.rest_0_), channel_id=1, source_target_pairs={{0,8},{1,9},{2,10},{3,11},{4,12},{5,13},{6,14},{7,15},{8,0},{9,1},... | collective-permute-start | bytes 3145736 | tf_op jit(solution)/shard_map/ppermute | solution.py:39
  127.7 25.0 %collective-permute-start.24 = (f32[8,128,256]{2,1,0:T(8,128)S(1)}, f32[8,128,256]{2,1,0:T(8,128)S(1)}, u32[]{:S(2)}, u32[]{:S(2)}) collective-permute-start(f32[8,128,256]{2,1,0:T(8,128)S(1)} %collective-permute-done.22.rest_1_), channel_id=1, source_target_pairs={{0,8},{1,9},{2,10},{3,11},{4,12},{5,13},{6,14},{7,15},{8,0},{9,1},... | collective-permute-start | bytes 3145736 | tf_op jit(solution)/shard_map/ppermute | solution.py:39
  128.9 28.5 %collective-permute-start.5 = (f32[8,128,256]{2,1,0:T(8,128)}, f32[8,128,256]{2,1,0:T(8,128)S(1)}, u32[]{:S(2)}, u32[]{:S(2)}) collective-permute-start(f32[8,128,256]{2,1,0:T(8,128)} %collective-permute-done.3.rest_1_), channel_id=1, source_target_pairs={{0,8},{1,9},{2,10},{3,11},{4,12},{5,13},{6,14},{7,15},{8,0},{9,1},... | collective-permute-start | bytes 3145736 | tf_op jit(solution)/shard_map/ppermute | solution.py:39
  140.5 17.5 %collective-permute-start.31 = (f32[4,128,128]{2,1,0:T(8,128)}, f32[4,128,128]{2,1,0:T(8,128)}, u32[]{:S(2)}, u32[]{:S(2)}) collective-permute-start(f32[4,128,128]{2,1,0:T(8,128)} %get-tuple-element.19), channel_id=1, source_target_pairs={{0,1},{1,0},{2,3},{3,2},{4,5},{5,4},{6,7},{7,6},{8,9},{9,8},{10,11... | collective-permute-start | bytes 786440 | tf_op jit(solution)/shard_map/ppermute | solution.py:39
  149.6 18.7 %collective-permute-start.32 = (f32[4,128,128]{2,1,0:T(8,128)}, f32[4,128,128]{2,1,0:T(8,128)S(1)}, u32[]{:S(2)}, u32[]{:S(2)}) collective-permute-start(f32[4,128,128]{2,1,0:T(8,128)} %get-tuple-element.18), channel_id=1, source_target_pairs={{0,2},{1,3},{2,0},{3,1},{4,6},{5,7},{6,4},{7,5},{8,10},{9,11},{10,... | collective-permute-start | bytes 786440 | tf_op jit(solution)/shard_map/ppermute | solution.py:39
  151.2 21.3 %collective-permute-start.33 = (f32[4,128,128]{2,1,0:T(8,128)S(1)}, f32[4,128,128]{2,1,0:T(8,128)S(1)}, u32[]{:S(2)}, u32[]{:S(2)}) collective-permute-start(f32[4,128,128]{2,1,0:T(8,128)S(1)} %get-tuple-element.17), channel_id=1, source_target_pairs={{0,3},{1,2},{2,1},{3,0},{4,7},{5,6},{6,5},{7,4},{8,11},{9,10},{10,... | collective-permute-start | bytes 786440 | tf_op jit(solution)/shard_map/ppermute | solution.py:39
  152.6 21.7 %collective-permute-start.34 = (f32[4,128,128]{2,1,0:T(8,128)S(1)}, f32[4,128,128]{2,1,0:T(8,128)S(1)}, u32[]{:S(2)}, u32[]{:S(2)}) collective-permute-start(f32[4,128,128]{2,1,0:T(8,128)S(1)} %get-tuple-element.16), channel_id=1, source_target_pairs={{0,4},{1,5},{2,6},{3,7},{4,0},{5,1},{6,2},{7,3},{8,12},{9,13},{10,... | collective-permute-start | bytes 786440 | tf_op jit(solution)/shard_map/ppermute | solution.py:39
  157.5 33.4 %collective-permute-start.35 = (f32[4,128,128]{2,1,0:T(8,128)}, f32[4,128,128]{2,1,0:T(8,128)S(1)}, u32[]{:S(2)}, u32[]{:S(2)}) collective-permute-start(f32[4,128,128]{2,1,0:T(8,128)} %get-tuple-element.15), channel_id=1, source_target_pairs={{0,5},{1,4},{2,7},{3,6},{4,1},{5,0},{6,3},{7,2},{8,13},{9,12},{10,... | collective-permute-start | bytes 786440 | tf_op jit(solution)/shard_map/ppermute | solution.py:39
  158.0 38.9 %collective-permute-start.36 = (f32[4,128,128]{2,1,0:T(8,128)}, f32[4,128,128]{2,1,0:T(8,128)S(1)}, u32[]{:S(2)}, u32[]{:S(2)}) collective-permute-start(f32[4,128,128]{2,1,0:T(8,128)} %get-tuple-element.14), channel_id=1, source_target_pairs={{0,6},{1,7},{2,4},{3,5},{4,2},{5,3},{6,0},{7,1},{8,14},{9,15},{10,... | collective-permute-start | bytes 786440 | tf_op jit(solution)/shard_map/ppermute | solution.py:39
  168.3 43.5 %collective-permute-start.37 = (f32[4,128,128]{2,1,0:T(8,128)S(1)}, f32[4,128,128]{2,1,0:T(8,128)S(1)}, u32[]{:S(2)}, u32[]{:S(2)}) collective-permute-start(f32[4,128,128]{2,1,0:T(8,128)S(1)} %get-tuple-element.13), channel_id=1, source_target_pairs={{0,7},{1,6},{2,5},{3,4},{4,3},{5,2},{6,1},{7,0},{8,15},{9,14},{10,... | collective-permute-start | bytes 786440 | tf_op jit(solution)/shard_map/ppermute | solution.py:39
  172.5 39.3 %collective-permute-start.12 = (f32[4,128,128]{2,1,0:T(8,128)S(1)}, f32[4,128,128]{2,1,0:T(8,128)S(1)}, u32[]{:S(2)}, u32[]{:S(2)}) collective-permute-start(f32[4,128,128]{2,1,0:T(8,128)S(1)} %get-tuple-element.26), channel_id=1, source_target_pairs={{0,1},{1,0},{2,3},{3,2},{4,5},{5,4},{6,7},{7,6},{8,9},{9,8},{10,11... | collective-permute-start | bytes 786440 | tf_op jit(solution)/shard_map/ppermute | solution.py:39
  174.4 37.5 %collective-permute-start.13 = (f32[4,128,128]{2,1,0:T(8,128)S(1)}, f32[4,128,128]{2,1,0:T(8,128)S(1)}, u32[]{:S(2)}, u32[]{:S(2)}) collective-permute-start(f32[4,128,128]{2,1,0:T(8,128)S(1)} %get-tuple-element.25), channel_id=1, source_target_pairs={{0,2},{1,3},{2,0},{3,1},{4,6},{5,7},{6,4},{7,5},{8,10},{9,11},{10,... | collective-permute-start | bytes 786440 | tf_op jit(solution)/shard_map/ppermute | solution.py:39
  190.8 31.4 %collective-permute-start.14 = (f32[4,128,128]{2,1,0:T(8,128)S(1)}, f32[4,128,128]{2,1,0:T(8,128)S(1)}, u32[]{:S(2)}, u32[]{:S(2)}) collective-permute-start(f32[4,128,128]{2,1,0:T(8,128)S(1)} %get-tuple-element.24), channel_id=1, source_target_pairs={{0,3},{1,2},{2,1},{3,0},{4,7},{5,6},{6,5},{7,4},{8,11},{9,10},{10,... | collective-permute-start | bytes 786440 | tf_op jit(solution)/shard_map/ppermute | solution.py:39
  196.9 33.2 %collective-permute-start.15 = (f32[4,128,128]{2,1,0:T(8,128)S(1)}, f32[4,128,128]{2,1,0:T(8,128)S(1)}, u32[]{:S(2)}, u32[]{:S(2)}) collective-permute-start(f32[4,128,128]{2,1,0:T(8,128)S(1)} %get-tuple-element.23), channel_id=1, source_target_pairs={{0,4},{1,5},{2,6},{3,7},{4,0},{5,1},{6,2},{7,3},{8,12},{9,13},{10,... | collective-permute-start | bytes 786440 | tf_op jit(solution)/shard_map/ppermute | solution.py:39
  211.8 23.9 %collective-permute-start.16 = (f32[4,128,128]{2,1,0:T(8,128)S(1)}, f32[4,128,128]{2,1,0:T(8,128)S(1)}, u32[]{:S(2)}, u32[]{:S(2)}) collective-permute-start(f32[4,128,128]{2,1,0:T(8,128)S(1)} %get-tuple-element.22), channel_id=1, source_target_pairs={{0,5},{1,4},{2,7},{3,6},{4,1},{5,0},{6,3},{7,2},{8,13},{9,12},{10,... | collective-permute-start | bytes 786440 | tf_op jit(solution)/shard_map/ppermute | solution.py:39
  211.8 30.3 %collective-permute-start.17 = (f32[4,128,128]{2,1,0:T(8,128)S(1)}, f32[4,128,128]{2,1,0:T(8,128)S(1)}, u32[]{:S(2)}, u32[]{:S(2)}) collective-permute-start(f32[4,128,128]{2,1,0:T(8,128)S(1)} %get-tuple-element.21), channel_id=1, source_target_pairs={{0,6},{1,7},{2,4},{3,5},{4,2},{5,3},{6,0},{7,1},{8,14},{9,15},{10,... | collective-permute-start | bytes 786440 | tf_op jit(solution)/shard_map/ppermute | solution.py:39
  211.9 34.7 %collective-permute-start.18 = (f32[4,128,128]{2,1,0:T(8,128)S(1)}, f32[4,128,128]{2,1,0:T(8,128)S(1)}, u32[]{:S(2)}, u32[]{:S(2)}) collective-permute-start(f32[4,128,128]{2,1,0:T(8,128)S(1)} %get-tuple-element.20), channel_id=1, source_target_pairs={{0,7},{1,6},{2,5},{3,4},{4,3},{5,2},{6,1},{7,0},{8,15},{9,14},{10,... | collective-permute-start | bytes 786440 | tf_op jit(solution)/shard_map/ppermute | solution.py:39
  (30 other events, 601.7 us)

commit v2 on v1

v2 whole, which is shorter than its diff:
```python
import functools

import jax
import jax.numpy as jnp
from jax import lax
from jax.experimental import pallas as pl
from jax.experimental.pallas import tpu as pltpu
from jax.sharding import PartitionSpec as P

VMEM_BYTES = 56 * 1024 * 1024
SMEM = pl.BlockSpec(memory_space=pltpu.SMEM)
VMEM = pl.BlockSpec(memory_space=pltpu.VMEM)
PARAMS = pltpu.CompilerParams(vmem_limit_bytes=VMEM_BYTES)


def cost(flops, moved):
    return pl.CostEstimate(flops=flops, bytes_accessed=moved, transcendentals=0)


def listed_mask(tile_lists, part_index, block_index):
    block_table = lax.dynamic_index_in_dim(tile_lists, part_index, 1, keepdims=False)
    listed_row = lax.dynamic_index_in_dim(block_table, block_index, 1, keepdims=False)
    block_ids = jnp.arange(tile_lists.shape[3], dtype=jnp.int32)
    matches = listed_row[:, :, None] == block_ids[None, None, :]
    return jnp.sum(matches.astype(jnp.float32), axis=1)


def halves(value):
    high = value.astype(jnp.bfloat16)
    return high, (value - high.astype(jnp.float32)).astype(jnp.bfloat16)


def three_products(left_high, left_low, right_high, right_low):
    dot = functools.partial(jnp.dot, preferred_element_type=jnp.float32)
    small = dot(left_low, right_high) + dot(left_high, right_low)
    return dot(left_high, right_high) + small


def after(value, *others):
    return lax.optimization_barrier((value, *others))[0]


def permute(value, target):
    n_aux, n_orb = lax.axis_size("aux"), lax.axis_size("orb")
    pairs = []
    for a in range(n_aux):
        for o in range(n_orb):
            to_aux, to_orb = target(a, o)
            pairs.append((a * n_orb + o, to_aux * n_orb + to_orb))
    return lax.ppermute(value, ("aux", "orb"), pairs)


def swap(value, aux_bits=0, orb_bits=0):
    return permute(value, lambda a, o: (a ^ aux_bits, o ^ orb_bits))


def together(*gathers):
    arrays = [array for g in gathers for array in (g.arrays() if isinstance(g, Gather) else g)]
    arrays = list(lax.optimization_barrier(tuple(arrays)))
    found = [g for g in gathers if isinstance(g, Gather)]
    return [Gather([(arrays.pop(0), keys) for keys in g.keys()]) for g in found]


def bits_of(size):
    return [1 << at for at in reversed(range(size.bit_length() - 1))]


class Gather:
    def __init__(self, parts):
        self.parts = parts

    def step(self, aux_bits=0, orb_bits=0, stack=True):
        parts = list(self.parts)
        for array, keys in self.parts:
            got = swap(array, aux_bits, orb_bits)
            names = [(a ^ aux_bits, o ^ orb_bits if orb_bits else o) for a, o in keys]
            if stack:
                parts = [(jnp.concatenate([array, got], axis=0), keys + names)]
            else:
                parts.append((got, names))
        return Gather(parts)

    def rows(self, start, stop):
        return Gather([(array[:, start:stop], keys) for array, keys in self.parts])

    def at(self, time):
        return Gather([(array[:, time], keys) for array, keys in self.parts])

    def after(self, *others):
        return Gather([(after(array, *others), keys) for array, keys in self.parts])

    def arrays(self):
        return [array for array, _ in self.parts]

    def keys(self):
        return [keys for _, keys in self.parts]


def owner_of(my_orb, key):
    return key[0] if isinstance(key, tuple) else my_orb ^ key


def split_integrals_kernel(listed, integrals, *outs):
    aux_count, block, orbitals = integrals.shape
    for n in range(orbitals // block):
        cols = slice(n * block, (n + 1) * block)
        part = integrals[:, :, cols].reshape(aux_count * block, block)
        for time in range(listed.shape[0]):
            outs[2 * time][:, cols], outs[2 * time + 1][:, cols] = halves(part * listed[time, n])


def split_integrals(listed, integrals):
    aux_count, block, orbitals = integrals.shape
    times = listed.shape[0]
    shape = jax.ShapeDtypeStruct((aux_count * block, orbitals), jnp.bfloat16)
    return pl.pallas_call(
        split_integrals_kernel,
        out_shape=[shape] * (2 * times),
        in_specs=[SMEM, VMEM],
        out_specs=[VMEM] * (2 * times),
        compiler_params=PARAMS,
        cost_estimate=cost(8 * aux_count * block * orbitals, 12 * aux_count * block * orbitals),
        name="split_integrals",
    )(listed, integrals)


def half_kernel(keys, time, split, position, listed, a_high, a_low, *rest):
    refs, (out, b_high, b_low) = rest[: len(keys)], rest[len(keys) :]
    my_aux, my_orb = position[0], position[1]
    _, share, block, _ = out.shape
    for ref, (names, offset, stride) in zip(refs, keys):
        rows, cols = ref.shape[1:]
        for at, (aux_bits, orb_bits) in enumerate(names):
            row = pl.multiple_of(owner_of(my_orb, orb_bits) * stride + offset, rows)
            col = pl.multiple_of((my_aux ^ aux_bits) * cols, cols)
            high, low = halves(ref[at])
            b_high[pl.ds(row, rows), pl.ds(col, cols)] = high
            b_low[pl.ds(row, rows), pl.ds(col, cols)] = low
    width = 2 * block
    for pair in range(b_high.shape[1] // width):
        cols = slice(pair * width, (pair + 1) * width)
        product = three_products(a_high[...], a_low[...], b_high[:, cols], b_low[:, cols])
        for side in range(2):
            column = pair * 2 + side
            part = product[:, side * block : (side + 1) * block] * listed[time, column]
            part = part.reshape(split, share, block, block)
            for h in range(split):
                out[column * split + h] = part[h]


def half_products(position, listed, a_split, sources, time, split, block):
    a_high, a_low = a_split
    rows, orbitals = a_high.shape
    aux_count = rows // block
    shape = (orbitals // block * split, aux_count // split, block, block)
    arrays, keys = [], []
    for gathered, offset, stride in sources:
        for array, names in gathered.parts:
            arrays.append(array)
            keys.append((names, offset, stride))
    return pl.pallas_call(
        functools.partial(half_kernel, keys, time, split),
        out_shape=jax.ShapeDtypeStruct(shape, jnp.float32),
        in_specs=[SMEM, SMEM, VMEM, VMEM] + [VMEM] * len(arrays),
        out_specs=VMEM,
        scratch_shapes=[pltpu.VMEM((orbitals, orbitals), jnp.bfloat16)] * 2,
        compiler_params=PARAMS,
        cost_estimate=cost(6 * aux_count * block * orbitals * orbitals, 10 * orbitals * orbitals),
        name="half_products",
    )(position, listed, a_high, a_low, *arrays)


def split_kernel(keys, position, *rest):
    refs, (high_ref, low_ref) = rest[: len(keys)], rest[len(keys) :]
    my_aux, my_orb = position[0], position[1]
    for ref, names in zip(refs, keys):
        rows, cols = ref.shape[1:]
        for at, (aux_bits, orb_bits) in enumerate(names):
            row = pl.multiple_of(owner_of(my_orb, orb_bits) * rows, rows)
            col = pl.multiple_of((my_aux ^ aux_bits) * cols, cols)
            high, low = halves(ref[at])
            high_ref[pl.ds(row, rows), pl.ds(col, cols)] = high
            low_ref[pl.ds(row, rows), pl.ds(col, cols)] = low


def split_whole(position, gathered, orbitals):
    return pl.pallas_call(
        functools.partial(split_kernel, gathered.keys()),
        out_shape=[jax.ShapeDtypeStruct((orbitals, orbitals), jnp.bfloat16)] * 2,
        in_specs=[SMEM] + [VMEM] * len(gathered.parts),
        out_specs=[VMEM] * 2,
        compiler_params=PARAMS,
        cost_estimate=cost(4 * orbitals * orbitals, 8 * orbitals * orbitals),
        name="split_whole",
    )(position, *gathered.arrays())


def full_kernel(split, a_high, a_low, received, *rest):
    out, b_high, b_low = rest[-3:]
    units, share, block, _ = received.shape
    for source in range(units):
        rows = slice(source // split * block, (source // split + 1) * block)
        for at in range(share):
            col = (source % split * share + at) * block
            b_high[rows, col : col + block], b_low[rows, col : col + block] = halves(received[source, at])
    orbitals = a_high.shape[0]
    tile = 2 * block
    for start in range(0, orbitals, tile):
        rows = slice(start, start + tile)
        product = three_products(a_high[rows], a_low[rows], b_high[...], b_low[...])
        for at in range(share * split):
            out[0, at, 0, rows] = product[:, at * block : (at + 1) * block]


def full_products(vir, received, time, times, split, earlier):
    high, low = vir
    orbitals = high.shape[0]
    units, share, block, _ = received.shape
    aux_count = share * split
    operands = [high, low, received]
    in_specs = [VMEM] * 3
    aliases = {}
    if earlier is not None:
        aliases = {len(operands): 0}
        operands.append(earlier)
        in_specs.append(pl.BlockSpec(memory_space=pl.ANY))
    return pl.pallas_call(
        functools.partial(full_kernel, split),
        grid=(1,),
        out_shape=jax.ShapeDtypeStruct((times, aux_count, 1, orbitals, block), jnp.float32),
        in_specs=in_specs,
        out_specs=pl.BlockSpec((1, aux_count, 1, orbitals, block), lambda i: (time, 0, 0, 0, 0)),
        scratch_shapes=[pltpu.VMEM((orbitals, aux_count * block), jnp.bfloat16)] * 2,
        input_output_aliases=aliases,
        compiler_params=PARAMS,
        cost_estimate=cost(6 * aux_count * block * orbitals * orbitals, 12 * orbitals * orbitals),
        name="full_products",
    )(*operands)


def local(three_center, tile_lists, occ_density, vir_density):
    integrals = three_center.reshape(three_center.shape[0], *three_center.shape[2:])
    block, orbitals = three_center.shape[2:]
    owners, n_aux = lax.axis_size("orb"), lax.axis_size("aux")
    split = owners // (orbitals // block)
    unit = lax.axis_index("orb")
    position = jnp.stack([lax.axis_index("aux"), unit]).astype(jnp.int32)
    times = occ_density.shape[0]
    orb_bits, aux_bits = bits_of(owners), bits_of(n_aux)
    core_bit, far_bits = aux_bits[-1], aux_bits[:-1]

    listed = listed_mask(tile_lists, unit % split, unit // split)
    a_split = split_integrals(listed, integrals)

    half_rows = occ_density.shape[1] // 2

    def begin(value):
        return Gather([(value[None], [(0, 0)])])

    def products(sources, time):
        pair = a_split[2 * time : 2 * time + 2]
        return half_products(position, listed, pair, sources, time, split, block)

    def deliver(made):
        return lax.all_to_all(made, "orb", split_axis=0, concat_axis=0, tiled=True)

    far_orb, middle_orb, near_orb = orb_bits[0], orb_bits[1:-1], orb_bits[-1]

    def over_orb(value):
        whole = lax.all_gather(value, "orb", axis=0)
        return Gather([(whole, [(0, (owner,)) for owner in range(owners)])])

    begun = begin(occ_density[0]).step(orb_bits=far_orb)
    begun = together(begun, a_split)[0]
    one, two = begun.rows(0, half_rows), begun.rows(half_rows, 2 * half_rows)
    for bit in middle_orb:
        one = one.step(orb_bits=bit)
    for bit in far_bits:
        two = two.step(aux_bits=bit)
    one, two = together(one, two)
    rest = over_orb(jnp.concatenate([occ_density[1:], vir_density], axis=0))
    one = one.step(orb_bits=near_orb)
    for bit in middle_orb:
        two = two.step(orb_bits=bit)
    for bit in far_bits:
        one = one.step(aux_bits=bit, stack=False)
    two = two.step(orb_bits=near_orb, stack=False)
    one = one.step(aux_bits=core_bit, stack=False)
    two = two.step(aux_bits=core_bit, stack=False)
    sources = [(one, 0, 2 * half_rows), (two, half_rows, 2 * half_rows)]
    made = products(sources, 0)
    received = [deliver(made)]
    rest = rest.after(made)

    def cross(gathered):
        for bit in far_bits:
            gathered = gathered.step(aux_bits=bit, stack=False)
        return gathered

    def finish(gathered):
        return gathered.step(aux_bits=core_bit, stack=False)

    for time in range(1, times):
        made = products([(finish(cross(rest.at(time - 1))), 0, 2 * half_rows)], time)
        received.append(deliver(made))
    virs = [cross(rest.at(times - 1 + time)) for time in range(times)]
    coupled = None
    for time in range(times):
        gathered = virs[time] if coupled is None else virs[time].after(coupled)
        whole = split_whole(position, finish(gathered), orbitals)
        coupled = full_products(whole, received[time], time, times, split, coupled)
    return coupled


def solution(mesh):
    in_specs = (
        P("aux", "orb", None, None),
        P(None, "aux", None, None),
        P(None, "orb", "aux"),
        P(None, "orb", "aux"),
    )
    out_specs = P(None, "aux", "orb", None, None)
    return jax.shard_map(local, mesh=mesh, in_specs=in_specs, out_specs=out_specs, check_vma=False)
```

time: 255 us -> 214 us (0.84)
  the two profiles are of different devices: /device:TPU:10 before, /device:TPU:0 now
where the time goes in v2:
time: 214 us
  waiting for transfers between devices  115 us (54%)
  Pallas kernels  46.3 us (22%)
  starting transfers between devices  25.6 us (12%)
  between operations  13.6 us (6%)
  local copies, waits for them, and re-layouts  10 us (5%)
  other arithmetic  3.05 us (1%)
    ppermute x20, waiting for transfers between devices, permute(): return lax.ppermute(value, ('aux', 'orb'), pairs)  106 us
    pallas_call x2, Pallas kernels, half_products(): pl.pallas_call(functools.partial(half_kernel, keys, time, split), out_sha...  16.6 us
    pallas_call x2, Pallas kernels, full_products(): pl.pallas_call(functools.partial(full_kernel, split), grid=(1,), out_shap...  15.5 us
    ppermute x20, starting transfers between devices, permute(): return lax.ppermute(value, ('aux', 'orb'), pairs)  14.7 us
    all_to_all x2, starting transfers between devices, deliver(): return lax.all_to_all(made, 'orb', split_axis=0, concat_axis=0, tiled=True)  10.9 us
    pallas_call x2, Pallas kernels, split_whole(): pl.pallas_call(functools.partial(split_kernel, gathered.keys()), out_shap...  9.69 us
    unnamed x42, local copies, waits for them, and re-layouts  5.81 us
    all_gather x1, waiting for transfers between devices, over_orb(): whole = lax.all_gather(value, 'orb', axis=0)  4.55 us
  transfers between devices with their start and end apart: 23, of which 16 were waited for; matrix products, arithmetic and copies ran while one was open for 2% of the time, Pallas kernels for 18%

profile of v2, /device:TPU:0, one launch (start us, length us, event | category | flops | bytes accessed | tf_op | source)
XLA Modules:
  0.0 213.5 jit_solution(1423201899835343330)
XLA Ops:
  7.5 1.7 pad_maximum_fusion
  9.3 4.1 %collective-permute-start = (f32[1,128,256]{2,1,0:T(8,128)S(1)}, f32[1,128,256]{2,1,0:T(8,128)S(1)}, u32[]{:S(2)}, u32[]{:S(2)}) collective-permute-start(f32[1,128,256]{2,1,0:T(8,128)S(1)} %get-tuple-element.38), channel_id=1, source_target_pairs={{0,4},{1,5},{2,6},{3,7},{4,0},{5,1},{6,2},{7,3},{8,12},{9,13},{10,... | collective-permute-start | bytes 393224 | tf_op jit(solution)/shard_map/ppermute | solution.py:50
  14.0 4.5 %split_integrals.1 = (bf16[512,1024]{1,0:T(8,128)(2,1)}, bf16[512,1024]{1,0:T(8,128)(2,1)}, bf16[512,1024]{1,0:T(8,128)(2,1)}, bf16[512,1024]{1,0:T(8,128)(2,1)}) custom-call(f32[2,8]{1,0:T(2,128)} %convert_reduce_fusion.listed, f32[4,128,1024]{2,1,0:T(8,128)} %bitcast.12), custom_call_target="tpu_custom_call" | custom-call | flops 4194304 | bytes 6291456 | tf_op jit(solution)/shard_map/split_integrals/pallas_call | solution.py:116
  18.6 1.1 collective-permute-done
  19.8 1.6 collective-permute-start.2
  22.0 2.8 %collective-permute-done.2 = f32[2,64,256]{2,1,0:T(8,128)S(1)} collective-permute-done((f32[2,64,256]{2,1,0:T(8,128)S(1)}, f32[2,64,256]{2,1,0:T(8,128)S(1)}, u32[]{:S(2)}, u32[]{:S(2)}) %collective-permute-start.2) | collective-permute-done | bytes 131104 | tf_op jit(solution)/shard_map/ppermute | solution.py:50
  24.8 7.3 %collective-permute-done.1 = f32[2,64,256]{2,1,0:T(8,128)S(1)} collective-permute-done((f32[2,64,256]{2,1,0:T(8,128)S(1)}, f32[2,64,256]{2,1,0:T(8,128)S(1)}, u32[]{:S(2)}, u32[]{:S(2)}) %collective-permute-start.1) | collective-permute-done | bytes 131104 | tf_op jit(solution)/shard_map/ppermute | solution.py:50
  32.2 1.3 collective-permute-start.3
  33.5 10.2 %collective-permute-done.7 = f32[4,64,256]{2,1,0:T(8,128)S(1)} collective-permute-done((f32[4,64,256]{2,1,0:T(8,128)S(1)}, f32[4,64,256]{2,1,0:T(8,128)S(1)}, u32[]{:S(2)}, u32[]{:S(2)}) %collective-permute-start.7) | collective-permute-done | bytes 262176 | tf_op jit(solution)/shard_map/ppermute | solution.py:50
  43.8 1.6 collective-permute-start.8
  46.5 18.6 %collective-permute-done.8.rest_5_ = f32[8,64,256]{2,1,0:T(8,128)S(1)} collective-permute-done((f32[8,64,256]{2,1,0:T(8,128)S(1)}, f32[8,64,256]{2,1,0:T(8,128)S(1)}, u32[]{:S(2)}, u32[]{:S(2)}) %collective-permute-start.8) | collective-permute-done | bytes 524320 | tf_op jit(solution)/shard_map/ppermute | solution.py:50
  67.9 8.2 %half_products.2 = f32[8,4,128,128]{3,2,1,0:T(8,128)} custom-call(s32[2]{0:T(128)} %pad_add_fusion.position, f32[2,8]{1,0:T(2,128)} %convert_reduce_fusion.listed, bf16[512,1024]{1,0:T(8,128)(2,1)} %get-tuple-element.19.a_high, bf16[512,1024]{1,0:T(8,128)(2,1)} %get-tuple-element.20.a_low, f32[8,64,256]{2,1,0:T(8,128)} %copy-done.11, ...), custom_call_target="tpu_custom_call" | custom-call | flops 3221225472 | bytes 10485760 | tf_op jit(solution)/shard_map/half_products/pallas_call | solution.py:161
  76.1 7.1 %all-to-all-start = ((f32[8,4,128,128]{3,2,1,0:T(8,128)}), f32[8,4,128,128]{3,2,1,0:T(8,128)S(1)}, u32[]{:S(2)}, u32[]{:S(2)}) async-start(f32[8,4,128,128]{3,2,1,0:T(8,128)} %half_products.2), calls=%async_computation | async-start | bytes 4194304 | tf_op jit(solution)/shard_map/all_to_all | solution.py:265
  83.2 4.5 %all-gather.3.cloned.1.call-done = f32[24,128,256]{2,1,0:T(8,128)} async-done(((f32[3,128,256]{2,1,0:T(8,128)}), f32[24,128,256]{2,1,0:T(8,128)}) %all-gather.3.cloned.1.call-update) | async-done | bytes 3145744 | tf_op jit(solution)/shard_map/all_gather | solution.py:270
  87.8 3.1 %slice_bitcast_fusion = (f32[8,128,256]{2,1,0:T(8,128)S(1)}, f32[8,128,256]{2,1,0:T(8,128)}, f32[8,128,256]{2,1,0:T(8,128)S(1)}) fusion(f32[8,3,128,256]{3,2,1,0:T(8,128)} %bitcast.11), kind=kLoop, calls=%fused_computation | loop fusion | bytes 6291456 | tf_op jit(solution)/shard_map/squeeze | solution.py:87
  91.8 24.2 %collective-permute-done.17.rest_1_ = f32[8,128,256]{2,1,0:T(8,128)S(1)} collective-permute-done((f32[8,128,256]{2,1,0:T(8,128)S(1)}, f32[8,128,256]{2,1,0:T(8,128)S(1)}, u32[]{:S(2)}, u32[]{:S(2)}) %collective-permute-start.17) | collective-permute-done | bytes 1048608 | tf_op jit(solution)/shard_map/ppermute | solution.py:50
  116.0 2.6 %collective-permute-done.19.rest_3_ = f32[8,128,256]{2,1,0:T(8,128)S(1)} collective-permute-done((f32[8,128,256]{2,1,0:T(8,128)S(1)}, f32[8,128,256]{2,1,0:T(8,128)S(1)}, u32[]{:S(2)}, u32[]{:S(2)}) %collective-permute-start.19) | collective-permute-done | bytes 1048608 | tf_op jit(solution)/shard_map/ppermute | solution.py:50
  119.7 8.4 %half_products.3 = f32[8,4,128,128]{3,2,1,0:T(8,128)} custom-call(s32[2]{0:T(128)} %pad_add_fusion.position, f32[2,8]{1,0:T(2,128)} %convert_reduce_fusion.listed, bf16[512,1024]{1,0:T(8,128)(2,1)} %get-tuple-element.21.a_high, bf16[512,1024]{1,0:T(8,128)(2,1)} %get-tuple-element.22.a_low, f32[8,128,256]{2,1,0:T(8,128)} %copy-done.10, ...), custom_call_target="tpu_custom_call" | custom-call | flops 3221225472 | bytes 10485760 | tf_op jit(solution)/shard_map/half_products/pallas_call | solution.py:161
  128.1 4.2 %all-to-all-done.received = f32[8,4,128,128]{3,2,1,0:T(8,128)S(1)} async-done(((f32[8,4,128,128]{3,2,1,0:T(8,128)}), f32[8,4,128,128]{3,2,1,0:T(8,128)S(1)}, u32[]{:S(2)}, u32[]{:S(2)}) %all-to-all-start) | async-done | bytes 2097184 | tf_op jit(solution)/shard_map/all_to_all | solution.py:265
  132.3 1.3 copy-done.3
  133.6 3.8 %all-to-all-start.1 = ((f32[8,4,128,128]{3,2,1,0:T(8,128)}), f32[8,4,128,128]{3,2,1,0:T(8,128)S(1)}, u32[]{:S(2)}, u32[]{:S(2)}) async-start(f32[8,4,128,128]{3,2,1,0:T(8,128)} %half_products.3), calls=%async_computation.1 | async-start | bytes 4194304 | tf_op jit(solution)/shard_map/all_to_all | solution.py:265
  138.5 23.5 %collective-permute-done.11.rest_1_ = f32[8,128,256]{2,1,0:T(8,128)S(1)} collective-permute-done((f32[8,128,256]{2,1,0:T(8,128)}, f32[8,128,256]{2,1,0:T(8,128)S(1)}, u32[]{:S(2)}, u32[]{:S(2)}) %collective-permute-start.11) | collective-permute-done | bytes 1048608 | tf_op jit(solution)/shard_map/ppermute | solution.py:50
  162.0 1.2 collective-permute-start.14
  163.3 1.4 collective-permute-done.13.rest_3_
  165.7 4.8 %split_whole.2 = (bf16[1024,1024]{1,0:T(8,128)(2,1)}, bf16[1024,1024]{1,0:T(8,128)(2,1)}) custom-call(s32[2]{0:T(128)} %pad_add_fusion.position, f32[8,128,256]{2,1,0:T(8,128)} %get-tuple-element.34.rest_0_, f32[8,128,256]{2,1,0:T(8,128)} %copy-done.5, f32[8,128,256]{2,1,0:T(8,128)} %copy-done.6, f32[8,128,256]{2,1,0:T(8,128)} %copy-done.7), custom_call_target="tpu_custom_call" | custom-call | flops 4194304 | bytes 8388608 | tf_op jit(solution)/shard_map/split_whole/pallas_call | solution.py:187
  170.5 7.8 %full_products.2.rest_0_ = f32[2,4,1,1024,128]{4,3,2,1,0:T(8,128)} custom-call(bf16[1024,1024]{1,0:T(8,128)(2,1)} %get-tuple-element.27.a_high, bf16[1024,1024]{1,0:T(8,128)(2,1)} %get-tuple-element.28.a_low, f32[8,4,128,128]{3,2,1,0:T(8,128)} %copy-done.3), custom_call_target="tpu_custom_call" | custom-call | flops 3221225472 | bytes 12582912 | tf_op jit(solution)/shard_map/full_products/pallas_call | solution.py:227
  178.3 9.3 %collective-permute-done.14.rest_1_ = f32[8,128,256]{2,1,0:T(8,128)S(1)} collective-permute-done((f32[8,128,256]{2,1,0:T(8,128)S(1)}, f32[8,128,256]{2,1,0:T(8,128)S(1)}, u32[]{:S(2)}, u32[]{:S(2)}) %collective-permute-start.14) | collective-permute-done | bytes 1048608 | tf_op jit(solution)/shard_map/ppermute | solution.py:50
  188.1 2.1 %collective-permute-done.15.rest_2_ = f32[8,128,256]{2,1,0:T(8,128)S(1)} collective-permute-done((f32[8,128,256]{2,1,0:T(8,128)S(1)}, f32[8,128,256]{2,1,0:T(8,128)S(1)}, u32[]{:S(2)}, u32[]{:S(2)}) %collective-permute-start.15) | collective-permute-done | bytes 1048608 | tf_op jit(solution)/shard_map/ppermute | solution.py:50
  190.3 1.5 collective-permute-done.16.rest_3_
  192.7 4.9 %split_whole.3 = (bf16[1024,1024]{1,0:T(8,128)(2,1)}, bf16[1024,1024]{1,0:T(8,128)(2,1)}) custom-call(s32[2]{0:T(128)} %pad_add_fusion.position, f32[8,128,256]{2,1,0:T(8,128)} %copy-done.2, f32[8,128,256]{2,1,0:T(8,128)} %copy-done.4, f32[8,128,256]{2,1,0:T(8,128)} %copy-done.8, f32[8,128,256]{2,1,0:T(8,128)} %copy-done.9), custom_call_target="tpu_custom_call" | custom-call | flops 4194304 | bytes 8388608 | tf_op jit(solution)/shard_map/split_whole/pallas_call | solution.py:187
  197.6 1.3 copy-done.1
  198.9 7.8 %full_products.3 = f32[2,4,1,1024,128]{4,3,2,1,0:T(8,128)} custom-call(bf16[1024,1024]{1,0:T(8,128)(2,1)} %get-tuple-element.31.a_high, bf16[1024,1024]{1,0:T(8,128)(2,1)} %get-tuple-element.32.a_low, f32[8,4,128,128]{3,2,1,0:T(8,128)} %copy-done.1, f32[2,4,1,1024,128]{4,3,2,1,0:T(8,128)} %full_products.2.rest_0_), custom_call_target="tpu_custom_call", output_to_operand_aliasing={{}: (3, {})} | custom-call | flops 3221225472 | bytes 12582912 | tf_op jit(solution)/shard_map/full_products/pallas_call | solution.py:227
  (76 shorter events, 12.1 us)
Async XLA Ops:
  6.5 6.9 %copy-start = (s32[2,1,8,8]{3,2,1,0:T(8,128)S(1)}, s32[2,1,8,8]{3,2,1,0:T(8,128)}, u32[]{:S(2)}) copy-start(s32[2,1,8,8]{3,2,1,0:T(8,128)} %param.5) | copy-start | bytes 1540
  6.5 81.2 %all-gather.3.cloned.1.call-start = ((), (), s32[]{:S(2)}) async-start(), calls=%async_computation.2 | async-start | bytes 3538944 | tf_op jit(solution)/shard_map/all_gather | solution.py:270
  9.3 10.4 %collective-permute-start = (f32[1,128,256]{2,1,0:T(8,128)S(1)}, f32[1,128,256]{2,1,0:T(8,128)S(1)}, u32[]{:S(2)}, u32[]{:S(2)}) collective-permute-start(f32[1,128,256]{2,1,0:T(8,128)S(1)} %get-tuple-element.38), channel_id=1, source_target_pairs={{0,4},{1,5},{2,6},{3,7},{4,0},{5,1},{6,2},{7,3},{8,12},{9,13},{10,... | collective-permute-start | bytes 393224 | tf_op jit(solution)/shard_map/ppermute | solution.py:50
  19.8 5.0 %collective-permute-start.2 = (f32[2,64,256]{2,1,0:T(8,128)S(1)}, f32[2,64,256]{2,1,0:T(8,128)S(1)}, u32[]{:S(2)}, u32[]{:S(2)}) collective-permute-start(f32[2,64,256]{2,1,0:T(8,128)S(1)} %get-tuple-element.36), channel_id=1, source_target_pairs={{0,16},{1,17},{2,18},{3,19},{4,20},{5,21},{6,22},{7,23},{8,24},{9,... | collective-permute-start | bytes 393224 | tf_op jit(solution)/shard_map/ppermute | solution.py:50
  21.4 10.7 %collective-permute-start.1 = (f32[2,64,256]{2,1,0:T(8,128)S(1)}, f32[2,64,256]{2,1,0:T(8,128)S(1)}, u32[]{:S(2)}, u32[]{:S(2)}) collective-permute-start(f32[2,64,256]{2,1,0:T(8,128)S(1)} %get-tuple-element.37), channel_id=1, source_target_pairs={{0,2},{1,3},{2,0},{3,1},{4,6},{5,7},{6,4},{7,5},{8,10},{9,11},{10,... | collective-permute-start | bytes 393224 | tf_op jit(solution)/shard_map/ppermute | solution.py:50
  32.1 11.6 %collective-permute-start.7 = (f32[4,64,256]{2,1,0:T(8,128)S(1)}, f32[4,64,256]{2,1,0:T(8,128)S(1)}, u32[]{:S(2)}, u32[]{:S(2)}) collective-permute-start(f32[4,64,256]{2,1,0:T(8,128)S(1)} %pad_maximum_fusion.3), channel_id=1, source_target_pairs={{0,2},{1,3},{2,0},{3,1},{4,6},{5,7},{6,4},{7,5},{8,10},{9,11},{10,... | collective-permute-start | bytes 786440 | tf_op jit(solution)/shard_map/ppermute | solution.py:50
  32.2 13.1 %collective-permute-start.3 = (f32[4,64,256]{2,1,0:T(8,128)S(1)}, f32[4,64,256]{2,1,0:T(8,128)S(1)}, u32[]{:S(2)}, u32[]{:S(2)}) collective-permute-start(f32[4,64,256]{2,1,0:T(8,128)S(1)} %pad_maximum_fusion.2), channel_id=1, source_target_pairs={{0,1},{1,0},{2,3},{3,2},{4,5},{5,4},{6,7},{7,6},{8,9},{9,8},{10,11... | collective-permute-start | bytes 786440 | tf_op jit(solution)/shard_map/ppermute | solution.py:50
  43.8 24.1 %copy-start.12 = (f32[8,64,256]{2,1,0:T(8,128)}, f32[8,64,256]{2,1,0:T(8,128)S(1)}, u32[]{:S(2)}) copy-start(f32[8,64,256]{2,1,0:T(8,128)S(1)} %constant_dynamic-update-slice_fusion.2.rest_4_) | copy-start | bytes 1572868
  43.8 21.3 %collective-permute-start.8 = (f32[8,64,256]{2,1,0:T(8,128)S(1)}, f32[8,64,256]{2,1,0:T(8,128)S(1)}, u32[]{:S(2)}, u32[]{:S(2)}) collective-permute-start(f32[8,64,256]{2,1,0:T(8,128)S(1)} %constant_dynamic-update-slice_fusion.2.rest_4_), channel_id=1, source_target_pairs={{0,1},{1,0},{2,3},{3,2},{4,5},{5,4},{6,7},{7,6},{8,9},{9,8},{10,11... | collective-permute-start | bytes 1572872 | tf_op jit(solution)/shard_map/ppermute | solution.py:50
  45.4 22.5 %copy-start.11 = (f32[8,64,256]{2,1,0:T(8,128)}, f32[8,64,256]{2,1,0:T(8,128)S(1)}, u32[]{:S(2)}) copy-start(f32[8,64,256]{2,1,0:T(8,128)S(1)} %constant_dynamic-update-slice_fusion.rest_0_) | copy-start | bytes 1572868
  45.4 19.7 %collective-permute-start.4 = (f32[8,64,256]{2,1,0:T(8,128)S(1)}, f32[8,64,256]{2,1,0:T(8,128)S(1)}, u32[]{:S(2)}, u32[]{:S(2)}) collective-permute-start(f32[8,64,256]{2,1,0:T(8,128)S(1)} %constant_dynamic-update-slice_fusion.rest_0_), channel_id=1, source_target_pairs={{0,16},{1,17},{2,18},{3,19},{4,20},{5,21},{6,22},{7,23},{8,24},{9,... | collective-permute-start | bytes 1572872 | tf_op jit(solution)/shard_map/ppermute | solution.py:50
  46.0 20.2 %collective-permute-start.9 = (f32[8,64,256]{2,1,0:T(8,128)S(1)}, f32[8,64,256]{2,1,0:T(8,128)S(1)}, u32[]{:S(2)}, u32[]{:S(2)}) collective-permute-start(f32[8,64,256]{2,1,0:T(8,128)S(1)} %constant_dynamic-update-slice_fusion.2.rest_4_), channel_id=1, source_target_pairs={{0,8},{1,9},{2,10},{3,11},{4,12},{5,13},{6,14},{7,15},{8,0},{9,1},... | collective-permute-start | bytes 1572872 | tf_op jit(solution)/shard_map/ppermute | solution.py:50
  46.0 20.2 %collective-permute-start.5 = (f32[8,64,256]{2,1,0:T(8,128)S(1)}, f32[8,64,256]{2,1,0:T(8,128)S(1)}, u32[]{:S(2)}, u32[]{:S(2)}) collective-permute-start(f32[8,64,256]{2,1,0:T(8,128)S(1)} %constant_dynamic-update-slice_fusion.rest_0_), channel_id=1, source_target_pairs={{0,8},{1,9},{2,10},{3,11},{4,12},{5,13},{6,14},{7,15},{8,0},{9,1},... | collective-permute-start | bytes 1572872 | tf_op jit(solution)/shard_map/ppermute | solution.py:50
  65.1 2.8 %copy-start.16 = (f32[8,64,256]{2,1,0:T(8,128)}, f32[8,64,256]{2,1,0:T(8,128)S(1)}, u32[]{:S(2)}) copy-start(f32[8,64,256]{2,1,0:T(8,128)S(1)} %collective-permute-done.8.rest_5_) | copy-start | bytes 1572868
  65.1 2.0 collective-permute-start.10
  65.1 2.8 %copy-start.17 = (f32[8,64,256]{2,1,0:T(8,128)}, f32[8,64,256]{2,1,0:T(8,128)S(1)}, u32[]{:S(2)}) copy-start(f32[8,64,256]{2,1,0:T(8,128)S(1)} %collective-permute-done.4.rest_1_) | copy-start | bytes 1572868
  65.1 2.8 %collective-permute-start.6 = (f32[8,64,256]{2,1,0:T(8,128)S(1)}, f32[8,64,256]{2,1,0:T(8,128)}, u32[]{:S(2)}, u32[]{:S(2)}) collective-permute-start(f32[8,64,256]{2,1,0:T(8,128)S(1)} %collective-permute-done.4.rest_1_), channel_id=1, source_target_pairs={{0,8},{1,9},{2,10},{3,11},{4,12},{5,13},{6,14},{7,15},{8,0},{9,1},... | collective-permute-start | bytes 1572872 | tf_op jit(solution)/shard_map/ppermute | solution.py:50
  76.1 56.1 %all-to-all-start = ((f32[8,4,128,128]{3,2,1,0:T(8,128)}), f32[8,4,128,128]{3,2,1,0:T(8,128)S(1)}, u32[]{:S(2)}, u32[]{:S(2)}) async-start(f32[8,4,128,128]{3,2,1,0:T(8,128)} %half_products.2), calls=%async_computation | async-start | bytes 4194304 | tf_op jit(solution)/shard_map/all_to_all | solution.py:265
  90.9 27.8 %copy-start.10 = (f32[8,128,256]{2,1,0:T(8,128)}, f32[8,128,256]{2,1,0:T(8,128)S(1)}, u32[]{:S(2)}) copy-start(f32[8,128,256]{2,1,0:T(8,128)S(1)} %get-tuple-element.33.rest_0_) | copy-start | bytes 3145732
  90.9 96.7 %copy-start.2 = (f32[8,128,256]{2,1,0:T(8,128)}, f32[8,128,256]{2,1,0:T(8,128)S(1)}, u32[]{:S(2)}) copy-start(f32[8,128,256]{2,1,0:T(8,128)S(1)} %get-tuple-element.29.rest_0_) | copy-start | bytes 3145732
  90.9 25.1 %collective-permute-start.17 = (f32[8,128,256]{2,1,0:T(8,128)S(1)}, f32[8,128,256]{2,1,0:T(8,128)S(1)}, u32[]{:S(2)}, u32[]{:S(2)}) collective-permute-start(f32[8,128,256]{2,1,0:T(8,128)S(1)} %get-tuple-element.33.rest_0_), channel_id=1, source_target_pairs={{0,16},{1,17},{2,18},{3,19},{4,20},{5,21},{6,22},{7,23},{8,24},{9,... | collective-permute-start | bytes 3145736 | tf_op jit(solution)/shard_map/ppermute | solution.py:50
  91.8 24.2 %collective-permute-start.18 = (f32[8,128,256]{2,1,0:T(8,128)S(1)}, f32[8,128,256]{2,1,0:T(8,128)S(1)}, u32[]{:S(2)}, u32[]{:S(2)}) collective-permute-start(f32[8,128,256]{2,1,0:T(8,128)S(1)} %get-tuple-element.33.rest_0_), channel_id=1, source_target_pairs={{0,8},{1,9},{2,10},{3,11},{4,12},{5,13},{6,14},{7,15},{8,0},{9,1},... | collective-permute-start | bytes 3145736 | tf_op jit(solution)/shard_map/ppermute | solution.py:50
  116.0 2.7 %copy-start.13 = (f32[8,128,256]{2,1,0:T(8,128)}, f32[8,128,256]{2,1,0:T(8,128)S(1)}, u32[]{:S(2)}) copy-start(f32[8,128,256]{2,1,0:T(8,128)S(1)} %collective-permute-done.17.rest_1_) | copy-start | bytes 3145732
  116.0 2.7 %collective-permute-start.19 = (f32[8,128,256]{2,1,0:T(8,128)S(1)}, f32[8,128,256]{2,1,0:T(8,128)S(1)}, u32[]{:S(2)}, u32[]{:S(2)}) collective-permute-start(f32[8,128,256]{2,1,0:T(8,128)S(1)} %collective-permute-done.17.rest_1_), channel_id=1, source_target_pairs={{0,8},{1,9},{2,10},{3,11},{4,12},{5,13},{6,14},{7,15},{8,0},{9,1},... | collective-permute-start | bytes 3145736 | tf_op jit(solution)/shard_map/ppermute | solution.py:50
  133.6 64.0 %all-to-all-start.1 = ((f32[8,4,128,128]{3,2,1,0:T(8,128)}), f32[8,4,128,128]{3,2,1,0:T(8,128)S(1)}, u32[]{:S(2)}, u32[]{:S(2)}) async-start(f32[8,4,128,128]{3,2,1,0:T(8,128)} %half_products.3), calls=%async_computation.1 | async-start | bytes 4194304 | tf_op jit(solution)/shard_map/all_to_all | solution.py:265
  137.4 24.6 %collective-permute-start.11 = (f32[8,128,256]{2,1,0:T(8,128)}, f32[8,128,256]{2,1,0:T(8,128)S(1)}, u32[]{:S(2)}, u32[]{:S(2)}) collective-permute-start(f32[8,128,256]{2,1,0:T(8,128)} %get-tuple-element.34.rest_0_), channel_id=1, source_target_pairs={{0,16},{1,17},{2,18},{3,19},{4,20},{5,21},{6,22},{7,23},{8,24},{9,... | collective-permute-start | bytes 3145736 | tf_op jit(solution)/shard_map/ppermute | solution.py:50
  138.5 24.8 %collective-permute-start.12 = (f32[8,128,256]{2,1,0:T(8,128)}, f32[8,128,256]{2,1,0:T(8,128)S(1)}, u32[]{:S(2)}, u32[]{:S(2)}) collective-permute-start(f32[8,128,256]{2,1,0:T(8,128)} %get-tuple-element.34.rest_0_), channel_id=1, source_target_pairs={{0,8},{1,9},{2,10},{3,11},{4,12},{5,13},{6,14},{7,15},{8,0},{9,1},... | collective-permute-start | bytes 3145736 | tf_op jit(solution)/shard_map/ppermute | solution.py:50
  162.0 2.7 %collective-permute-start.13 = (f32[8,128,256]{2,1,0:T(8,128)S(1)}, f32[8,128,256]{2,1,0:T(8,128)S(1)}, u32[]{:S(2)}, u32[]{:S(2)}) collective-permute-start(f32[8,128,256]{2,1,0:T(8,128)S(1)} %collective-permute-done.11.rest_1_), channel_id=1, source_target_pairs={{0,8},{1,9},{2,10},{3,11},{4,12},{5,13},{6,14},{7,15},{8,0},{9,1},... | collective-permute-start | bytes 3145736 | tf_op jit(solution)/shard_map/ppermute | solution.py:50
  162.0 25.6 %collective-permute-start.14 = (f32[8,128,256]{2,1,0:T(8,128)S(1)}, f32[8,128,256]{2,1,0:T(8,128)S(1)}, u32[]{:S(2)}, u32[]{:S(2)}) collective-permute-start(f32[8,128,256]{2,1,0:T(8,128)S(1)} %get-tuple-element.29.rest_0_), channel_id=1, source_target_pairs={{0,16},{1,17},{2,18},{3,19},{4,20},{5,21},{6,22},{7,23},{8,24},{9,... | collective-permute-start | bytes 3145736 | tf_op jit(solution)/shard_map/ppermute | solution.py:50
  187.6 4.2 %copy-start.4 = (f32[8,128,256]{2,1,0:T(8,128)}, f32[8,128,256]{2,1,0:T(8,128)S(1)}, u32[]{:S(2)}) copy-start(f32[8,128,256]{2,1,0:T(8,128)S(1)} %collective-permute-done.14.rest_1_) | copy-start | bytes 3145732
  187.6 2.7 %collective-permute-start.15 = (f32[8,128,256]{2,1,0:T(8,128)S(1)}, f32[8,128,256]{2,1,0:T(8,128)S(1)}, u32[]{:S(2)}, u32[]{:S(2)}) collective-permute-start(f32[8,128,256]{2,1,0:T(8,128)S(1)} %get-tuple-element.29.rest_0_), channel_id=1, source_target_pairs={{0,8},{1,9},{2,10},{3,11},{4,12},{5,13},{6,14},{7,15},{8,0},{9,1},... | collective-permute-start | bytes 3145736 | tf_op jit(solution)/shard_map/ppermute | solution.py:50
  187.6 4.2 %collective-permute-start.16 = (f32[8,128,256]{2,1,0:T(8,128)S(1)}, f32[8,128,256]{2,1,0:T(8,128)S(1)}, u32[]{:S(2)}, u32[]{:S(2)}) collective-permute-start(f32[8,128,256]{2,1,0:T(8,128)S(1)} %collective-permute-done.14.rest_1_), channel_id=1, source_target_pairs={{0,8},{1,9},{2,10},{3,11},{4,12},{5,13},{6,14},{7,15},{8,0},{9,1},... | collective-permute-start | bytes 3145736 | tf_op jit(solution)/shard_map/ppermute | solution.py:50
  (11 other events, 17.3 us)
Sparse Core Ops, SparseCore 0:
  9.5 78.1 all-gather.2

commit v3 on v2

--- a/solution.py
+++ b/solution.py
@@ -54,11 +54,16 @@
     return permute(value, lambda a, o: (a ^ aux_bits, o ^ orb_bits))
 
 
-def together(*gathers):
-    arrays = [array for g in gathers for array in (g.arrays() if isinstance(g, Gather) else g)]
-    arrays = list(lax.optimization_barrier(tuple(arrays)))
-    found = [g for g in gathers if isinstance(g, Gather)]
-    return [Gather([(arrays.pop(0), keys) for keys in g.keys()]) for g in found]
+def together(*values):
+    parts = [value.arrays() if isinstance(value, Gather) else [value] for value in values]
+    arrays = list(lax.optimization_barrier(tuple(array for part in parts for array in part)))
+    found = []
+    for value in values:
+        if isinstance(value, Gather):
+            found.append(Gather([(arrays.pop(0), keys) for keys in value.keys()]))
+        else:
+            found.append(arrays.pop(0))
+    return found
 
 
 def bits_of(size):
@@ -170,29 +175,37 @@
     )(position, listed, a_high, a_low, *arrays)
 
 
-def split_kernel(keys, position, *rest):
-    refs, (high_ref, low_ref) = rest[: len(keys)], rest[len(keys) :]
-    my_aux, my_orb = position[0], position[1]
-    for ref, names in zip(refs, keys):
-        rows, cols = ref.shape[1:]
+def place_kernel(keys, span, position, *rest):
+    refs, outs = rest[: len(keys)], rest[len(keys) :]
+    for ref, (names, offset, stride) in zip(refs, keys):
+        _, times, rows, cols = ref.shape
         for at, (aux_bits, orb_bits) in enumerate(names):
-            row = pl.multiple_of(owner_of(my_orb, orb_bits) * rows, rows)
-            col = pl.multiple_of((my_aux ^ aux_bits) * cols, cols)
-            high, low = halves(ref[at])
-            high_ref[pl.ds(row, rows), pl.ds(col, cols)] = high
-            low_ref[pl.ds(row, rows), pl.ds(col, cols)] = low
-
-
-def split_whole(position, gathered, orbitals):
+            row = pl.multiple_of((position[1] ^ orb_bits) * stride + offset, rows)
+            col = pl.multiple_of((position[0] ^ aux_bits) % span * cols, cols)
+            for time in range(times):
+                high, low = halves(ref[at, time])
+                outs[2 * time][pl.ds(row, rows), pl.ds(col, cols)] = high
+                outs[2 * time + 1][pl.ds(row, rows), pl.ds(col, cols)] = low
+
+
+def place(position, gathers, orbitals, span):
+    arrays, keys, offset = [], [], 0
+    stride = sum(g.arrays()[0].shape[2] for g in gathers)
+    for g in gathers:
+        arrays += g.arrays()
+        keys += [(names, offset, stride) for names in g.keys()]
+        offset += g.arrays()[0].shape[2]
+    _, times, _, cols = arrays[0].shape
+    shape = jax.ShapeDtypeStruct((orbitals, span * cols), jnp.bfloat16)
     return pl.pallas_call(
-        functools.partial(split_kernel, gathered.keys()),
-        out_shape=[jax.ShapeDtypeStruct((orbitals, orbitals), jnp.bfloat16)] * 2,
-        in_specs=[SMEM] + [VMEM] * len(gathered.parts),
-        out_specs=[VMEM] * 2,
+        functools.partial(place_kernel, keys, span),
+        out_shape=[shape] * (2 * times),
+        in_specs=[SMEM] + [VMEM] * len(arrays),
+        out_specs=[VMEM] * (2 * times),
         compiler_params=PARAMS,
-        cost_estimate=cost(4 * orbitals * orbitals, 8 * orbitals * orbitals),
-        name="split_whole",
-    )(position, *gathered.arrays())
+        cost_estimate=cost(8 * orbitals * orbitals, 12 * orbitals * orbitals),
+        name="place",
+    )(position, *arrays)
 
 
 def full_kernel(split, a_high, a_low, received, *rest):
@@ -266,49 +279,75 @@
 
     far_orb, middle_orb, near_orb = orb_bits[0], orb_bits[1:-1], orb_bits[-1]
 
-    def over_orb(value):
-        whole = lax.all_gather(value, "orb", axis=0)
-        return Gather([(whole, [(0, (owner,)) for owner in range(owners)])])
-
-    begun = begin(occ_density[0]).step(orb_bits=far_orb)
-    begun = together(begun, a_split)[0]
-    one, two = begun.rows(0, half_rows), begun.rows(half_rows, 2 * half_rows)
-    for bit in middle_orb:
-        one = one.step(orb_bits=bit)
-    for bit in far_bits:
-        two = two.step(aux_bits=bit)
-    one, two = together(one, two)
-    rest = over_orb(jnp.concatenate([occ_density[1:], vir_density], axis=0))
-    one = one.step(orb_bits=near_orb)
-    for bit in middle_orb:
-        two = two.step(orb_bits=bit)
-    for bit in far_bits:
-        one = one.step(aux_bits=bit, stack=False)
-    two = two.step(orb_bits=near_orb, stack=False)
-    one = one.step(aux_bits=core_bit, stack=False)
-    two = two.step(aux_bits=core_bit, stack=False)
-    sources = [(one, 0, 2 * half_rows), (two, half_rows, 2 * half_rows)]
-    made = products(sources, 0)
-    received = [deliver(made)]
-    rest = rest.after(made)
+    def step(state, at):
+        if at == 0:
+            begun = state.step(orb_bits=far_orb)
+            return begun.rows(0, half_rows), begun.rows(half_rows, 2 * half_rows)
+        one, two = state
+        for bit in middle_orb if at == 1 else ():
+            one = one.step(orb_bits=bit)
+        for bit in far_bits if at == 1 else ():
+            two = two.step(aux_bits=bit)
+        for bit in middle_orb if at == 2 else ():
+            two = two.step(orb_bits=bit)
+        if at == 2:
+            one = one.step(orb_bits=near_orb)
+        for bit in far_bits if at == 3 else ():
+            one = one.step(aux_bits=bit, stack=False)
+        if at == 3:
+            two = two.step(orb_bits=near_orb, stack=False)
+        if at == 4:
+            one, two = one.step(aux_bits=core_bit, stack=False), two.step(aux_bits=core_bit, stack=False)
+        return one, two
 
     def cross(gathered):
         for bit in far_bits:
             gathered = gathered.step(aux_bits=bit, stack=False)
         return gathered
 
-    def finish(gathered):
-        return gathered.step(aux_bits=core_bit, stack=False)
-
-    for time in range(1, times):
-        made = products([(finish(cross(rest.at(time - 1))), 0, 2 * half_rows)], time)
-        received.append(deliver(made))
-    virs = [cross(rest.at(times - 1 + time)) for time in range(times)]
+    states = [begin(occ_density[time]) for time in range(times)]
+    received = []
+    for turn in range(4 + times):
+        for time in range(times):
+            if 0 <= turn - time <= 4:
+                states[time] = step(states[time], turn - time)
+        if turn < 4:
+            busy = [time for time in range(times) if turn - time >= 0]
+            waited = [g for time in busy for g in states[time]]
+            if turn == 0:
+                waited += a_split
+            if turn == 2:
+                waited.append(vir)
+            found = together(*waited)
+            if turn == 0:
+                a_split = found[2:]
+                vir = begin(vir_density).after(*found[0].arrays()).step(orb_bits=far_orb)
+            if turn == 2:
+                vir = found[-1]
+                for bit in middle_orb:
+                    vir = vir.step(orb_bits=bit)
+            for at, time in enumerate(busy):
+                states[time] = tuple(found[2 * at : 2 * at + 2])
+        time = turn - 4
+        if time >= 0:
+            one, two = states[time]
+            sources = [(one, 0, 2 * half_rows), (two, half_rows, 2 * half_rows)]
+            made = products(sources, time)
+            if time == 0:
+                made, vir, *later = together(made, vir, *[g for state in states[1:] for g in state])
+                for at in range(1, times):
+                    states[at] = tuple(later[2 * at - 2 : 2 * at])
+                over = Gather(vir.step(orb_bits=near_orb, stack=False).parts[1:])
+                vir = cross(vir)
+            if time == times - 1:
+                made, vir, over = together(made, vir, over)
+                vir = Gather(vir.parts + cross(over).parts).step(aux_bits=core_bit, stack=False)
+            received.append(deliver(made))
+    virs = place(position, [vir], orbitals, n_aux)
     coupled = None
     for time in range(times):
-        gathered = virs[time] if coupled is None else virs[time].after(coupled)
-        whole = split_whole(position, finish(gathered), orbitals)
-        coupled = full_products(whole, received[time], time, times, split, coupled)
+        pair = virs[2 * time : 2 * time + 2]
+        coupled = full_products(pair, received[time], time, times, split, coupled)
     return coupled
 
 

time: 214 us -> 192 us (0.90)
  waiting for transfers between devices: 115 us -> 98.4 us
  between operations: 13.6 us -> 0.28 us
  starting transfers between devices: 25.6 us -> 38 us
  local copies, waits for them, and re-layouts: 10 us -> 6.53 us
    ppermute x20 -> x31, starting transfers between devices: 14.7 us -> 28.4 us  [permute(): return lax.ppermute(value, ('aux', 'orb'), pairs)]
    ppermute x20 -> x31, waiting for transfers between devices: 106 us -> 93.6 us  [permute(): return lax.ppermute(value, ('aux', 'orb'), pairs)]
    all_gather x1 -> x0, waiting for transfers between devices: 4.55 us -> none  [over_orb(): whole = lax.all_gather(value, 'orb', axis=0)]
    squeeze x1 -> x0, local copies, waits for them, and re-layouts: 3.13 us -> none  [at(): return Gather([(array[:, time], keys) for array, keys in self.parts])]
    concatenate x3 -> x12, other arithmetic: 0.05 us -> 2.25 us  [step(): parts = [(jnp.concatenate([array, got], axis=0), keys + names)]]
    pallas_call x2 -> x1, Pallas kernels: 9.69 us -> 7.99 us  [place(): pl.pallas_call(functools.partial(place_kernel, keys, span), out_shape=[sh...]
    unnamed x42 -> x40, local copies, waits for them, and re-layouts: 5.81 us -> 5.53 us
  transfers between devices with their start and end apart: 23 -> 33, of which waited for: 16 -> 17; matrix products, arithmetic and copies ran while one was open for 2% -> 1% of each run, Pallas kernels for 18% -> 19%
where the time goes in v3:
time: 192 us
  waiting for transfers between devices  98.4 us (51%)
  Pallas kernels  44.8 us (23%)
  starting transfers between devices  38 us (20%)
  local copies, waits for them, and re-layouts  6.53 us (3%)
  other arithmetic  3.58 us (2%)
    ppermute x31, waiting for transfers between devices, permute(): return lax.ppermute(value, ('aux', 'orb'), pairs)  93.6 us
    ppermute x31, starting transfers between devices, permute(): return lax.ppermute(value, ('aux', 'orb'), pairs)  28.4 us
    pallas_call x2, Pallas kernels, half_products(): pl.pallas_call(functools.partial(half_kernel, keys, time, split), out_sha...  16.7 us
    pallas_call x2, Pallas kernels, full_products(): pl.pallas_call(functools.partial(full_kernel, split), grid=(1,), out_shap...  15.5 us
    all_to_all x2, starting transfers between devices, deliver(): return lax.all_to_all(made, 'orb', split_axis=0, concat_axis=0, tiled=True)  9.67 us
    pallas_call x1, Pallas kernels, place(): pl.pallas_call(functools.partial(place_kernel, keys, span), out_shape=[sh...  7.99 us
    unnamed x40, local copies, waits for them, and re-layouts  5.53 us
    all_to_all x2, waiting for transfers between devices, deliver(): return lax.all_to_all(made, 'orb', split_axis=0, concat_axis=0, tiled=True)  4.85 us
  transfers between devices with their start and end apart: 33, of which 17 were waited for; matrix products, arithmetic and copies ran while one was open for 1% of the time, Pallas kernels for 19%

profile of v3, /device:TPU:0, one launch (start us, length us, event | category | flops | bytes accessed | tf_op | source)
XLA Modules:
  0.0 191.6 jit_solution(9928696593142048931)
XLA Ops:
  1.0 4.1 %collective-permute-start.3 = (f32[1,128,256]{2,1,0:T(8,128)S(1)}, f32[1,128,256]{2,1,0:T(8,128)S(1)}, u32[]{:S(2)}, u32[]{:S(2)}) collective-permute-start(f32[1,128,256]{2,1,0:T(8,128)S(1)} %get-tuple-element.87), channel_id=1, source_target_pairs={{0,4},{1,5},{2,6},{3,7},{4,0},{5,1},{6,2},{7,3},{8,12},{9,13},{10,... | collective-permute-start | bytes 393224 | tf_op jit(solution)/shard_map/ppermute | solution.py:50
  5.9 4.6 %split_integrals.1 = (bf16[512,1024]{1,0:T(8,128)(2,1)}, bf16[512,1024]{1,0:T(8,128)(2,1)}, bf16[512,1024]{1,0:T(8,128)(2,1)}, bf16[512,1024]{1,0:T(8,128)(2,1)}) custom-call(f32[2,8]{1,0:T(2,128)} %convert_reduce_fusion.listed, f32[4,128,1024]{2,1,0:T(8,128)} %bitcast.5), custom_call_target="tpu_custom_call" | custom-call | flops 4194304 | bytes 6291456 | tf_op jit(solution)/shard_map/split_integrals/pallas_call | solution.py:121
  10.4 6.6 %collective-permute-done = f32[1,128,256]{2,1,0:T(8,128)S(1)} collective-permute-done((f32[1,128,256]{2,1,0:T(8,128)S(1)}, f32[1,128,256]{2,1,0:T(8,128)S(1)}, u32[]{:S(2)}, u32[]{:S(2)}) %collective-permute-start) | collective-permute-done | bytes 131104 | tf_op jit(solution)/shard_map/ppermute | solution.py:50
  17.1 1.6 collective-permute-start.2
  19.4 2.7 %collective-permute-done.2 = f32[2,64,256]{2,1,0:T(8,128)S(1)} collective-permute-done((f32[2,64,256]{2,1,0:T(8,128)S(1)}, f32[2,64,256]{2,1,0:T(8,128)S(1)}, u32[]{:S(2)}, u32[]{:S(2)}) %collective-permute-start.2) | collective-permute-done | bytes 131104 | tf_op jit(solution)/shard_map/ppermute | solution.py:50
  22.1 1.5 collective-permute-done.1
  24.6 3.4 %collective-permute-start.8 = (f32[1,2,128,256]{3,2,1,0:T(8,128)S(1)}, f32[1,2,128,256]{3,2,1,0:T(8,128)S(1)}, u32[]{:S(2)}, u32[]{:S(2)}) collective-permute-start(f32[1,2,128,256]{3,2,1,0:T(8,128)S(1)} %bitcast.6), channel_id=1, source_target_pairs={{0,4},{1,5},{2,6},{3,7},{4,0},{5,1},{6,2},{7,3},{8,12},{9,13},{10,... | collective-permute-start | bytes 786440 | tf_op jit(solution)/shard_map/ppermute | solution.py:50
  28.5 1.5 collective-permute-start.4
  31.3 1.6 collective-permute-done.7
  32.9 5.8 %collective-permute-done.8 = f32[1,2,128,256]{3,2,1,0:T(8,128)S(1)} collective-permute-done((f32[1,2,128,256]{3,2,1,0:T(8,128)S(1)}, f32[1,2,128,256]{3,2,1,0:T(8,128)S(1)}, u32[]{:S(2)}, u32[]{:S(2)}) %collective-permute-start.8) | collective-permute-done | bytes 262176 | tf_op jit(solution)/shard_map/ppermute | solution.py:50
  41.6 1.2 collective-permute-start.10
  44.2 1.5 collective-permute-start.17
  45.6 13.5 %collective-permute-done.11 = f32[4,64,256]{2,1,0:T(8,128)S(1)} collective-permute-done((f32[4,64,256]{2,1,0:T(8,128)S(1)}, f32[4,64,256]{2,1,0:T(8,128)S(1)}, u32[]{:S(2)}, u32[]{:S(2)}) %collective-permute-start.11) | collective-permute-done | bytes 262176 | tf_op jit(solution)/shard_map/ppermute | solution.py:50
  60.5 1.7 collective-permute-start.18
  62.2 1.7 collective-permute-start.19
  65.8 8.5 %half_products.2 = f32[8,4,128,128]{3,2,1,0:T(8,128)} custom-call(s32[2]{0:T(128)} %pad_add_fusion.position, f32[2,8]{1,0:T(2,128)} %convert_reduce_fusion.listed, bf16[512,1024]{1,0:T(8,128)(2,1)} %get-tuple-element.51.a_high, bf16[512,1024]{1,0:T(8,128)(2,1)} %get-tuple-element.52.a_low, f32[8,64,256]{2,1,0:T(8,128)} %copy-done.11, ...), custom_call_target="tpu_custom_call" | custom-call | flops 3221225472 | bytes 10485760 | tf_op jit(solution)/shard_map/half_products/pallas_call | solution.py:166
  75.9 5.1 %all-to-all-start.1 = ((f32[8,4,128,128]{3,2,1,0:T(8,128)}), f32[8,4,128,128]{3,2,1,0:T(8,128)S(1)}, u32[]{:S(2)}, u32[]{:S(2)}) async-start(f32[8,4,128,128]{3,2,1,0:T(8,128)} %half_products.2), calls=%async_computation.1 | async-start | bytes 4194304 | tf_op jit(solution)/shard_map/all_to_all | solution.py:278
  81.0 2.0 %collective-permute-start.25 = (f32[4,2,128,256]{3,2,1,0:T(8,128)S(1)}, f32[4,2,128,256]{3,2,1,0:T(8,128)S(1)}, u32[]{:S(2)}, u32[]{:S(2)}) collective-permute-start(f32[4,2,128,256]{3,2,1,0:T(8,128)S(1)} %pad_maximum_fusion.rest_0_), channel_id=1, source_target_pairs={{0,1},{1,0},{2,3},{3,2},{4,5},{5,4},{6,7},{7,6},{8,9},{9,8},{10,11... | collective-permute-start | bytes 3145736 | tf_op jit(solution)/shard_map/ppermute | solution.py:50
  83.0 1.2 collective-permute-start.24
  84.8 1.5 collective-permute-done.21.rest_3_
  88.8 8.2 %half_products.3 = f32[8,4,128,128]{3,2,1,0:T(8,128)} custom-call(s32[2]{0:T(128)} %pad_add_fusion.position, f32[2,8]{1,0:T(2,128)} %convert_reduce_fusion.listed, bf16[512,1024]{1,0:T(8,128)(2,1)} %get-tuple-element.49.a_high, bf16[512,1024]{1,0:T(8,128)(2,1)} %get-tuple-element.50.a_low, f32[8,64,256]{2,1,0:T(8,128)} %copy-done.9, ...), custom_call_target="tpu_custom_call" | custom-call | flops 3221225472 | bytes 10485760 | tf_op jit(solution)/shard_map/half_products/pallas_call | solution.py:166
  97.1 30.4 %collective-permute-done.25.rest_2_ = f32[4,2,128,256]{3,2,1,0:T(8,128)S(1)} collective-permute-done((f32[4,2,128,256]{3,2,1,0:T(8,128)S(1)}, f32[4,2,128,256]{3,2,1,0:T(8,128)S(1)}, u32[]{:S(2)}, u32[]{:S(2)}) %collective-permute-start.25) | collective-permute-done | bytes 1048608 | tf_op jit(solution)/shard_map/ppermute | solution.py:50
  128.5 1.4 copy-done.3
  129.9 4.5 %all-to-all-start = ((f32[8,4,128,128]{3,2,1,0:T(8,128)}), f32[8,4,128,128]{3,2,1,0:T(8,128)S(1)}, u32[]{:S(2)}, u32[]{:S(2)}) async-start(f32[8,4,128,128]{3,2,1,0:T(8,128)} %half_products.3), calls=%async_computation | async-start | bytes 4194304 | tf_op jit(solution)/shard_map/all_to_all | solution.py:278
  134.4 1.5 collective-permute-start.26
  136.4 22.7 %collective-permute-done.26.rest_3_ = f32[4,2,128,256]{3,2,1,0:T(8,128)S(1)} collective-permute-done((f32[4,2,128,256]{3,2,1,0:T(8,128)}, f32[4,2,128,256]{3,2,1,0:T(8,128)S(1)}, u32[]{:S(2)}, u32[]{:S(2)}) %collective-permute-start.26) | collective-permute-done | bytes 1048608 | tf_op jit(solution)/shard_map/ppermute | solution.py:50
  159.2 2.7 %collective-permute-done.30.rest_7_ = f32[4,2,128,256]{3,2,1,0:T(8,128)} collective-permute-done((f32[4,2,128,256]{3,2,1,0:T(8,128)S(1)}, f32[4,2,128,256]{3,2,1,0:T(8,128)}, u32[]{:S(2)}, u32[]{:S(2)}) %collective-permute-start.30) | collective-permute-done | bytes 1048608 | tf_op jit(solution)/shard_map/ppermute | solution.py:50
  161.9 8.0 %place.1 = (bf16[1024,1024]{1,0:T(8,128)(2,1)}, bf16[1024,1024]{1,0:T(8,128)(2,1)}, bf16[1024,1024]{1,0:T(8,128)(2,1)}, bf16[1024,1024]{1,0:T(8,128)(2,1)}) custom-call(s32[2]{0:T(128)} %pad_add_fusion.position, f32[4,2,128,256]{3,2,1,0:T(8,128)} %copy-done.2, f32[4,2,128,256]{3,2,1,0:T(8,128)} %collective-permute-done.24.rest_1_, ...), custom_call_target="tpu_custom_call" | custom-call | flops 8388608 | bytes 12582912 | tf_op jit(solution)/shard_map/place/pallas_call | solution.py:200
  169.9 7.8 %full_products.2.rest_0_ = f32[2,4,1,1024,128]{4,3,2,1,0:T(8,128)} custom-call(bf16[1024,1024]{1,0:T(8,128)(2,1)} %get-tuple-element.82.a_high, bf16[1024,1024]{1,0:T(8,128)(2,1)} %get-tuple-element.83.a_low, f32[8,4,128,128]{3,2,1,0:T(8,128)} %copy-done.3), custom_call_target="tpu_custom_call" | custom-call | flops 3221225472 | bytes 12582912 | tf_op jit(solution)/shard_map/full_products/pallas_call | solution.py:240
  177.7 4.8 %all-to-all-done.received = f32[8,4,128,128]{3,2,1,0:T(8,128)S(1)} async-done(((f32[8,4,128,128]{3,2,1,0:T(8,128)}), f32[8,4,128,128]{3,2,1,0:T(8,128)S(1)}, u32[]{:S(2)}, u32[]{:S(2)}) %all-to-all-start) | async-done | bytes 2097184 | tf_op jit(solution)/shard_map/all_to_all | solution.py:278
  182.5 1.3 copy-done.1
  183.9 7.8 %full_products.3 = f32[2,4,1,1024,128]{4,3,2,1,0:T(8,128)} custom-call(bf16[1024,1024]{1,0:T(8,128)(2,1)} %get-tuple-element.79.a_high, bf16[1024,1024]{1,0:T(8,128)(2,1)} %get-tuple-element.80.a_low, f32[8,4,128,128]{3,2,1,0:T(8,128)} %copy-done.1, f32[2,4,1,1024,128]{4,3,2,1,0:T(8,128)} %full_products.2.rest_0_), custom_call_target="tpu_custom_call", output_to_operand_aliasing={{}: (3, {})} | custom-call | flops 3221225472 | bytes 12582912 | tf_op jit(solution)/shard_map/full_products/pallas_call | solution.py:240
  (96 shorter events, 18.6 us)
Async XLA Ops:
  1.0 18.3 %collective-permute-start.3 = (f32[1,128,256]{2,1,0:T(8,128)S(1)}, f32[1,128,256]{2,1,0:T(8,128)S(1)}, u32[]{:S(2)}, u32[]{:S(2)}) collective-permute-start(f32[1,128,256]{2,1,0:T(8,128)S(1)} %get-tuple-element.87), channel_id=1, source_target_pairs={{0,4},{1,5},{2,6},{3,7},{4,0},{5,1},{6,2},{7,3},{8,12},{9,13},{10,... | collective-permute-start | bytes 393224 | tf_op jit(solution)/shard_map/ppermute | solution.py:50
  5.1 11.9 %collective-permute-start = (f32[1,128,256]{2,1,0:T(8,128)S(1)}, f32[1,128,256]{2,1,0:T(8,128)S(1)}, u32[]{:S(2)}, u32[]{:S(2)}) collective-permute-start(f32[1,128,256]{2,1,0:T(8,128)S(1)} %get-tuple-element.88), channel_id=1, source_target_pairs={{0,4},{1,5},{2,6},{3,7},{4,0},{5,1},{6,2},{7,3},{8,12},{9,13},{10,... | collective-permute-start | bytes 393224 | tf_op jit(solution)/shard_map/ppermute | solution.py:50
  17.1 5.0 %collective-permute-start.2 = (f32[2,64,256]{2,1,0:T(8,128)S(1)}, f32[2,64,256]{2,1,0:T(8,128)S(1)}, u32[]{:S(2)}, u32[]{:S(2)}) collective-permute-start(f32[2,64,256]{2,1,0:T(8,128)S(1)} %get-tuple-element.54), channel_id=1, source_target_pairs={{0,16},{1,17},{2,18},{3,19},{4,20},{5,21},{6,22},{7,23},{8,24},{9,... | collective-permute-start | bytes 393224 | tf_op jit(solution)/shard_map/ppermute | solution.py:50
  18.7 5.0 %collective-permute-start.1 = (f32[2,64,256]{2,1,0:T(8,128)S(1)}, f32[2,64,256]{2,1,0:T(8,128)S(1)}, u32[]{:S(2)}, u32[]{:S(2)}) collective-permute-start(f32[2,64,256]{2,1,0:T(8,128)S(1)} %get-tuple-element.53), channel_id=1, source_target_pairs={{0,2},{1,3},{2,0},{3,1},{4,6},{5,7},{6,4},{7,5},{8,10},{9,11},{10,... | collective-permute-start | bytes 393224 | tf_op jit(solution)/shard_map/ppermute | solution.py:50
  23.6 7.6 %collective-permute-start.6 = (f32[2,64,256]{2,1,0:T(8,128)S(1)}, f32[2,64,256]{2,1,0:T(8,128)S(1)}, u32[]{:S(2)}, u32[]{:S(2)}) collective-permute-start(f32[2,64,256]{2,1,0:T(8,128)S(1)} %get-tuple-element.57), channel_id=1, source_target_pairs={{0,2},{1,3},{2,0},{3,1},{4,6},{5,7},{6,4},{7,5},{8,10},{9,11},{10,... | collective-permute-start | bytes 393224 | tf_op jit(solution)/shard_map/ppermute | solution.py:50
  24.6 14.2 %collective-permute-start.8 = (f32[1,2,128,256]{3,2,1,0:T(8,128)S(1)}, f32[1,2,128,256]{3,2,1,0:T(8,128)S(1)}, u32[]{:S(2)}, u32[]{:S(2)}) collective-permute-start(f32[1,2,128,256]{3,2,1,0:T(8,128)S(1)} %bitcast.6), channel_id=1, source_target_pairs={{0,4},{1,5},{2,6},{3,7},{4,0},{5,1},{6,2},{7,3},{8,12},{9,13},{10,... | collective-permute-start | bytes 786440 | tf_op jit(solution)/shard_map/ppermute | solution.py:50
  27.9 5.0 %collective-permute-start.7 = (f32[2,64,256]{2,1,0:T(8,128)S(1)}, f32[2,64,256]{2,1,0:T(8,128)S(1)}, u32[]{:S(2)}, u32[]{:S(2)}) collective-permute-start(f32[2,64,256]{2,1,0:T(8,128)S(1)} %get-tuple-element.58), channel_id=1, source_target_pairs={{0,16},{1,17},{2,18},{3,19},{4,20},{5,21},{6,22},{7,23},{8,24},{9,... | collective-permute-start | bytes 393224 | tf_op jit(solution)/shard_map/ppermute | solution.py:50
  28.5 10.3 %collective-permute-start.4 = (f32[4,64,256]{2,1,0:T(8,128)S(1)}, f32[4,64,256]{2,1,0:T(8,128)S(1)}, u32[]{:S(2)}, u32[]{:S(2)}) collective-permute-start(f32[4,64,256]{2,1,0:T(8,128)S(1)} %pad_maximum_fusion.6), channel_id=1, source_target_pairs={{0,1},{1,0},{2,3},{3,2},{4,5},{5,4},{6,7},{7,6},{8,9},{9,8},{10,11... | collective-permute-start | bytes 786440 | tf_op jit(solution)/shard_map/ppermute | solution.py:50
  30.0 9.9 %collective-permute-start.5 = (f32[4,64,256]{2,1,0:T(8,128)S(1)}, f32[4,64,256]{2,1,0:T(8,128)S(1)}, u32[]{:S(2)}, u32[]{:S(2)}) collective-permute-start(f32[4,64,256]{2,1,0:T(8,128)S(1)} %pad_maximum_fusion.7), channel_id=1, source_target_pairs={{0,2},{1,3},{2,0},{3,1},{4,6},{5,7},{6,4},{7,5},{8,10},{9,11},{10,... | collective-permute-start | bytes 786440 | tf_op jit(solution)/shard_map/ppermute | solution.py:50
  40.8 18.5 %collective-permute-start.9 = (f32[8,64,256]{2,1,0:T(8,128)S(1)}, f32[8,64,256]{2,1,0:T(8,128)}, u32[]{:S(2)}, u32[]{:S(2)}) collective-permute-start(f32[8,64,256]{2,1,0:T(8,128)S(1)} %pad_maximum_fusion.1.rest_0_), channel_id=1, source_target_pairs={{0,16},{1,17},{2,18},{3,19},{4,20},{5,21},{6,22},{7,23},{8,24},{9,... | collective-permute-start | bytes 1572872 | tf_op jit(solution)/shard_map/ppermute | solution.py:50
  41.6 17.7 %collective-permute-start.10 = (f32[8,64,256]{2,1,0:T(8,128)}, f32[8,64,256]{2,1,0:T(8,128)}, u32[]{:S(2)}, u32[]{:S(2)}) collective-permute-start(f32[8,64,256]{2,1,0:T(8,128)} %pad_maximum_fusion.2.rest_4_), channel_id=1, source_target_pairs={{0,1},{1,0},{2,3},{3,2},{4,5},{5,4},{6,7},{7,6},{8,9},{9,8},{10,11... | collective-permute-start | bytes 1572872 | tf_op jit(solution)/shard_map/ppermute | solution.py:50
  42.8 16.4 %collective-permute-start.11 = (f32[4,64,256]{2,1,0:T(8,128)S(1)}, f32[4,64,256]{2,1,0:T(8,128)S(1)}, u32[]{:S(2)}, u32[]{:S(2)}) collective-permute-start(f32[4,64,256]{2,1,0:T(8,128)S(1)} %pad_maximum_fusion.8), channel_id=1, source_target_pairs={{0,1},{1,0},{2,3},{3,2},{4,5},{5,4},{6,7},{7,6},{8,9},{9,8},{10,11... | collective-permute-start | bytes 786440 | tf_op jit(solution)/shard_map/ppermute | solution.py:50
  43.6 15.6 %collective-permute-start.12 = (f32[4,64,256]{2,1,0:T(8,128)S(1)}, f32[4,64,256]{2,1,0:T(8,128)S(1)}, u32[]{:S(2)}, u32[]{:S(2)}) collective-permute-start(f32[4,64,256]{2,1,0:T(8,128)S(1)} %pad_maximum_fusion.9), channel_id=1, source_target_pairs={{0,2},{1,3},{2,0},{3,1},{4,6},{5,7},{6,4},{7,5},{8,10},{9,11},{10,... | collective-permute-start | bytes 786440 | tf_op jit(solution)/shard_map/ppermute | solution.py:50
  44.2 16.3 %collective-permute-start.17 = (f32[2,2,128,256]{3,2,1,0:T(8,128)S(1)}, f32[2,2,128,256]{3,2,1,0:T(8,128)S(1)}, u32[]{:S(2)}, u32[]{:S(2)}) collective-permute-start(f32[2,2,128,256]{3,2,1,0:T(8,128)S(1)} %pad_maximum_fusion.3), channel_id=1, source_target_pairs={{0,2},{1,3},{2,0},{3,1},{4,6},{5,7},{6,4},{7,5},{8,10},{9,11},{10,... | collective-permute-start | bytes 1572872 | tf_op jit(solution)/shard_map/ppermute | solution.py:50
  59.3 2.9 %collective-permute-start.13 = (f32[8,64,256]{2,1,0:T(8,128)S(1)}, f32[8,64,256]{2,1,0:T(8,128)S(1)}, u32[]{:S(2)}, u32[]{:S(2)}) collective-permute-start(f32[8,64,256]{2,1,0:T(8,128)S(1)} %pad_maximum_fusion.1.rest_0_), channel_id=1, source_target_pairs={{0,8},{1,9},{2,10},{3,11},{4,12},{5,13},{6,14},{7,15},{8,0},{9,1},... | collective-permute-start | bytes 1572872 | tf_op jit(solution)/shard_map/ppermute | solution.py:50
  59.4 6.4 %collective-permute-start.14 = (f32[8,64,256]{2,1,0:T(8,128)}, f32[8,64,256]{2,1,0:T(8,128)}, u32[]{:S(2)}, u32[]{:S(2)}) collective-permute-start(f32[8,64,256]{2,1,0:T(8,128)} %collective-permute-done.9.rest_1_), channel_id=1, source_target_pairs={{0,8},{1,9},{2,10},{3,11},{4,12},{5,13},{6,14},{7,15},{8,0},{9,1},... | collective-permute-start | bytes 1572872 | tf_op jit(solution)/shard_map/ppermute | solution.py:50
  59.9 5.9 %collective-permute-start.15 = (f32[8,64,256]{2,1,0:T(8,128)}, f32[8,64,256]{2,1,0:T(8,128)}, u32[]{:S(2)}, u32[]{:S(2)}) collective-permute-start(f32[8,64,256]{2,1,0:T(8,128)} %pad_maximum_fusion.2.rest_4_), channel_id=1, source_target_pairs={{0,8},{1,9},{2,10},{3,11},{4,12},{5,13},{6,14},{7,15},{8,0},{9,1},... | collective-permute-start | bytes 1572872 | tf_op jit(solution)/shard_map/ppermute | solution.py:50
  60.0 5.8 %collective-permute-start.16 = (f32[8,64,256]{2,1,0:T(8,128)}, f32[8,64,256]{2,1,0:T(8,128)}, u32[]{:S(2)}, u32[]{:S(2)}) collective-permute-start(f32[8,64,256]{2,1,0:T(8,128)} %collective-permute-done.10.rest_5_), channel_id=1, source_target_pairs={{0,8},{1,9},{2,10},{3,11},{4,12},{5,13},{6,14},{7,15},{8,0},{9,1},... | collective-permute-start | bytes 1572872 | tf_op jit(solution)/shard_map/ppermute | solution.py:50
  60.5 13.9 %collective-permute-start.18 = (f32[8,64,256]{2,1,0:T(8,128)S(1)}, f32[8,64,256]{2,1,0:T(8,128)S(1)}, u32[]{:S(2)}, u32[]{:S(2)}) collective-permute-start(f32[8,64,256]{2,1,0:T(8,128)S(1)} %pad_maximum_fusion.4.rest_0_), channel_id=1, source_target_pairs={{0,16},{1,17},{2,18},{3,19},{4,20},{5,21},{6,22},{7,23},{8,24},{9,... | collective-permute-start | bytes 1572872 | tf_op jit(solution)/shard_map/ppermute | solution.py:50
  62.2 13.7 %collective-permute-start.19 = (f32[8,64,256]{2,1,0:T(8,128)S(1)}, f32[8,64,256]{2,1,0:T(8,128)}, u32[]{:S(2)}, u32[]{:S(2)}) collective-permute-start(f32[8,64,256]{2,1,0:T(8,128)S(1)} %pad_maximum_fusion.5.rest_4_), channel_id=1, source_target_pairs={{0,1},{1,0},{2,3},{3,2},{4,5},{5,4},{6,7},{7,6},{8,9},{9,8},{10,11... | collective-permute-start | bytes 1572872 | tf_op jit(solution)/shard_map/ppermute | solution.py:50
  75.9 52.6 %all-to-all-start.1 = ((f32[8,4,128,128]{3,2,1,0:T(8,128)}), f32[8,4,128,128]{3,2,1,0:T(8,128)S(1)}, u32[]{:S(2)}, u32[]{:S(2)}) async-start(f32[8,4,128,128]{3,2,1,0:T(8,128)} %half_products.2), calls=%async_computation.1 | async-start | bytes 4194304 | tf_op jit(solution)/shard_map/all_to_all | solution.py:278
  81.0 3.8 %collective-permute-start.20 = (f32[8,64,256]{2,1,0:T(8,128)}, f32[8,64,256]{2,1,0:T(8,128)S(1)}, u32[]{:S(2)}, u32[]{:S(2)}) collective-permute-start(f32[8,64,256]{2,1,0:T(8,128)} %copy-done.9), channel_id=1, source_target_pairs={{0,8},{1,9},{2,10},{3,11},{4,12},{5,13},{6,14},{7,15},{8,0},{9,1},... | collective-permute-start | bytes 1572872 | tf_op jit(solution)/shard_map/ppermute | solution.py:50
  81.0 46.4 %collective-permute-start.25 = (f32[4,2,128,256]{3,2,1,0:T(8,128)S(1)}, f32[4,2,128,256]{3,2,1,0:T(8,128)S(1)}, u32[]{:S(2)}, u32[]{:S(2)}) collective-permute-start(f32[4,2,128,256]{3,2,1,0:T(8,128)S(1)} %pad_maximum_fusion.rest_0_), channel_id=1, source_target_pairs={{0,1},{1,0},{2,3},{3,2},{4,5},{5,4},{6,7},{7,6},{8,9},{9,8},{10,11... | collective-permute-start | bytes 3145736 | tf_op jit(solution)/shard_map/ppermute | solution.py:50
  83.0 45.4 %collective-permute-start.24 = (f32[4,2,128,256]{3,2,1,0:T(8,128)S(1)}, f32[4,2,128,256]{3,2,1,0:T(8,128)}, u32[]{:S(2)}, u32[]{:S(2)}) collective-permute-start(f32[4,2,128,256]{3,2,1,0:T(8,128)S(1)} %pad_maximum_fusion.rest_0_), channel_id=1, source_target_pairs={{0,16},{1,17},{2,18},{3,19},{4,20},{5,21},{6,22},{7,23},{8,24},{9,... | collective-permute-start | bytes 3145736 | tf_op jit(solution)/shard_map/ppermute | solution.py:50
  84.3 2.9 %collective-permute-start.22 = (f32[8,64,256]{2,1,0:T(8,128)}, f32[8,64,256]{2,1,0:T(8,128)S(1)}, u32[]{:S(2)}, u32[]{:S(2)}) collective-permute-start(f32[8,64,256]{2,1,0:T(8,128)} %copy-done.10), channel_id=1, source_target_pairs={{0,8},{1,9},{2,10},{3,11},{4,12},{5,13},{6,14},{7,15},{8,0},{9,1},... | collective-permute-start | bytes 1572872 | tf_op jit(solution)/shard_map/ppermute | solution.py:50
  84.8 3.1 %collective-permute-start.23 = (f32[8,64,256]{2,1,0:T(8,128)}, f32[8,64,256]{2,1,0:T(8,128)S(1)}, u32[]{:S(2)}, u32[]{:S(2)}) collective-permute-start(f32[8,64,256]{2,1,0:T(8,128)} %collective-permute-done.19.rest_5_), channel_id=1, source_target_pairs={{0,8},{1,9},{2,10},{3,11},{4,12},{5,13},{6,14},{7,15},{8,0},{9,1},... | collective-permute-start | bytes 1572872 | tf_op jit(solution)/shard_map/ppermute | solution.py:50
  129.9 52.7 %all-to-all-start = ((f32[8,4,128,128]{3,2,1,0:T(8,128)}), f32[8,4,128,128]{3,2,1,0:T(8,128)S(1)}, u32[]{:S(2)}, u32[]{:S(2)}) async-start(f32[8,4,128,128]{3,2,1,0:T(8,128)} %half_products.3), calls=%async_computation | async-start | bytes 4194304 | tf_op jit(solution)/shard_map/all_to_all | solution.py:278
  134.4 24.7 %collective-permute-start.26 = (f32[4,2,128,256]{3,2,1,0:T(8,128)}, f32[4,2,128,256]{3,2,1,0:T(8,128)S(1)}, u32[]{:S(2)}, u32[]{:S(2)}) collective-permute-start(f32[4,2,128,256]{3,2,1,0:T(8,128)} %copy-done.4), channel_id=1, source_target_pairs={{0,16},{1,17},{2,18},{3,19},{4,20},{5,21},{6,22},{7,23},{8,24},{9,... | collective-permute-start | bytes 3145736 | tf_op jit(solution)/shard_map/ppermute | solution.py:50
  135.9 23.2 %collective-permute-start.29 = (f32[4,2,128,256]{3,2,1,0:T(8,128)}, f32[4,2,128,256]{3,2,1,0:T(8,128)S(1)}, u32[]{:S(2)}, u32[]{:S(2)}) collective-permute-start(f32[4,2,128,256]{3,2,1,0:T(8,128)} %copy-done.4), channel_id=1, source_target_pairs={{0,8},{1,9},{2,10},{3,11},{4,12},{5,13},{6,14},{7,15},{8,0},{9,1},... | collective-permute-start | bytes 3145736 | tf_op jit(solution)/shard_map/ppermute | solution.py:50
  135.9 23.2 %collective-permute-start.27 = (f32[4,2,128,256]{3,2,1,0:T(8,128)S(1)}, f32[4,2,128,256]{3,2,1,0:T(8,128)S(1)}, u32[]{:S(2)}, u32[]{:S(2)}) collective-permute-start(f32[4,2,128,256]{3,2,1,0:T(8,128)S(1)} %pad_maximum_fusion.rest_0_), channel_id=1, source_target_pairs={{0,8},{1,9},{2,10},{3,11},{4,12},{5,13},{6,14},{7,15},{8,0},{9,1},... | collective-permute-start | bytes 3145736 | tf_op jit(solution)/shard_map/ppermute | solution.py:50
  136.4 22.7 %collective-permute-start.28 = (f32[4,2,128,256]{3,2,1,0:T(8,128)}, f32[4,2,128,256]{3,2,1,0:T(8,128)S(1)}, u32[]{:S(2)}, u32[]{:S(2)}) collective-permute-start(f32[4,2,128,256]{3,2,1,0:T(8,128)} %collective-permute-done.24.rest_1_), channel_id=1, source_target_pairs={{0,8},{1,9},{2,10},{3,11},{4,12},{5,13},{6,14},{7,15},{8,0},{9,1},... | collective-permute-start | bytes 3145736 | tf_op jit(solution)/shard_map/ppermute | solution.py:50
  159.1 2.8 %collective-permute-start.30 = (f32[4,2,128,256]{3,2,1,0:T(8,128)S(1)}, f32[4,2,128,256]{3,2,1,0:T(8,128)}, u32[]{:S(2)}, u32[]{:S(2)}) collective-permute-start(f32[4,2,128,256]{3,2,1,0:T(8,128)S(1)} %collective-permute-done.26.rest_3_), channel_id=1, source_target_pairs={{0,8},{1,9},{2,10},{3,11},{4,12},{5,13},{6,14},{7,15},{8,0},{9,1},... | collective-permute-start | bytes 3145736 | tf_op jit(solution)/shard_map/ppermute | solution.py:50
  (21 other events, 180.4 us)

commit v4 on v3

--- a/solution.py
+++ b/solution.py
@@ -7,7 +7,7 @@
 from jax.experimental.pallas import tpu as pltpu
 from jax.sharding import PartitionSpec as P
 
-VMEM_BYTES = 56 * 1024 * 1024
+VMEM_BYTES = 32 * 1024 * 1024
 SMEM = pl.BlockSpec(memory_space=pltpu.SMEM)
 VMEM = pl.BlockSpec(memory_space=pltpu.VMEM)
 PARAMS = pltpu.CompilerParams(vmem_limit_bytes=VMEM_BYTES)
@@ -321,6 +321,7 @@
             found = together(*waited)
             if turn == 0:
                 a_split = found[2:]
+                states[1:] = [state.after(*found[0].arrays()) for state in states[1:]]
                 vir = begin(vir_density).after(*found[0].arrays()).step(orb_bits=far_orb)
             if turn == 2:
                 vir = found[-1]

time: 192 us -> 189 us (0.984)
  Pallas kernels: 44.8 us -> 25.1 us
  local copies, waits for them, and re-layouts: 6.53 us -> 24.3 us
    unnamed x40 -> x61, local copies, waits for them, and re-layouts: 5.53 us -> 23.3 us
    pallas_call x2, Pallas kernels: 16.7 us -> 11 us  [half_products(): pl.pallas_call(functools.partial(half_kernel, keys, time, split), out_sha...]
    pallas_call x2, Pallas kernels: 15.5 us -> 9.8 us  [full_products(): pl.pallas_call(functools.partial(full_kernel, split), grid=(1,), out_shap...]
    pallas_call x1, Pallas kernels: 7.99 us -> 2.51 us  [place(): pl.pallas_call(functools.partial(place_kernel, keys, span), out_shape=[sh...]
    ppermute x31, waiting for transfers between devices: 93.6 us -> 88.1 us  [permute(): return lax.ppermute(value, ('aux', 'orb'), pairs)]
    all_to_all x2, waiting for transfers between devices: 4.85 us -> 9.33 us  [deliver(): return lax.all_to_all(made, 'orb', split_axis=0, concat_axis=0, tiled=True)]
    pallas_call x1, Pallas kernels: 4.57 us -> 1.87 us  [split_integrals(): pl.pallas_call(split_integrals_kernel, out_shape=[shape] * (2 * times), i...]
  transfers between devices with their start and end apart: 33 -> 33, of which waited for: 17 -> 18; matrix products, arithmetic and copies ran while one was open for 1% -> 1% of each run, Pallas kernels for 19% -> 11%
where the time goes in v4:
time: 189 us; the launch traced here: 188 us
  waiting for transfers between devices  97.4 us (52%)
  starting transfers between devices  38.8 us (21%)
  Pallas kernels  25.1 us (13%)
  local copies, waits for them, and re-layouts  24.3 us (13%)
    ppermute x31, waiting for transfers between devices, permute(): return lax.ppermute(value, ('aux', 'orb'), pairs)  88.1 us
    ppermute x31, starting transfers between devices, permute(): return lax.ppermute(value, ('aux', 'orb'), pairs)  29.3 us
    unnamed x61, local copies, waits for them, and re-layouts  23.3 us
    pallas_call x2, Pallas kernels, half_products(): pl.pallas_call(functools.partial(half_kernel, keys, time, split), out_sha...  11 us
    pallas_call x2, Pallas kernels, full_products(): pl.pallas_call(functools.partial(full_kernel, split), grid=(1,), out_shap...  9.8 us
    all_to_all x2, starting transfers between devices, deliver(): return lax.all_to_all(made, 'orb', split_axis=0, concat_axis=0, tiled=True)  9.52 us
    all_to_all x2, waiting for transfers between devices, deliver(): return lax.all_to_all(made, 'orb', split_axis=0, concat_axis=0, tiled=True)  9.33 us
  transfers between devices with their start and end apart: 33, of which 18 were waited for; matrix products, arithmetic and copies ran while one was open for 1% of the time, Pallas kernels for 11%

profile of v4, /device:TPU:0, one launch (start us, length us, event | category | flops | bytes accessed | tf_op | source)
XLA Modules:
  0.0 187.9 jit_solution(18014898621875488117)
XLA Ops:
  1.0 4.1 %collective-permute-start = (f32[1,128,256]{2,1,0:T(8,128)S(1)}, f32[1,128,256]{2,1,0:T(8,128)S(1)}, u32[]{:S(2)}, u32[]{:S(2)}) collective-permute-start(f32[1,128,256]{2,1,0:T(8,128)S(1)} %get-tuple-element.90), channel_id=1, source_target_pairs={{0,4},{1,5},{2,6},{3,7},{4,0},{5,1},{6,2},{7,3},{8,12},{9,13},{10,... | collective-permute-start | bytes 393224 | tf_op jit(solution)/shard_map/ppermute | solution.py:50
  5.2 1.6 copy-done.5
  6.8 1.9 split_integrals.1
  8.7 2.7 %collective-permute-done = f32[1,128,256]{2,1,0:T(8,128)S(1)} collective-permute-done((f32[1,128,256]{2,1,0:T(8,128)S(1)}, f32[1,128,256]{2,1,0:T(8,128)S(1)}, u32[]{:S(2)}, u32[]{:S(2)}) %collective-permute-start) | collective-permute-done | bytes 131104 | tf_op jit(solution)/shard_map/ppermute | solution.py:50
  11.5 4.1 %collective-permute-start.1 = (f32[2,64,256]{2,1,0:T(8,128)S(1)}, f32[2,64,256]{2,1,0:T(8,128)S(1)}, u32[]{:S(2)}, u32[]{:S(2)}) collective-permute-start(f32[2,64,256]{2,1,0:T(8,128)S(1)} %get-tuple-element.54), channel_id=1, source_target_pairs={{0,2},{1,3},{2,0},{3,1},{4,6},{5,7},{6,4},{7,5},{8,10},{9,11},{10,... | collective-permute-start | bytes 393224 | tf_op jit(solution)/shard_map/ppermute | solution.py:50
  15.6 1.5 collective-permute-start.2
  17.1 3.1 %collective-permute-done.3 = f32[1,128,256]{2,1,0:T(8,128)S(1)} collective-permute-done((f32[1,128,256]{2,1,0:T(8,128)S(1)}, f32[1,128,256]{2,1,0:T(8,128)S(1)}, u32[]{:S(2)}, u32[]{:S(2)}) %collective-permute-start.3) | collective-permute-done | bytes 131104 | tf_op jit(solution)/shard_map/ppermute | solution.py:50
  20.9 3.1 %collective-permute-start.8 = (f32[1,2,128,256]{3,2,1,0:T(8,128)S(1)}, f32[1,2,128,256]{3,2,1,0:T(8,128)S(1)}, u32[]{:S(2)}, u32[]{:S(2)}) collective-permute-start(f32[1,2,128,256]{3,2,1,0:T(8,128)S(1)} %bitcast.6), channel_id=1, source_target_pairs={{0,4},{1,5},{2,6},{3,7},{4,0},{5,1},{6,2},{7,3},{8,12},{9,13},{10,... | collective-permute-start | bytes 786440 | tf_op jit(solution)/shard_map/ppermute | solution.py:50
  24.0 1.5 collective-permute-start.7
  25.5 1.5 collective-permute-start.4
  29.0 6.1 %collective-permute-done.8 = f32[1,2,128,256]{3,2,1,0:T(8,128)S(1)} collective-permute-done((f32[1,2,128,256]{3,2,1,0:T(8,128)S(1)}, f32[1,2,128,256]{3,2,1,0:T(8,128)S(1)}, u32[]{:S(2)}, u32[]{:S(2)}) %collective-permute-start.8) | collective-permute-done | bytes 262176 | tf_op jit(solution)/shard_map/ppermute | solution.py:50
  36.5 1.6 collective-permute-start.9
  38.0 1.5 collective-permute-start.10
  40.7 1.4 collective-permute-start.17
  42.1 14.0 %collective-permute-done.11 = f32[4,64,256]{2,1,0:T(8,128)S(1)} collective-permute-done((f32[4,64,256]{2,1,0:T(8,128)S(1)}, f32[4,64,256]{2,1,0:T(8,128)S(1)}, u32[]{:S(2)}, u32[]{:S(2)}) %collective-permute-start.11) | collective-permute-done | bytes 262176 | tf_op jit(solution)/shard_map/ppermute | solution.py:50
  59.0 1.7 collective-permute-start.19
  64.6 5.8 %half_products.2 = f32[8,4,128,128]{3,2,1,0:T(8,128)S(1)} custom-call(s32[2]{0:T(128)S(1)} %pad_add_fusion.position, f32[2,8]{1,0:T(2,128)S(1)} %convert_reduce_fusion.listed, bf16[512,1024]{1,0:T(8,128)(2,1)S(1)} %copy-done.21, bf16[512,1024]{1,0:T(8,128)(2,1)S(1)} %copy-done.23, f32[8,64,256]{2,1,0:T(8,128)S(1)} %pad_maximum_fusion.1.rest_0_, ...), custom_call_target="tpu_custom_call" | custom-call | flops 3221225472 | bytes 10485760 | tf_op jit(solution)/shard_map/half_products/pallas_call | solution.py:166
  73.0 5.0 %all-to-all-start.1 = ((f32[8,4,128,128]{3,2,1,0:T(8,128)}), f32[8,4,128,128]{3,2,1,0:T(8,128)S(1)}, u32[]{:S(2)}, u32[]{:S(2)}) async-start(f32[8,4,128,128]{3,2,1,0:T(8,128)} %copy-done.9), calls=%async_computation.1 | async-start | bytes 4194304 | tf_op jit(solution)/shard_map/all_to_all | solution.py:278
  78.0 2.0 %collective-permute-start.25 = (f32[4,2,128,256]{3,2,1,0:T(8,128)S(1)}, f32[4,2,128,256]{3,2,1,0:T(8,128)S(1)}, u32[]{:S(2)}, u32[]{:S(2)}) collective-permute-start(f32[4,2,128,256]{3,2,1,0:T(8,128)S(1)} %pad_maximum_fusion.rest_0_), channel_id=1, source_target_pairs={{0,1},{1,0},{2,3},{3,2},{4,5},{5,4},{6,7},{7,6},{8,9},{9,8},{10,11... | collective-permute-start | bytes 3145736 | tf_op jit(solution)/shard_map/ppermute | solution.py:50
  81.4 1.6 collective-permute-done.21.rest_3_
  90.1 5.2 %half_products.3 = f32[8,4,128,128]{3,2,1,0:T(8,128)S(1)} custom-call(s32[2]{0:T(128)S(1)} %pad_add_fusion.position, f32[2,8]{1,0:T(2,128)S(1)} %convert_reduce_fusion.listed, bf16[512,1024]{1,0:T(8,128)(2,1)S(1)} %copy-done.17, bf16[512,1024]{1,0:T(8,128)(2,1)S(1)} %copy-done.19, f32[8,64,256]{2,1,0:T(8,128)S(1)} %copy-done.13, ...), custom_call_target="tpu_custom_call" | custom-call | flops 3221225472 | bytes 10485760 | tf_op jit(solution)/shard_map/half_products/pallas_call | solution.py:166
  96.6 28.2 %collective-permute-done.25.rest_2_ = f32[4,2,128,256]{3,2,1,0:T(8,128)S(1)} collective-permute-done((f32[4,2,128,256]{3,2,1,0:T(8,128)S(1)}, f32[4,2,128,256]{3,2,1,0:T(8,128)S(1)}, u32[]{:S(2)}, u32[]{:S(2)}) %collective-permute-start.25) | collective-permute-done | bytes 1048608 | tf_op jit(solution)/shard_map/ppermute | solution.py:50
  127.1 4.5 %all-to-all-start = ((f32[8,4,128,128]{3,2,1,0:T(8,128)}), f32[8,4,128,128]{3,2,1,0:T(8,128)S(1)}, u32[]{:S(2)}, u32[]{:S(2)}) async-start(f32[8,4,128,128]{3,2,1,0:T(8,128)} %copy-done.8), calls=%async_computation | async-start | bytes 4194304 | tf_op jit(solution)/shard_map/all_to_all | solution.py:278
  132.4 24.1 %collective-permute-done.26.rest_3_ = f32[4,2,128,256]{3,2,1,0:T(8,128)S(1)} collective-permute-done((f32[4,2,128,256]{3,2,1,0:T(8,128)}, f32[4,2,128,256]{3,2,1,0:T(8,128)S(1)}, u32[]{:S(2)}, u32[]{:S(2)}) %collective-permute-start.26) | collective-permute-done | bytes 1048608 | tf_op jit(solution)/shard_map/ppermute | solution.py:50
  156.5 2.6 %collective-permute-done.30.rest_7_ = f32[4,2,128,256]{3,2,1,0:T(8,128)S(1)} collective-permute-done((f32[4,2,128,256]{3,2,1,0:T(8,128)S(1)}, f32[4,2,128,256]{3,2,1,0:T(8,128)S(1)}, u32[]{:S(2)}, u32[]{:S(2)}) %collective-permute-start.30) | collective-permute-done | bytes 1048608 | tf_op jit(solution)/shard_map/ppermute | solution.py:50
  160.3 2.5 %place.1 = (bf16[1024,1024]{1,0:T(8,128)(2,1)S(1)}, bf16[1024,1024]{1,0:T(8,128)(2,1)S(1)}, bf16[1024,1024]{1,0:T(8,128)(2,1)S(1)}, bf16[1024,1024]{1,0:T(8,128)(2,1)S(1)}) custom-call(s32[2]{0:T(128)S(1)} %pad_add_fusion.position, f32[4,2,128,256]{3,2,1,0:T(8,128)S(1)} %pad_maximum_fusion.rest_0_, f32[4,2,128,256]{3,2,1,0:T(8,128)} %collective-permute-done.24.rest_1_, ...), custom_call_target="tpu_custom_call" | custom-call | flops 8388608 | bytes 12582912 | tf_op jit(solution)/shard_map/place/pallas_call | solution.py:200
  164.2 1.4 copy-done.3
  165.6 4.9 %full_products.2.rest_0_ = f32[2,4,1,1024,128]{4,3,2,1,0:T(8,128)} custom-call(bf16[1024,1024]{1,0:T(8,128)(2,1)S(1)} %get-tuple-element.84.a_high, bf16[1024,1024]{1,0:T(8,128)(2,1)S(1)} %get-tuple-element.85.a_low, f32[8,4,128,128]{3,2,1,0:T(8,128)S(1)} %copy-done.7), custom_call_target="tpu_custom_call" | custom-call | flops 3221225472 | bytes 12582912 | tf_op jit(solution)/shard_map/full_products/pallas_call | solution.py:240
  170.5 9.3 %all-to-all-done.received = f32[8,4,128,128]{3,2,1,0:T(8,128)S(1)} async-done(((f32[8,4,128,128]{3,2,1,0:T(8,128)}), f32[8,4,128,128]{3,2,1,0:T(8,128)S(1)}, u32[]{:S(2)}, u32[]{:S(2)}) %all-to-all-start) | async-done | bytes 2097184 | tf_op jit(solution)/shard_map/all_to_all | solution.py:278
  179.8 1.6 copy-done.2
  181.4 1.6 copy-done.4
  183.0 4.9 %full_products.3 = f32[2,4,1,1024,128]{4,3,2,1,0:T(8,128)} custom-call(bf16[1024,1024]{1,0:T(8,128)(2,1)S(1)} %copy-done.2, bf16[1024,1024]{1,0:T(8,128)(2,1)S(1)} %copy-done.4, f32[8,4,128,128]{3,2,1,0:T(8,128)S(1)} %all-to-all-done.received, f32[2,4,1,1024,128]{4,3,2,1,0:T(8,128)} %full_products.2.rest_0_), custom_call_target="tpu_custom_call", output_to_operand_aliasing={{}: (3, {})} | custom-call | flops 3221225472 | bytes 12582912 | tf_op jit(solution)/shard_map/full_products/pallas_call | solution.py:240
  (118 shorter events, 30.9 us)
Async XLA Ops:
  1.0 10.4 %collective-permute-start = (f32[1,128,256]{2,1,0:T(8,128)S(1)}, f32[1,128,256]{2,1,0:T(8,128)S(1)}, u32[]{:S(2)}, u32[]{:S(2)}) collective-permute-start(f32[1,128,256]{2,1,0:T(8,128)S(1)} %get-tuple-element.90), channel_id=1, source_target_pairs={{0,4},{1,5},{2,6},{3,7},{4,0},{5,1},{6,2},{7,3},{8,12},{9,13},{10,... | collective-permute-start | bytes 393224 | tf_op jit(solution)/shard_map/ppermute | solution.py:50
  11.4 8.8 %collective-permute-start.3 = (f32[1,128,256]{2,1,0:T(8,128)S(1)}, f32[1,128,256]{2,1,0:T(8,128)S(1)}, u32[]{:S(2)}, u32[]{:S(2)}) collective-permute-start(f32[1,128,256]{2,1,0:T(8,128)S(1)} %get-tuple-element.56), channel_id=1, source_target_pairs={{0,4},{1,5},{2,6},{3,7},{4,0},{5,1},{6,2},{7,3},{8,12},{9,13},{10,... | collective-permute-start | bytes 393224 | tf_op jit(solution)/shard_map/ppermute | solution.py:50
  11.5 9.1 %collective-permute-start.1 = (f32[2,64,256]{2,1,0:T(8,128)S(1)}, f32[2,64,256]{2,1,0:T(8,128)S(1)}, u32[]{:S(2)}, u32[]{:S(2)}) collective-permute-start(f32[2,64,256]{2,1,0:T(8,128)S(1)} %get-tuple-element.54), channel_id=1, source_target_pairs={{0,2},{1,3},{2,0},{3,1},{4,6},{5,7},{6,4},{7,5},{8,10},{9,11},{10,... | collective-permute-start | bytes 393224 | tf_op jit(solution)/shard_map/ppermute | solution.py:50
  15.6 5.0 %collective-permute-start.2 = (f32[2,64,256]{2,1,0:T(8,128)S(1)}, f32[2,64,256]{2,1,0:T(8,128)S(1)}, u32[]{:S(2)}, u32[]{:S(2)}) collective-permute-start(f32[2,64,256]{2,1,0:T(8,128)S(1)} %get-tuple-element.55), channel_id=1, source_target_pairs={{0,16},{1,17},{2,18},{3,19},{4,20},{5,21},{6,22},{7,23},{8,24},{9,... | collective-permute-start | bytes 393224 | tf_op jit(solution)/shard_map/ppermute | solution.py:50
  20.6 7.2 %collective-permute-start.6 = (f32[2,64,256]{2,1,0:T(8,128)S(1)}, f32[2,64,256]{2,1,0:T(8,128)S(1)}, u32[]{:S(2)}, u32[]{:S(2)}) collective-permute-start(f32[2,64,256]{2,1,0:T(8,128)S(1)} %get-tuple-element.59), channel_id=1, source_target_pairs={{0,2},{1,3},{2,0},{3,1},{4,6},{5,7},{6,4},{7,5},{8,10},{9,11},{10,... | collective-permute-start | bytes 393224 | tf_op jit(solution)/shard_map/ppermute | solution.py:50
  20.9 14.2 %collective-permute-start.8 = (f32[1,2,128,256]{3,2,1,0:T(8,128)S(1)}, f32[1,2,128,256]{3,2,1,0:T(8,128)S(1)}, u32[]{:S(2)}, u32[]{:S(2)}) collective-permute-start(f32[1,2,128,256]{3,2,1,0:T(8,128)S(1)} %bitcast.6), channel_id=1, source_target_pairs={{0,4},{1,5},{2,6},{3,7},{4,0},{5,1},{6,2},{7,3},{8,12},{9,13},{10,... | collective-permute-start | bytes 786440 | tf_op jit(solution)/shard_map/ppermute | solution.py:50
  24.0 5.0 %collective-permute-start.7 = (f32[2,64,256]{2,1,0:T(8,128)S(1)}, f32[2,64,256]{2,1,0:T(8,128)S(1)}, u32[]{:S(2)}, u32[]{:S(2)}) collective-permute-start(f32[2,64,256]{2,1,0:T(8,128)S(1)} %get-tuple-element.60), channel_id=1, source_target_pairs={{0,16},{1,17},{2,18},{3,19},{4,20},{5,21},{6,22},{7,23},{8,24},{9,... | collective-permute-start | bytes 393224 | tf_op jit(solution)/shard_map/ppermute | solution.py:50
  25.5 9.7 %collective-permute-start.4 = (f32[4,64,256]{2,1,0:T(8,128)S(1)}, f32[4,64,256]{2,1,0:T(8,128)S(1)}, u32[]{:S(2)}, u32[]{:S(2)}) collective-permute-start(f32[4,64,256]{2,1,0:T(8,128)S(1)} %pad_maximum_fusion.6), channel_id=1, source_target_pairs={{0,1},{1,0},{2,3},{3,2},{4,5},{5,4},{6,7},{7,6},{8,9},{9,8},{10,11... | collective-permute-start | bytes 786440 | tf_op jit(solution)/shard_map/ppermute | solution.py:50
  27.0 9.4 %collective-permute-start.5 = (f32[4,64,256]{2,1,0:T(8,128)S(1)}, f32[4,64,256]{2,1,0:T(8,128)S(1)}, u32[]{:S(2)}, u32[]{:S(2)}) collective-permute-start(f32[4,64,256]{2,1,0:T(8,128)S(1)} %pad_maximum_fusion.7), channel_id=1, source_target_pairs={{0,2},{1,3},{2,0},{3,1},{4,6},{5,7},{6,4},{7,5},{8,10},{9,11},{10,... | collective-permute-start | bytes 786440 | tf_op jit(solution)/shard_map/ppermute | solution.py:50
  36.5 19.7 %collective-permute-start.9 = (f32[8,64,256]{2,1,0:T(8,128)S(1)}, f32[8,64,256]{2,1,0:T(8,128)}, u32[]{:S(2)}, u32[]{:S(2)}) collective-permute-start(f32[8,64,256]{2,1,0:T(8,128)S(1)} %pad_maximum_fusion.1.rest_0_), channel_id=1, source_target_pairs={{0,16},{1,17},{2,18},{3,19},{4,20},{5,21},{6,22},{7,23},{8,24},{9,... | collective-permute-start | bytes 1572872 | tf_op jit(solution)/shard_map/ppermute | solution.py:50
  38.0 18.2 %collective-permute-start.10 = (f32[8,64,256]{2,1,0:T(8,128)S(1)}, f32[8,64,256]{2,1,0:T(8,128)}, u32[]{:S(2)}, u32[]{:S(2)}) collective-permute-start(f32[8,64,256]{2,1,0:T(8,128)S(1)} %pad_maximum_fusion.2.rest_4_), channel_id=1, source_target_pairs={{0,1},{1,0},{2,3},{3,2},{4,5},{5,4},{6,7},{7,6},{8,9},{9,8},{10,11... | collective-permute-start | bytes 1572872 | tf_op jit(solution)/shard_map/ppermute | solution.py:50
  39.5 16.5 %collective-permute-start.11 = (f32[4,64,256]{2,1,0:T(8,128)S(1)}, f32[4,64,256]{2,1,0:T(8,128)S(1)}, u32[]{:S(2)}, u32[]{:S(2)}) collective-permute-start(f32[4,64,256]{2,1,0:T(8,128)S(1)} %pad_maximum_fusion.8), channel_id=1, source_target_pairs={{0,1},{1,0},{2,3},{3,2},{4,5},{5,4},{6,7},{7,6},{8,9},{9,8},{10,11... | collective-permute-start | bytes 786440 | tf_op jit(solution)/shard_map/ppermute | solution.py:50
  40.0 16.1 %collective-permute-start.12 = (f32[4,64,256]{2,1,0:T(8,128)S(1)}, f32[4,64,256]{2,1,0:T(8,128)S(1)}, u32[]{:S(2)}, u32[]{:S(2)}) collective-permute-start(f32[4,64,256]{2,1,0:T(8,128)S(1)} %pad_maximum_fusion.9), channel_id=1, source_target_pairs={{0,2},{1,3},{2,0},{3,1},{4,6},{5,7},{6,4},{7,5},{8,10},{9,11},{10,... | collective-permute-start | bytes 786440 | tf_op jit(solution)/shard_map/ppermute | solution.py:50
  40.7 17.0 %collective-permute-start.17 = (f32[2,2,128,256]{3,2,1,0:T(8,128)S(1)}, f32[2,2,128,256]{3,2,1,0:T(8,128)}, u32[]{:S(2)}, u32[]{:S(2)}) collective-permute-start(f32[2,2,128,256]{3,2,1,0:T(8,128)S(1)} %pad_maximum_fusion.3), channel_id=1, source_target_pairs={{0,2},{1,3},{2,0},{3,1},{4,6},{5,7},{6,4},{7,5},{8,10},{9,11},{10,... | collective-permute-start | bytes 1572872 | tf_op jit(solution)/shard_map/ppermute | solution.py:50
  56.3 5.9 %collective-permute-start.14 = (f32[8,64,256]{2,1,0:T(8,128)}, f32[8,64,256]{2,1,0:T(8,128)}, u32[]{:S(2)}, u32[]{:S(2)}) collective-permute-start(f32[8,64,256]{2,1,0:T(8,128)} %collective-permute-done.9.rest_1_), channel_id=1, source_target_pairs={{0,8},{1,9},{2,10},{3,11},{4,12},{5,13},{6,14},{7,15},{8,0},{9,1},... | collective-permute-start | bytes 1572872 | tf_op jit(solution)/shard_map/ppermute | solution.py:50
  56.8 5.4 %collective-permute-start.15 = (f32[8,64,256]{2,1,0:T(8,128)S(1)}, f32[8,64,256]{2,1,0:T(8,128)}, u32[]{:S(2)}, u32[]{:S(2)}) collective-permute-start(f32[8,64,256]{2,1,0:T(8,128)S(1)} %pad_maximum_fusion.2.rest_4_), channel_id=1, source_target_pairs={{0,8},{1,9},{2,10},{3,11},{4,12},{5,13},{6,14},{7,15},{8,0},{9,1},... | collective-permute-start | bytes 1572872 | tf_op jit(solution)/shard_map/ppermute | solution.py:50
  56.9 5.3 %collective-permute-start.16 = (f32[8,64,256]{2,1,0:T(8,128)}, f32[8,64,256]{2,1,0:T(8,128)}, u32[]{:S(2)}, u32[]{:S(2)}) collective-permute-start(f32[8,64,256]{2,1,0:T(8,128)} %collective-permute-done.10.rest_5_), channel_id=1, source_target_pairs={{0,8},{1,9},{2,10},{3,11},{4,12},{5,13},{6,14},{7,15},{8,0},{9,1},... | collective-permute-start | bytes 1572872 | tf_op jit(solution)/shard_map/ppermute | solution.py:50
  57.7 14.1 %collective-permute-start.18 = (f32[8,64,256]{2,1,0:T(8,128)S(1)}, f32[8,64,256]{2,1,0:T(8,128)S(1)}, u32[]{:S(2)}, u32[]{:S(2)}) collective-permute-start(f32[8,64,256]{2,1,0:T(8,128)S(1)} %pad_maximum_fusion.4.rest_0_), channel_id=1, source_target_pairs={{0,16},{1,17},{2,18},{3,19},{4,20},{5,21},{6,22},{7,23},{8,24},{9,... | collective-permute-start | bytes 1572872 | tf_op jit(solution)/shard_map/ppermute | solution.py:50
  59.0 14.1 %collective-permute-start.19 = (f32[8,64,256]{2,1,0:T(8,128)S(1)}, f32[8,64,256]{2,1,0:T(8,128)}, u32[]{:S(2)}, u32[]{:S(2)}) collective-permute-start(f32[8,64,256]{2,1,0:T(8,128)S(1)} %pad_maximum_fusion.5.rest_4_), channel_id=1, source_target_pairs={{0,1},{1,0},{2,3},{3,2},{4,5},{5,4},{6,7},{7,6},{8,9},{9,8},{10,11... | collective-permute-start | bytes 1572872 | tf_op jit(solution)/shard_map/ppermute | solution.py:50
  73.0 52.7 %all-to-all-start.1 = ((f32[8,4,128,128]{3,2,1,0:T(8,128)}), f32[8,4,128,128]{3,2,1,0:T(8,128)S(1)}, u32[]{:S(2)}, u32[]{:S(2)}) async-start(f32[8,4,128,128]{3,2,1,0:T(8,128)} %copy-done.9), calls=%async_computation.1 | async-start | bytes 4194304 | tf_op jit(solution)/shard_map/all_to_all | solution.py:278
  78.0 3.3 %collective-permute-start.20 = (f32[8,64,256]{2,1,0:T(8,128)}, f32[8,64,256]{2,1,0:T(8,128)S(1)}, u32[]{:S(2)}, u32[]{:S(2)}) collective-permute-start(f32[8,64,256]{2,1,0:T(8,128)} %copy-done.12), channel_id=1, source_target_pairs={{0,8},{1,9},{2,10},{3,11},{4,12},{5,13},{6,14},{7,15},{8,0},{9,1},... | collective-permute-start | bytes 1572872 | tf_op jit(solution)/shard_map/ppermute | solution.py:50
  78.0 46.8 %collective-permute-start.25 = (f32[4,2,128,256]{3,2,1,0:T(8,128)S(1)}, f32[4,2,128,256]{3,2,1,0:T(8,128)S(1)}, u32[]{:S(2)}, u32[]{:S(2)}) collective-permute-start(f32[4,2,128,256]{3,2,1,0:T(8,128)S(1)} %pad_maximum_fusion.rest_0_), channel_id=1, source_target_pairs={{0,1},{1,0},{2,3},{3,2},{4,5},{5,4},{6,7},{7,6},{8,9},{9,8},{10,11... | collective-permute-start | bytes 3145736 | tf_op jit(solution)/shard_map/ppermute | solution.py:50
  80.1 45.7 %collective-permute-start.24 = (f32[4,2,128,256]{3,2,1,0:T(8,128)S(1)}, f32[4,2,128,256]{3,2,1,0:T(8,128)}, u32[]{:S(2)}, u32[]{:S(2)}) collective-permute-start(f32[4,2,128,256]{3,2,1,0:T(8,128)S(1)} %pad_maximum_fusion.rest_0_), channel_id=1, source_target_pairs={{0,16},{1,17},{2,18},{3,19},{4,20},{5,21},{6,22},{7,23},{8,24},{9,... | collective-permute-start | bytes 3145736 | tf_op jit(solution)/shard_map/ppermute | solution.py:50
  80.9 2.1 %collective-permute-start.21 = (f32[8,64,256]{2,1,0:T(8,128)}, f32[8,64,256]{2,1,0:T(8,128)S(1)}, u32[]{:S(2)}, u32[]{:S(2)}) collective-permute-start(f32[8,64,256]{2,1,0:T(8,128)} %copy-done.24), channel_id=1, source_target_pairs={{0,8},{1,9},{2,10},{3,11},{4,12},{5,13},{6,14},{7,15},{8,0},{9,1},... | collective-permute-start | bytes 1572872 | tf_op jit(solution)/shard_map/ppermute | solution.py:50
  80.9 2.9 %collective-permute-start.22 = (f32[8,64,256]{2,1,0:T(8,128)}, f32[8,64,256]{2,1,0:T(8,128)S(1)}, u32[]{:S(2)}, u32[]{:S(2)}) collective-permute-start(f32[8,64,256]{2,1,0:T(8,128)} %copy-done.14), channel_id=1, source_target_pairs={{0,8},{1,9},{2,10},{3,11},{4,12},{5,13},{6,14},{7,15},{8,0},{9,1},... | collective-permute-start | bytes 1572872 | tf_op jit(solution)/shard_map/ppermute | solution.py:50
  81.4 3.1 %collective-permute-start.23 = (f32[8,64,256]{2,1,0:T(8,128)}, f32[8,64,256]{2,1,0:T(8,128)S(1)}, u32[]{:S(2)}, u32[]{:S(2)}) collective-permute-start(f32[8,64,256]{2,1,0:T(8,128)} %collective-permute-done.19.rest_5_), channel_id=1, source_target_pairs={{0,8},{1,9},{2,10},{3,11},{4,12},{5,13},{6,14},{7,15},{8,0},{9,1},... | collective-permute-start | bytes 1572872 | tf_op jit(solution)/shard_map/ppermute | solution.py:50
  127.1 52.7 %all-to-all-start = ((f32[8,4,128,128]{3,2,1,0:T(8,128)}), f32[8,4,128,128]{3,2,1,0:T(8,128)S(1)}, u32[]{:S(2)}, u32[]{:S(2)}) async-start(f32[8,4,128,128]{3,2,1,0:T(8,128)} %copy-done.8), calls=%async_computation | async-start | bytes 4194304 | tf_op jit(solution)/shard_map/all_to_all | solution.py:278
  131.7 24.8 %collective-permute-start.26 = (f32[4,2,128,256]{3,2,1,0:T(8,128)}, f32[4,2,128,256]{3,2,1,0:T(8,128)S(1)}, u32[]{:S(2)}, u32[]{:S(2)}) collective-permute-start(f32[4,2,128,256]{3,2,1,0:T(8,128)} %copy-done.10), channel_id=1, source_target_pairs={{0,16},{1,17},{2,18},{3,19},{4,20},{5,21},{6,22},{7,23},{8,24},{9,... | collective-permute-start | bytes 3145736 | tf_op jit(solution)/shard_map/ppermute | solution.py:50
  131.8 24.7 %collective-permute-start.29 = (f32[4,2,128,256]{3,2,1,0:T(8,128)}, f32[4,2,128,256]{3,2,1,0:T(8,128)S(1)}, u32[]{:S(2)}, u32[]{:S(2)}) collective-permute-start(f32[4,2,128,256]{3,2,1,0:T(8,128)} %copy-done.10), channel_id=1, source_target_pairs={{0,8},{1,9},{2,10},{3,11},{4,12},{5,13},{6,14},{7,15},{8,0},{9,1},... | collective-permute-start | bytes 3145736 | tf_op jit(solution)/shard_map/ppermute | solution.py:50
  131.8 24.6 %collective-permute-start.27 = (f32[4,2,128,256]{3,2,1,0:T(8,128)S(1)}, f32[4,2,128,256]{3,2,1,0:T(8,128)S(1)}, u32[]{:S(2)}, u32[]{:S(2)}) collective-permute-start(f32[4,2,128,256]{3,2,1,0:T(8,128)S(1)} %pad_maximum_fusion.rest_0_), channel_id=1, source_target_pairs={{0,8},{1,9},{2,10},{3,11},{4,12},{5,13},{6,14},{7,15},{8,0},{9,1},... | collective-permute-start | bytes 3145736 | tf_op jit(solution)/shard_map/ppermute | solution.py:50
  132.3 24.1 %collective-permute-start.28 = (f32[4,2,128,256]{3,2,1,0:T(8,128)}, f32[4,2,128,256]{3,2,1,0:T(8,128)S(1)}, u32[]{:S(2)}, u32[]{:S(2)}) collective-permute-start(f32[4,2,128,256]{3,2,1,0:T(8,128)} %collective-permute-done.24.rest_1_), channel_id=1, source_target_pairs={{0,8},{1,9},{2,10},{3,11},{4,12},{5,13},{6,14},{7,15},{8,0},{9,1},... | collective-permute-start | bytes 3145736 | tf_op jit(solution)/shard_map/ppermute | solution.py:50
  156.4 2.7 %collective-permute-start.30 = (f32[4,2,128,256]{3,2,1,0:T(8,128)S(1)}, f32[4,2,128,256]{3,2,1,0:T(8,128)S(1)}, u32[]{:S(2)}, u32[]{:S(2)}) collective-permute-start(f32[4,2,128,256]{3,2,1,0:T(8,128)S(1)} %collective-permute-done.26.rest_3_), channel_id=1, source_target_pairs={{0,8},{1,9},{2,10},{3,11},{4,12},{5,13},{6,14},{7,15},{8,0},{9,1},... | collective-permute-start | bytes 3145736 | tf_op jit(solution)/shard_map/ppermute | solution.py:50
  (31 other events, 235.3 us)

commit v5 on v4

--- a/solution.py
+++ b/solution.py
@@ -211,18 +211,19 @@
 def full_kernel(split, a_high, a_low, received, *rest):
     out, b_high, b_low = rest[-3:]
     units, share, block, _ = received.shape
-    for source in range(units):
-        rows = slice(source // split * block, (source // split + 1) * block)
-        for at in range(share):
-            col = (source % split * share + at) * block
-            b_high[rows, col : col + block], b_low[rows, col : col + block] = halves(received[source, at])
-    orbitals = a_high.shape[0]
-    tile = 2 * block
-    for start in range(0, orbitals, tile):
-        rows = slice(start, start + tile)
-        product = three_products(a_high[rows], a_low[rows], b_high[...], b_low[...])
-        for at in range(share * split):
-            out[0, at, 0, rows] = product[:, at * block : (at + 1) * block]
+
+    @pl.when(pl.program_id(0) == 0)
+    def _():
+        for source in range(units):
+            rows = slice(source // split * block, (source // split + 1) * block)
+            for at in range(share):
+                col = (source % split * share + at) * block
+                high, low = halves(received[source, at])
+                b_high[rows, col : col + block], b_low[rows, col : col + block] = high, low
+
+    product = three_products(a_high[...], a_low[...], b_high[...], b_low[...])
+    for at in range(share * split):
+        out[0, at, 0] = product[:, at * block : (at + 1) * block]
 
 
 def full_products(vir, received, time, times, split, earlier):
@@ -230,8 +231,10 @@
     orbitals = high.shape[0]
     units, share, block, _ = received.shape
     aux_count = share * split
+    tile = 2 * block
     operands = [high, low, received]
-    in_specs = [VMEM] * 3
+    some_rows = pl.BlockSpec((tile, orbitals), lambda i: (i, 0))
+    in_specs = [some_rows, some_rows, VMEM]
     aliases = {}
     if earlier is not None:
         aliases = {len(operands): 0}
@@ -239,13 +242,13 @@
         in_specs.append(pl.BlockSpec(memory_space=pl.ANY))
     return pl.pallas_call(
         functools.partial(full_kernel, split),
-        grid=(1,),
+        grid=(orbitals // tile,),
         out_shape=jax.ShapeDtypeStruct((times, aux_count, 1, orbitals, block), jnp.float32),
         in_specs=in_specs,
-        out_specs=pl.BlockSpec((1, aux_count, 1, orbitals, block), lambda i: (time, 0, 0, 0, 0)),
+        out_specs=pl.BlockSpec((1, aux_count, 1, tile, block), lambda i: (time, 0, 0, i, 0)),
         scratch_shapes=[pltpu.VMEM((orbitals, aux_count * block), jnp.bfloat16)] * 2,
         input_output_aliases=aliases,
-        compiler_params=PARAMS,
+        compiler_params=pltpu.CompilerParams(vmem_limit_bytes=52 * 1024 * 1024),
         cost_estimate=cost(6 * aux_count * block * orbitals * orbitals, 12 * orbitals * orbitals),
         name="full_products",
     )(*operands)

time: 189 us -> 187 us (0.989)
  local copies, waits for them, and re-layouts: 24.3 us -> 16.7 us
  Pallas kernels: 25.1 us -> 32.3 us
    unnamed x61 -> x45, local copies, waits for them, and re-layouts: 23.3 us -> 15.7 us
    pallas_call x2, Pallas kernels: 9.8 us -> 15 us  [full_products(): pl.pallas_call(functools.partial(full_kernel, split), grid=(orbitals // t...]
    pallas_call x2, Pallas kernels: 11 us -> 13.7 us  [half_products(): pl.pallas_call(functools.partial(half_kernel, keys, time, split), out_sha...]
  transfers between devices with their start and end apart: 33 -> 33, of which waited for: 18 -> 18; matrix products, arithmetic and copies ran while one was open for 1% -> 1% of each run, Pallas kernels for 11% -> 13%
where the time goes in v5:
time: 187 us
  waiting for transfers between devices  95.7 us (51%)
  starting transfers between devices  39 us (21%)
  Pallas kernels  32.3 us (17%)
  local copies, waits for them, and re-layouts  16.7 us (9%)
  other arithmetic  2.54 us (1%)
    ppermute x31, waiting for transfers between devices, permute(): return lax.ppermute(value, ('aux', 'orb'), pairs)  88.1 us
    ppermute x31, starting transfers between devices, permute(): return lax.ppermute(value, ('aux', 'orb'), pairs)  29.5 us
    unnamed x45, local copies, waits for them, and re-layouts  15.7 us
    pallas_call x2, Pallas kernels, full_products(): pl.pallas_call(functools.partial(full_kernel, split), grid=(orbitals // t...  15 us
    pallas_call x2, Pallas kernels, half_products(): pl.pallas_call(functools.partial(half_kernel, keys, time, split), out_sha...  13.7 us
    all_to_all x2, starting transfers between devices, deliver(): return lax.all_to_all(made, 'orb', split_axis=0, concat_axis=0, tiled=True)  9.51 us
    all_to_all x2, waiting for transfers between devices, deliver(): return lax.all_to_all(made, 'orb', split_axis=0, concat_axis=0, tiled=True)  7.56 us
  transfers between devices with their start and end apart: 33, of which 18 were waited for; matrix products, arithmetic and copies ran while one was open for 1% of the time, Pallas kernels for 13%

profile of v5, /device:TPU:0, one launch (start us, length us, event | category | flops | bytes accessed | tf_op | source)
XLA Modules:
  0.0 186.6 jit_solution(17488479044440641968)
XLA Ops:
  1.0 4.1 %collective-permute-start = (f32[1,128,256]{2,1,0:T(8,128)S(1)}, f32[1,128,256]{2,1,0:T(8,128)S(1)}, u32[]{:S(2)}, u32[]{:S(2)}) collective-permute-start(f32[1,128,256]{2,1,0:T(8,128)S(1)} %get-tuple-element.90), channel_id=1, source_target_pairs={{0,4},{1,5},{2,6},{3,7},{4,0},{5,1},{6,2},{7,3},{8,12},{9,13},{10,... | collective-permute-start | bytes 393224 | tf_op jit(solution)/shard_map/ppermute | solution.py:50
  5.2 1.6 copy-done.3
  6.8 1.9 %split_integrals.1 = (bf16[512,1024]{1,0:T(8,128)(2,1)S(1)}, bf16[512,1024]{1,0:T(8,128)(2,1)S(1)}, bf16[512,1024]{1,0:T(8,128)(2,1)S(1)}, bf16[512,1024]{1,0:T(8,128)(2,1)S(1)}) custom-call(f32[2,8]{1,0:T(2,128)S(1)} %convert_reduce_fusion.listed, f32[4,128,1024]{2,1,0:T(8,128)S(1)} %bitcast.5), custom_call_target="tpu_custom_call" | custom-call | flops 4194304 | bytes 6291456 | tf_op jit(solution)/shard_map/split_integrals/pallas_call | solution.py:121
  8.7 2.7 %collective-permute-done = f32[1,128,256]{2,1,0:T(8,128)S(1)} collective-permute-done((f32[1,128,256]{2,1,0:T(8,128)S(1)}, f32[1,128,256]{2,1,0:T(8,128)S(1)}, u32[]{:S(2)}, u32[]{:S(2)}) %collective-permute-start) | collective-permute-done | bytes 131104 | tf_op jit(solution)/shard_map/ppermute | solution.py:50
  11.5 4.1 %collective-permute-start.1 = (f32[2,64,256]{2,1,0:T(8,128)S(1)}, f32[2,64,256]{2,1,0:T(8,128)S(1)}, u32[]{:S(2)}, u32[]{:S(2)}) collective-permute-start(f32[2,64,256]{2,1,0:T(8,128)S(1)} %get-tuple-element.54), channel_id=1, source_target_pairs={{0,2},{1,3},{2,0},{3,1},{4,6},{5,7},{6,4},{7,5},{8,10},{9,11},{10,... | collective-permute-start | bytes 393224 | tf_op jit(solution)/shard_map/ppermute | solution.py:50
  15.6 1.5 collective-permute-start.2
  17.1 3.1 %collective-permute-done.3 = f32[1,128,256]{2,1,0:T(8,128)S(1)} collective-permute-done((f32[1,128,256]{2,1,0:T(8,128)S(1)}, f32[1,128,256]{2,1,0:T(8,128)S(1)}, u32[]{:S(2)}, u32[]{:S(2)}) %collective-permute-start.3) | collective-permute-done | bytes 131104 | tf_op jit(solution)/shard_map/ppermute | solution.py:50
  20.9 3.1 %collective-permute-start.8 = (f32[1,2,128,256]{3,2,1,0:T(8,128)S(1)}, f32[1,2,128,256]{3,2,1,0:T(8,128)S(1)}, u32[]{:S(2)}, u32[]{:S(2)}) collective-permute-start(f32[1,2,128,256]{3,2,1,0:T(8,128)S(1)} %bitcast.6), channel_id=1, source_target_pairs={{0,4},{1,5},{2,6},{3,7},{4,0},{5,1},{6,2},{7,3},{8,12},{9,13},{10,... | collective-permute-start | bytes 786440 | tf_op jit(solution)/shard_map/ppermute | solution.py:50
  24.0 1.5 collective-permute-start.7
  25.5 1.5 collective-permute-start.4
  29.0 6.1 %collective-permute-done.8 = f32[1,2,128,256]{3,2,1,0:T(8,128)S(1)} collective-permute-done((f32[1,2,128,256]{3,2,1,0:T(8,128)S(1)}, f32[1,2,128,256]{3,2,1,0:T(8,128)S(1)}, u32[]{:S(2)}, u32[]{:S(2)}) %collective-permute-start.8) | collective-permute-done | bytes 262176 | tf_op jit(solution)/shard_map/ppermute | solution.py:50
  36.5 1.6 collective-permute-start.9
  38.0 1.5 collective-permute-start.10
  40.7 1.4 collective-permute-start.17
  42.1 14.0 %collective-permute-done.11 = f32[4,64,256]{2,1,0:T(8,128)S(1)} collective-permute-done((f32[4,64,256]{2,1,0:T(8,128)S(1)}, f32[4,64,256]{2,1,0:T(8,128)S(1)}, u32[]{:S(2)}, u32[]{:S(2)}) %collective-permute-start.11) | collective-permute-done | bytes 262176 | tf_op jit(solution)/shard_map/ppermute | solution.py:50
  59.8 1.7 collective-permute-start.19
  65.5 7.0 %half_products.2 = f32[8,4,128,128]{3,2,1,0:T(8,128)} custom-call(s32[2]{0:T(128)S(1)} %pad_add_fusion.position, f32[2,8]{1,0:T(2,128)S(1)} %convert_reduce_fusion.listed, bf16[512,1024]{1,0:T(8,128)(2,1)S(1)} %copy-done.13, bf16[512,1024]{1,0:T(8,128)(2,1)S(1)} %copy-done.15, f32[8,64,256]{2,1,0:T(8,128)S(1)} %pad_maximum_fusion.1.rest_0_, ...), custom_call_target="tpu_custom_call" | custom-call | flops 3221225472 | bytes 10485760 | tf_op jit(solution)/shard_map/half_products/pallas_call | solution.py:166
  73.9 5.0 %all-to-all-start.1 = ((f32[8,4,128,128]{3,2,1,0:T(8,128)}), f32[8,4,128,128]{3,2,1,0:T(8,128)}, u32[]{:S(2)}, u32[]{:S(2)}) async-start(f32[8,4,128,128]{3,2,1,0:T(8,128)} %half_products.2), calls=%async_computation.1 | async-start | bytes 4194304 | tf_op jit(solution)/shard_map/all_to_all | solution.py:281
  78.9 2.0 %collective-permute-start.25 = (f32[4,2,128,256]{3,2,1,0:T(8,128)S(1)}, f32[4,2,128,256]{3,2,1,0:T(8,128)S(1)}, u32[]{:S(2)}, u32[]{:S(2)}) collective-permute-start(f32[4,2,128,256]{3,2,1,0:T(8,128)S(1)} %pad_maximum_fusion.rest_0_), channel_id=1, source_target_pairs={{0,1},{1,0},{2,3},{3,2},{4,5},{5,4},{6,7},{7,6},{8,9},{9,8},{10,11... | collective-permute-start | bytes 3145736 | tf_op jit(solution)/shard_map/ppermute | solution.py:50
  82.2 1.6 collective-permute-done.21.rest_3_
  89.9 6.7 %half_products.3 = f32[8,4,128,128]{3,2,1,0:T(8,128)} custom-call(s32[2]{0:T(128)S(1)} %pad_add_fusion.position, f32[2,8]{1,0:T(2,128)S(1)} %convert_reduce_fusion.listed, bf16[512,1024]{1,0:T(8,128)(2,1)S(1)} %copy-done.9, bf16[512,1024]{1,0:T(8,128)(2,1)S(1)} %copy-done.11, f32[8,64,256]{2,1,0:T(8,128)} %pad_maximum_fusion.4.rest_0_, ...), custom_call_target="tpu_custom_call" | custom-call | flops 3221225472 | bytes 10485760 | tf_op jit(solution)/shard_map/half_products/pallas_call | solution.py:166
  96.6 29.1 %collective-permute-done.25.rest_2_ = f32[4,2,128,256]{3,2,1,0:T(8,128)S(1)} collective-permute-done((f32[4,2,128,256]{3,2,1,0:T(8,128)S(1)}, f32[4,2,128,256]{3,2,1,0:T(8,128)S(1)}, u32[]{:S(2)}, u32[]{:S(2)}) %collective-permute-start.25) | collective-permute-done | bytes 1048608 | tf_op jit(solution)/shard_map/ppermute | solution.py:50
  126.8 4.5 %all-to-all-start = ((f32[8,4,128,128]{3,2,1,0:T(8,128)}), f32[8,4,128,128]{3,2,1,0:T(8,128)}, u32[]{:S(2)}, u32[]{:S(2)}) async-start(f32[8,4,128,128]{3,2,1,0:T(8,128)} %half_products.3), calls=%async_computation | async-start | bytes 4194304 | tf_op jit(solution)/shard_map/all_to_all | solution.py:281
  132.2 23.0 %collective-permute-done.26.rest_3_ = f32[4,2,128,256]{3,2,1,0:T(8,128)S(1)} collective-permute-done((f32[4,2,128,256]{3,2,1,0:T(8,128)S(1)}, f32[4,2,128,256]{3,2,1,0:T(8,128)S(1)}, u32[]{:S(2)}, u32[]{:S(2)}) %collective-permute-start.26) | collective-permute-done | bytes 1048608 | tf_op jit(solution)/shard_map/ppermute | solution.py:50
  155.3 2.6 %collective-permute-done.30.rest_7_ = f32[4,2,128,256]{3,2,1,0:T(8,128)S(1)} collective-permute-done((f32[4,2,128,256]{3,2,1,0:T(8,128)S(1)}, f32[4,2,128,256]{3,2,1,0:T(8,128)S(1)}, u32[]{:S(2)}, u32[]{:S(2)}) %collective-permute-start.30) | collective-permute-done | bytes 1048608 | tf_op jit(solution)/shard_map/ppermute | solution.py:50
  157.9 1.8 place.1
  159.7 1.4 copy-done.1
  161.1 1.3 copy-done.2
  162.4 1.4 copy-done.6
  165.1 7.5 %full_products.2.rest_0_ = f32[2,4,1,1024,128]{4,3,2,1,0:T(8,128)} custom-call(bf16[1024,1024]{1,0:T(8,128)(2,1)} %copy-done.6, bf16[1024,1024]{1,0:T(8,128)(2,1)} %copy-done.7, f32[8,4,128,128]{3,2,1,0:T(8,128)} %all-to-all-done.1.received), custom_call_target="tpu_custom_call" | custom-call | flops 3221225472 | bytes 12582912 | tf_op jit(solution)/shard_map/full_products/pallas_call | solution.py:243
  172.6 6.5 %all-to-all-done.received = f32[8,4,128,128]{3,2,1,0:T(8,128)} async-done(((f32[8,4,128,128]{3,2,1,0:T(8,128)}), f32[8,4,128,128]{3,2,1,0:T(8,128)}, u32[]{:S(2)}, u32[]{:S(2)}) %all-to-all-start) | async-done | bytes 2097184 | tf_op jit(solution)/shard_map/all_to_all | solution.py:281
  179.1 7.5 %full_products.3 = f32[2,4,1,1024,128]{4,3,2,1,0:T(8,128)} custom-call(bf16[1024,1024]{1,0:T(8,128)(2,1)} %copy-done.1, bf16[1024,1024]{1,0:T(8,128)(2,1)} %copy-done.2, f32[8,4,128,128]{3,2,1,0:T(8,128)} %all-to-all-done.received, f32[2,4,1,1024,128]{4,3,2,1,0:T(8,128)} %full_products.2.rest_0_), custom_call_target="tpu_custom_call", output_to_operand_aliasing={{}: (3, {})} | custom-call | flops 3221225472 | bytes 12582912 | tf_op jit(solution)/shard_map/full_products/pallas_call | solution.py:243
  (102 shorter events, 26.0 us)
Async XLA Ops:
  1.0 10.4 %collective-permute-start = (f32[1,128,256]{2,1,0:T(8,128)S(1)}, f32[1,128,256]{2,1,0:T(8,128)S(1)}, u32[]{:S(2)}, u32[]{:S(2)}) collective-permute-start(f32[1,128,256]{2,1,0:T(8,128)S(1)} %get-tuple-element.90), channel_id=1, source_target_pairs={{0,4},{1,5},{2,6},{3,7},{4,0},{5,1},{6,2},{7,3},{8,12},{9,13},{10,... | collective-permute-start | bytes 393224 | tf_op jit(solution)/shard_map/ppermute | solution.py:50
  11.4 8.8 %collective-permute-start.3 = (f32[1,128,256]{2,1,0:T(8,128)S(1)}, f32[1,128,256]{2,1,0:T(8,128)S(1)}, u32[]{:S(2)}, u32[]{:S(2)}) collective-permute-start(f32[1,128,256]{2,1,0:T(8,128)S(1)} %get-tuple-element.56), channel_id=1, source_target_pairs={{0,4},{1,5},{2,6},{3,7},{4,0},{5,1},{6,2},{7,3},{8,12},{9,13},{10,... | collective-permute-start | bytes 393224 | tf_op jit(solution)/shard_map/ppermute | solution.py:50
  11.5 9.1 %collective-permute-start.1 = (f32[2,64,256]{2,1,0:T(8,128)S(1)}, f32[2,64,256]{2,1,0:T(8,128)S(1)}, u32[]{:S(2)}, u32[]{:S(2)}) collective-permute-start(f32[2,64,256]{2,1,0:T(8,128)S(1)} %get-tuple-element.54), channel_id=1, source_target_pairs={{0,2},{1,3},{2,0},{3,1},{4,6},{5,7},{6,4},{7,5},{8,10},{9,11},{10,... | collective-permute-start | bytes 393224 | tf_op jit(solution)/shard_map/ppermute | solution.py:50
  15.6 5.0 %collective-permute-start.2 = (f32[2,64,256]{2,1,0:T(8,128)S(1)}, f32[2,64,256]{2,1,0:T(8,128)S(1)}, u32[]{:S(2)}, u32[]{:S(2)}) collective-permute-start(f32[2,64,256]{2,1,0:T(8,128)S(1)} %get-tuple-element.55), channel_id=1, source_target_pairs={{0,16},{1,17},{2,18},{3,19},{4,20},{5,21},{6,22},{7,23},{8,24},{9,... | collective-permute-start | bytes 393224 | tf_op jit(solution)/shard_map/ppermute | solution.py:50
  20.6 7.2 %collective-permute-start.6 = (f32[2,64,256]{2,1,0:T(8,128)S(1)}, f32[2,64,256]{2,1,0:T(8,128)S(1)}, u32[]{:S(2)}, u32[]{:S(2)}) collective-permute-start(f32[2,64,256]{2,1,0:T(8,128)S(1)} %get-tuple-element.59), channel_id=1, source_target_pairs={{0,2},{1,3},{2,0},{3,1},{4,6},{5,7},{6,4},{7,5},{8,10},{9,11},{10,... | collective-permute-start | bytes 393224 | tf_op jit(solution)/shard_map/ppermute | solution.py:50
  20.9 14.2 %collective-permute-start.8 = (f32[1,2,128,256]{3,2,1,0:T(8,128)S(1)}, f32[1,2,128,256]{3,2,1,0:T(8,128)S(1)}, u32[]{:S(2)}, u32[]{:S(2)}) collective-permute-start(f32[1,2,128,256]{3,2,1,0:T(8,128)S(1)} %bitcast.6), channel_id=1, source_target_pairs={{0,4},{1,5},{2,6},{3,7},{4,0},{5,1},{6,2},{7,3},{8,12},{9,13},{10,... | collective-permute-start | bytes 786440 | tf_op jit(solution)/shard_map/ppermute | solution.py:50
  24.0 5.0 %collective-permute-start.7 = (f32[2,64,256]{2,1,0:T(8,128)S(1)}, f32[2,64,256]{2,1,0:T(8,128)S(1)}, u32[]{:S(2)}, u32[]{:S(2)}) collective-permute-start(f32[2,64,256]{2,1,0:T(8,128)S(1)} %get-tuple-element.60), channel_id=1, source_target_pairs={{0,16},{1,17},{2,18},{3,19},{4,20},{5,21},{6,22},{7,23},{8,24},{9,... | collective-permute-start | bytes 393224 | tf_op jit(solution)/shard_map/ppermute | solution.py:50
  25.5 9.7 %collective-permute-start.4 = (f32[4,64,256]{2,1,0:T(8,128)S(1)}, f32[4,64,256]{2,1,0:T(8,128)S(1)}, u32[]{:S(2)}, u32[]{:S(2)}) collective-permute-start(f32[4,64,256]{2,1,0:T(8,128)S(1)} %pad_maximum_fusion.6), channel_id=1, source_target_pairs={{0,1},{1,0},{2,3},{3,2},{4,5},{5,4},{6,7},{7,6},{8,9},{9,8},{10,11... | collective-permute-start | bytes 786440 | tf_op jit(solution)/shard_map/ppermute | solution.py:50
  27.0 9.4 %collective-permute-start.5 = (f32[4,64,256]{2,1,0:T(8,128)S(1)}, f32[4,64,256]{2,1,0:T(8,128)S(1)}, u32[]{:S(2)}, u32[]{:S(2)}) collective-permute-start(f32[4,64,256]{2,1,0:T(8,128)S(1)} %pad_maximum_fusion.7), channel_id=1, source_target_pairs={{0,2},{1,3},{2,0},{3,1},{4,6},{5,7},{6,4},{7,5},{8,10},{9,11},{10,... | collective-permute-start | bytes 786440 | tf_op jit(solution)/shard_map/ppermute | solution.py:50
  36.5 20.5 %collective-permute-start.9 = (f32[8,64,256]{2,1,0:T(8,128)S(1)}, f32[8,64,256]{2,1,0:T(8,128)S(1)}, u32[]{:S(2)}, u32[]{:S(2)}) collective-permute-start(f32[8,64,256]{2,1,0:T(8,128)S(1)} %pad_maximum_fusion.1.rest_0_), channel_id=1, source_target_pairs={{0,16},{1,17},{2,18},{3,19},{4,20},{5,21},{6,22},{7,23},{8,24},{9,... | collective-permute-start | bytes 1572872 | tf_op jit(solution)/shard_map/ppermute | solution.py:50
  38.0 19.0 %collective-permute-start.10 = (f32[8,64,256]{2,1,0:T(8,128)S(1)}, f32[8,64,256]{2,1,0:T(8,128)}, u32[]{:S(2)}, u32[]{:S(2)}) collective-permute-start(f32[8,64,256]{2,1,0:T(8,128)S(1)} %pad_maximum_fusion.2.rest_4_), channel_id=1, source_target_pairs={{0,1},{1,0},{2,3},{3,2},{4,5},{5,4},{6,7},{7,6},{8,9},{9,8},{10,11... | collective-permute-start | bytes 1572872 | tf_op jit(solution)/shard_map/ppermute | solution.py:50
  39.5 16.5 %collective-permute-start.11 = (f32[4,64,256]{2,1,0:T(8,128)S(1)}, f32[4,64,256]{2,1,0:T(8,128)S(1)}, u32[]{:S(2)}, u32[]{:S(2)}) collective-permute-start(f32[4,64,256]{2,1,0:T(8,128)S(1)} %pad_maximum_fusion.8), channel_id=1, source_target_pairs={{0,1},{1,0},{2,3},{3,2},{4,5},{5,4},{6,7},{7,6},{8,9},{9,8},{10,11... | collective-permute-start | bytes 786440 | tf_op jit(solution)/shard_map/ppermute | solution.py:50
  40.0 16.9 %collective-permute-start.12 = (f32[4,64,256]{2,1,0:T(8,128)S(1)}, f32[4,64,256]{2,1,0:T(8,128)S(1)}, u32[]{:S(2)}, u32[]{:S(2)}) collective-permute-start(f32[4,64,256]{2,1,0:T(8,128)S(1)} %pad_maximum_fusion.9), channel_id=1, source_target_pairs={{0,2},{1,3},{2,0},{3,1},{4,6},{5,7},{6,4},{7,5},{8,10},{9,11},{10,... | collective-permute-start | bytes 786440 | tf_op jit(solution)/shard_map/ppermute | solution.py:50
  40.7 17.4 %collective-permute-start.17 = (f32[2,2,128,256]{3,2,1,0:T(8,128)S(1)}, f32[2,2,128,256]{3,2,1,0:T(8,128)}, u32[]{:S(2)}, u32[]{:S(2)}) collective-permute-start(f32[2,2,128,256]{3,2,1,0:T(8,128)S(1)} %pad_maximum_fusion.3), channel_id=1, source_target_pairs={{0,2},{1,3},{2,0},{3,1},{4,6},{5,7},{6,4},{7,5},{8,10},{9,11},{10,... | collective-permute-start | bytes 1572872 | tf_op jit(solution)/shard_map/ppermute | solution.py:50
  57.1 5.9 %collective-permute-start.14 = (f32[8,64,256]{2,1,0:T(8,128)S(1)}, f32[8,64,256]{2,1,0:T(8,128)}, u32[]{:S(2)}, u32[]{:S(2)}) collective-permute-start(f32[8,64,256]{2,1,0:T(8,128)S(1)} %collective-permute-done.9.rest_1_), channel_id=1, source_target_pairs={{0,8},{1,9},{2,10},{3,11},{4,12},{5,13},{6,14},{7,15},{8,0},{9,1},... | collective-permute-start | bytes 1572872 | tf_op jit(solution)/shard_map/ppermute | solution.py:50
  57.6 5.4 %collective-permute-start.15 = (f32[8,64,256]{2,1,0:T(8,128)S(1)}, f32[8,64,256]{2,1,0:T(8,128)}, u32[]{:S(2)}, u32[]{:S(2)}) collective-permute-start(f32[8,64,256]{2,1,0:T(8,128)S(1)} %pad_maximum_fusion.2.rest_4_), channel_id=1, source_target_pairs={{0,8},{1,9},{2,10},{3,11},{4,12},{5,13},{6,14},{7,15},{8,0},{9,1},... | collective-permute-start | bytes 1572872 | tf_op jit(solution)/shard_map/ppermute | solution.py:50
  57.6 5.4 %collective-permute-start.16 = (f32[8,64,256]{2,1,0:T(8,128)}, f32[8,64,256]{2,1,0:T(8,128)}, u32[]{:S(2)}, u32[]{:S(2)}) collective-permute-start(f32[8,64,256]{2,1,0:T(8,128)} %collective-permute-done.10.rest_5_), channel_id=1, source_target_pairs={{0,8},{1,9},{2,10},{3,11},{4,12},{5,13},{6,14},{7,15},{8,0},{9,1},... | collective-permute-start | bytes 1572872 | tf_op jit(solution)/shard_map/ppermute | solution.py:50
  58.1 14.4 %collective-permute-start.18 = (f32[8,64,256]{2,1,0:T(8,128)}, f32[8,64,256]{2,1,0:T(8,128)S(1)}, u32[]{:S(2)}, u32[]{:S(2)}) collective-permute-start(f32[8,64,256]{2,1,0:T(8,128)} %pad_maximum_fusion.4.rest_0_), channel_id=1, source_target_pairs={{0,16},{1,17},{2,18},{3,19},{4,20},{5,21},{6,22},{7,23},{8,24},{9,... | collective-permute-start | bytes 1572872 | tf_op jit(solution)/shard_map/ppermute | solution.py:50
  59.8 14.1 %collective-permute-start.19 = (f32[8,64,256]{2,1,0:T(8,128)S(1)}, f32[8,64,256]{2,1,0:T(8,128)}, u32[]{:S(2)}, u32[]{:S(2)}) collective-permute-start(f32[8,64,256]{2,1,0:T(8,128)S(1)} %pad_maximum_fusion.5.rest_4_), channel_id=1, source_target_pairs={{0,1},{1,0},{2,3},{3,2},{4,5},{5,4},{6,7},{7,6},{8,9},{9,8},{10,11... | collective-permute-start | bytes 1572872 | tf_op jit(solution)/shard_map/ppermute | solution.py:50
  73.9 52.9 %all-to-all-start.1 = ((f32[8,4,128,128]{3,2,1,0:T(8,128)}), f32[8,4,128,128]{3,2,1,0:T(8,128)}, u32[]{:S(2)}, u32[]{:S(2)}) async-start(f32[8,4,128,128]{3,2,1,0:T(8,128)} %half_products.2), calls=%async_computation.1 | async-start | bytes 4194304 | tf_op jit(solution)/shard_map/all_to_all | solution.py:281
  78.9 3.3 %collective-permute-start.20 = (f32[8,64,256]{2,1,0:T(8,128)}, f32[8,64,256]{2,1,0:T(8,128)S(1)}, u32[]{:S(2)}, u32[]{:S(2)}) collective-permute-start(f32[8,64,256]{2,1,0:T(8,128)} %pad_maximum_fusion.4.rest_0_), channel_id=1, source_target_pairs={{0,8},{1,9},{2,10},{3,11},{4,12},{5,13},{6,14},{7,15},{8,0},{9,1},... | collective-permute-start | bytes 1572872 | tf_op jit(solution)/shard_map/ppermute | solution.py:50
  78.9 46.8 %collective-permute-start.25 = (f32[4,2,128,256]{3,2,1,0:T(8,128)S(1)}, f32[4,2,128,256]{3,2,1,0:T(8,128)S(1)}, u32[]{:S(2)}, u32[]{:S(2)}) collective-permute-start(f32[4,2,128,256]{3,2,1,0:T(8,128)S(1)} %pad_maximum_fusion.rest_0_), channel_id=1, source_target_pairs={{0,1},{1,0},{2,3},{3,2},{4,5},{5,4},{6,7},{7,6},{8,9},{9,8},{10,11... | collective-permute-start | bytes 3145736 | tf_op jit(solution)/shard_map/ppermute | solution.py:50
  80.9 44.7 %collective-permute-start.24 = (f32[4,2,128,256]{3,2,1,0:T(8,128)S(1)}, f32[4,2,128,256]{3,2,1,0:T(8,128)S(1)}, u32[]{:S(2)}, u32[]{:S(2)}) collective-permute-start(f32[4,2,128,256]{3,2,1,0:T(8,128)S(1)} %pad_maximum_fusion.rest_0_), channel_id=1, source_target_pairs={{0,16},{1,17},{2,18},{3,19},{4,20},{5,21},{6,22},{7,23},{8,24},{9,... | collective-permute-start | bytes 3145736 | tf_op jit(solution)/shard_map/ppermute | solution.py:50
  81.7 2.1 %collective-permute-start.21 = (f32[8,64,256]{2,1,0:T(8,128)}, f32[8,64,256]{2,1,0:T(8,128)S(1)}, u32[]{:S(2)}, u32[]{:S(2)}) collective-permute-start(f32[8,64,256]{2,1,0:T(8,128)} %copy-done.16), channel_id=1, source_target_pairs={{0,8},{1,9},{2,10},{3,11},{4,12},{5,13},{6,14},{7,15},{8,0},{9,1},... | collective-permute-start | bytes 1572872 | tf_op jit(solution)/shard_map/ppermute | solution.py:50
  81.7 2.9 %collective-permute-start.22 = (f32[8,64,256]{2,1,0:T(8,128)}, f32[8,64,256]{2,1,0:T(8,128)S(1)}, u32[]{:S(2)}, u32[]{:S(2)}) collective-permute-start(f32[8,64,256]{2,1,0:T(8,128)} %copy-done.4), channel_id=1, source_target_pairs={{0,8},{1,9},{2,10},{3,11},{4,12},{5,13},{6,14},{7,15},{8,0},{9,1},... | collective-permute-start | bytes 1572872 | tf_op jit(solution)/shard_map/ppermute | solution.py:50
  82.2 3.1 %collective-permute-start.23 = (f32[8,64,256]{2,1,0:T(8,128)}, f32[8,64,256]{2,1,0:T(8,128)S(1)}, u32[]{:S(2)}, u32[]{:S(2)}) collective-permute-start(f32[8,64,256]{2,1,0:T(8,128)} %collective-permute-done.19.rest_5_), channel_id=1, source_target_pairs={{0,8},{1,9},{2,10},{3,11},{4,12},{5,13},{6,14},{7,15},{8,0},{9,1},... | collective-permute-start | bytes 1572872 | tf_op jit(solution)/shard_map/ppermute | solution.py:50
  126.8 52.3 %all-to-all-start = ((f32[8,4,128,128]{3,2,1,0:T(8,128)}), f32[8,4,128,128]{3,2,1,0:T(8,128)}, u32[]{:S(2)}, u32[]{:S(2)}) async-start(f32[8,4,128,128]{3,2,1,0:T(8,128)} %half_products.3), calls=%async_computation | async-start | bytes 4194304 | tf_op jit(solution)/shard_map/all_to_all | solution.py:281
  131.3 24.0 %collective-permute-start.26 = (f32[4,2,128,256]{3,2,1,0:T(8,128)S(1)}, f32[4,2,128,256]{3,2,1,0:T(8,128)S(1)}, u32[]{:S(2)}, u32[]{:S(2)}) collective-permute-start(f32[4,2,128,256]{3,2,1,0:T(8,128)S(1)} %collective-permute-done.25.rest_2_), channel_id=1, source_target_pairs={{0,16},{1,17},{2,18},{3,19},{4,20},{5,21},{6,22},{7,23},{8,24},{9,... | collective-permute-start | bytes 3145736 | tf_op jit(solution)/shard_map/ppermute | solution.py:50
  131.7 23.5 %collective-permute-start.29 = (f32[4,2,128,256]{3,2,1,0:T(8,128)S(1)}, f32[4,2,128,256]{3,2,1,0:T(8,128)S(1)}, u32[]{:S(2)}, u32[]{:S(2)}) collective-permute-start(f32[4,2,128,256]{3,2,1,0:T(8,128)S(1)} %collective-permute-done.25.rest_2_), channel_id=1, source_target_pairs={{0,8},{1,9},{2,10},{3,11},{4,12},{5,13},{6,14},{7,15},{8,0},{9,1},... | collective-permute-start | bytes 3145736 | tf_op jit(solution)/shard_map/ppermute | solution.py:50
  131.7 23.5 %collective-permute-start.27 = (f32[4,2,128,256]{3,2,1,0:T(8,128)S(1)}, f32[4,2,128,256]{3,2,1,0:T(8,128)S(1)}, u32[]{:S(2)}, u32[]{:S(2)}) collective-permute-start(f32[4,2,128,256]{3,2,1,0:T(8,128)S(1)} %pad_maximum_fusion.rest_0_), channel_id=1, source_target_pairs={{0,8},{1,9},{2,10},{3,11},{4,12},{5,13},{6,14},{7,15},{8,0},{9,1},... | collective-permute-start | bytes 3145736 | tf_op jit(solution)/shard_map/ppermute | solution.py:50
  132.2 23.0 %collective-permute-start.28 = (f32[4,2,128,256]{3,2,1,0:T(8,128)S(1)}, f32[4,2,128,256]{3,2,1,0:T(8,128)S(1)}, u32[]{:S(2)}, u32[]{:S(2)}) collective-permute-start(f32[4,2,128,256]{3,2,1,0:T(8,128)S(1)} %collective-permute-done.24.rest_1_), channel_id=1, source_target_pairs={{0,8},{1,9},{2,10},{3,11},{4,12},{5,13},{6,14},{7,15},{8,0},{9,1},... | collective-permute-start | bytes 3145736 | tf_op jit(solution)/shard_map/ppermute | solution.py:50
  155.3 2.7 %collective-permute-start.30 = (f32[4,2,128,256]{3,2,1,0:T(8,128)S(1)}, f32[4,2,128,256]{3,2,1,0:T(8,128)S(1)}, u32[]{:S(2)}, u32[]{:S(2)}) collective-permute-start(f32[4,2,128,256]{3,2,1,0:T(8,128)S(1)} %collective-permute-done.26.rest_3_), channel_id=1, source_target_pairs={{0,8},{1,9},{2,10},{3,11},{4,12},{5,13},{6,14},{7,15},{8,0},{9,1},... | collective-permute-start | bytes 3145736 | tf_op jit(solution)/shard_map/ppermute | solution.py:50
  (23 other events, 181.4 us)

commit v6 on v5

--- a/solution.py
+++ b/solution.py
@@ -169,7 +169,7 @@
         in_specs=[SMEM, SMEM, VMEM, VMEM] + [VMEM] * len(arrays),
         out_specs=VMEM,
         scratch_shapes=[pltpu.VMEM((orbitals, orbitals), jnp.bfloat16)] * 2,
-        compiler_params=PARAMS,
+        compiler_params=pltpu.CompilerParams(vmem_limit_bytes=56 * 1024 * 1024),
         cost_estimate=cost(6 * aux_count * block * orbitals * orbitals, 10 * orbitals * orbitals),
         name="half_products",
     )(position, listed, a_high, a_low, *arrays)

time: 187 us -> 186 us (level)
  local copies, waits for them, and re-layouts: 16.7 us -> 9.8 us
  waiting for transfers between devices: 95.7 us -> 98.6 us
  Pallas kernels: 32.3 us -> 35.1 us
    unnamed x45 -> x47, local copies, waits for them, and re-layouts: 15.7 us -> 8.77 us
    ppermute x31, waiting for transfers between devices: 88.1 us -> 91 us  [permute(): return lax.ppermute(value, ('aux', 'orb'), pairs)]
    pallas_call x2, Pallas kernels: 13.7 us -> 16.4 us  [half_products(): pl.pallas_call(functools.partial(half_kernel, keys, time, split), out_sha...]
  transfers between devices with their start and end apart: 33 -> 33, of which waited for: 18 -> 18; matrix products, arithmetic and copies ran while one was open for 1% -> 2% of each run, Pallas kernels for 13% -> 15%
where the time goes in v6:
time: 186 us
  waiting for transfers between devices  98.6 us (53%)
  starting transfers between devices  39.1 us (21%)
  Pallas kernels  35.1 us (19%)
  local copies, waits for them, and re-layouts  9.8 us (5%)
  other arithmetic  2.93 us (2%)
    ppermute x31, waiting for transfers between devices, permute(): return lax.ppermute(value, ('aux', 'orb'), pairs)  91 us
    ppermute x31, starting transfers between devices, permute(): return lax.ppermute(value, ('aux', 'orb'), pairs)  29.5 us
    pallas_call x2, Pallas kernels, half_products(): pl.pallas_call(functools.partial(half_kernel, keys, time, split), out_sha...  16.4 us
    pallas_call x2, Pallas kernels, full_products(): pl.pallas_call(functools.partial(full_kernel, split), grid=(orbitals // t...  15 us
    all_to_all x2, starting transfers between devices, deliver(): return lax.all_to_all(made, 'orb', split_axis=0, concat_axis=0, tiled=True)  9.51 us
    unnamed x47, local copies, waits for them, and re-layouts  8.77 us
    all_to_all x2, waiting for transfers between devices, deliver(): return lax.all_to_all(made, 'orb', split_axis=0, concat_axis=0, tiled=True)  7.55 us
  transfers between devices with their start and end apart: 33, of which 18 were waited for; matrix products, arithmetic and copies ran while one was open for 2% of the time, Pallas kernels for 15%

profile of v6, /device:TPU:0, one launch (start us, length us, event | category | flops | bytes accessed | tf_op | source)
XLA Modules:
  0.0 185.8 jit_solution(1462069516193549626)
XLA Ops:
  1.0 4.1 %collective-permute-start = (f32[1,128,256]{2,1,0:T(8,128)S(1)}, f32[1,128,256]{2,1,0:T(8,128)S(1)}, u32[]{:S(2)}, u32[]{:S(2)}) collective-permute-start(f32[1,128,256]{2,1,0:T(8,128)S(1)} %get-tuple-element.90), channel_id=1, source_target_pairs={{0,4},{1,5},{2,6},{3,7},{4,0},{5,1},{6,2},{7,3},{8,12},{9,13},{10,... | collective-permute-start | bytes 393224 | tf_op jit(solution)/shard_map/ppermute | solution.py:50
  5.2 1.6 copy-done.3
  6.8 1.9 %split_integrals.1 = (bf16[512,1024]{1,0:T(8,128)(2,1)S(1)}, bf16[512,1024]{1,0:T(8,128)(2,1)S(1)}, bf16[512,1024]{1,0:T(8,128)(2,1)S(1)}, bf16[512,1024]{1,0:T(8,128)(2,1)S(1)}) custom-call(f32[2,8]{1,0:T(2,128)S(1)} %convert_reduce_fusion.listed, f32[4,128,1024]{2,1,0:T(8,128)S(1)} %bitcast.5), custom_call_target="tpu_custom_call" | custom-call | flops 4194304 | bytes 6291456 | tf_op jit(solution)/shard_map/split_integrals/pallas_call | solution.py:121
  8.7 2.7 %collective-permute-done = f32[1,128,256]{2,1,0:T(8,128)S(1)} collective-permute-done((f32[1,128,256]{2,1,0:T(8,128)S(1)}, f32[1,128,256]{2,1,0:T(8,128)S(1)}, u32[]{:S(2)}, u32[]{:S(2)}) %collective-permute-start) | collective-permute-done | bytes 131104 | tf_op jit(solution)/shard_map/ppermute | solution.py:50
  11.5 4.1 %collective-permute-start.1 = (f32[2,64,256]{2,1,0:T(8,128)S(1)}, f32[2,64,256]{2,1,0:T(8,128)S(1)}, u32[]{:S(2)}, u32[]{:S(2)}) collective-permute-start(f32[2,64,256]{2,1,0:T(8,128)S(1)} %get-tuple-element.54), channel_id=1, source_target_pairs={{0,2},{1,3},{2,0},{3,1},{4,6},{5,7},{6,4},{7,5},{8,10},{9,11},{10,... | collective-permute-start | bytes 393224 | tf_op jit(solution)/shard_map/ppermute | solution.py:50
  15.6 1.5 collective-permute-start.2
  17.1 3.1 %collective-permute-done.3 = f32[1,128,256]{2,1,0:T(8,128)S(1)} collective-permute-done((f32[1,128,256]{2,1,0:T(8,128)S(1)}, f32[1,128,256]{2,1,0:T(8,128)S(1)}, u32[]{:S(2)}, u32[]{:S(2)}) %collective-permute-start.3) | collective-permute-done | bytes 131104 | tf_op jit(solution)/shard_map/ppermute | solution.py:50
  20.9 3.1 %collective-permute-start.8 = (f32[1,2,128,256]{3,2,1,0:T(8,128)S(1)}, f32[1,2,128,256]{3,2,1,0:T(8,128)S(1)}, u32[]{:S(2)}, u32[]{:S(2)}) collective-permute-start(f32[1,2,128,256]{3,2,1,0:T(8,128)S(1)} %bitcast.6), channel_id=1, source_target_pairs={{0,4},{1,5},{2,6},{3,7},{4,0},{5,1},{6,2},{7,3},{8,12},{9,13},{10,... | collective-permute-start | bytes 786440 | tf_op jit(solution)/shard_map/ppermute | solution.py:50
  24.0 1.5 collective-permute-start.7
  25.5 1.5 collective-permute-start.4
  29.0 6.1 %collective-permute-done.8 = f32[1,2,128,256]{3,2,1,0:T(8,128)S(1)} collective-permute-done((f32[1,2,128,256]{3,2,1,0:T(8,128)S(1)}, f32[1,2,128,256]{3,2,1,0:T(8,128)S(1)}, u32[]{:S(2)}, u32[]{:S(2)}) %collective-permute-start.8) | collective-permute-done | bytes 262176 | tf_op jit(solution)/shard_map/ppermute | solution.py:50
  36.5 1.6 collective-permute-start.9
  38.0 1.5 collective-permute-start.10
  40.7 1.4 collective-permute-start.17
  42.1 14.0 %collective-permute-done.11 = f32[4,64,256]{2,1,0:T(8,128)S(1)} collective-permute-done((f32[4,64,256]{2,1,0:T(8,128)S(1)}, f32[4,64,256]{2,1,0:T(8,128)S(1)}, u32[]{:S(2)}, u32[]{:S(2)}) %collective-permute-start.11) | collective-permute-done | bytes 262176 | tf_op jit(solution)/shard_map/ppermute | solution.py:50
  59.0 1.7 collective-permute-start.19
  62.5 8.2 %half_products.2 = f32[8,4,128,128]{3,2,1,0:T(8,128)} custom-call(s32[2]{0:T(128)} %pad_add_fusion.position, f32[2,8]{1,0:T(2,128)} %copy-done.4, bf16[512,1024]{1,0:T(8,128)(2,1)} %copy-done.10, bf16[512,1024]{1,0:T(8,128)(2,1)} %copy-done.11, f32[8,64,256]{2,1,0:T(8,128)} %copy-done.13, f32[8,64,256]{2,1,0:T(8,128)} %collective-permute-done.9.rest_1_, ...), custom_call_target="tpu_custom_call" | custom-call | flops 3221225472 | bytes 10485760 | tf_op jit(solution)/shard_map/half_products/pallas_call | solution.py:166
  70.7 1.5 collective-permute-done.18.rest_1_
  73.1 5.0 %all-to-all-start.1 = ((f32[8,4,128,128]{3,2,1,0:T(8,128)}), f32[8,4,128,128]{3,2,1,0:T(8,128)}, u32[]{:S(2)}, u32[]{:S(2)}) async-start(f32[8,4,128,128]{3,2,1,0:T(8,128)} %half_products.2), calls=%async_computation.1 | async-start | bytes 4194304 | tf_op jit(solution)/shard_map/all_to_all | solution.py:281
  78.1 2.0 %collective-permute-start.25 = (f32[4,2,128,256]{3,2,1,0:T(8,128)S(1)}, f32[4,2,128,256]{3,2,1,0:T(8,128)S(1)}, u32[]{:S(2)}, u32[]{:S(2)}) collective-permute-start(f32[4,2,128,256]{3,2,1,0:T(8,128)S(1)} %pad_maximum_fusion.rest_0_), channel_id=1, source_target_pairs={{0,1},{1,0},{2,3},{3,2},{4,5},{5,4},{6,7},{7,6},{8,9},{9,8},{10,11... | collective-permute-start | bytes 3145736 | tf_op jit(solution)/shard_map/ppermute | solution.py:50
  81.5 1.5 collective-permute-done.21.rest_3_
  85.4 8.2 %half_products.3 = f32[8,4,128,128]{3,2,1,0:T(8,128)} custom-call(s32[2]{0:T(128)} %pad_add_fusion.position, f32[2,8]{1,0:T(2,128)} %copy-done.4, bf16[512,1024]{1,0:T(8,128)(2,1)} %copy-done.8, bf16[512,1024]{1,0:T(8,128)(2,1)} %copy-done.9, f32[8,64,256]{2,1,0:T(8,128)} %pad_maximum_fusion.4.rest_0_, f32[8,64,256]{2,1,0:T(8,128)} %copy-done.17, ...), custom_call_target="tpu_custom_call" | custom-call | flops 3221225472 | bytes 10485760 | tf_op jit(solution)/shard_map/half_products/pallas_call | solution.py:166
  93.6 31.3 %collective-permute-done.25.rest_2_ = f32[4,2,128,256]{3,2,1,0:T(8,128)S(1)} collective-permute-done((f32[4,2,128,256]{3,2,1,0:T(8,128)S(1)}, f32[4,2,128,256]{3,2,1,0:T(8,128)S(1)}, u32[]{:S(2)}, u32[]{:S(2)}) %collective-permute-start.25) | collective-permute-done | bytes 1048608 | tf_op jit(solution)/shard_map/ppermute | solution.py:50
  126.0 4.5 %all-to-all-start = ((f32[8,4,128,128]{3,2,1,0:T(8,128)}), f32[8,4,128,128]{3,2,1,0:T(8,128)}, u32[]{:S(2)}, u32[]{:S(2)}) async-start(f32[8,4,128,128]{3,2,1,0:T(8,128)} %half_products.3), calls=%async_computation | async-start | bytes 4194304 | tf_op jit(solution)/shard_map/all_to_all | solution.py:281
  131.5 23.0 %collective-permute-done.26.rest_3_ = f32[4,2,128,256]{3,2,1,0:T(8,128)S(1)} collective-permute-done((f32[4,2,128,256]{3,2,1,0:T(8,128)S(1)}, f32[4,2,128,256]{3,2,1,0:T(8,128)S(1)}, u32[]{:S(2)}, u32[]{:S(2)}) %collective-permute-start.26) | collective-permute-done | bytes 1048608 | tf_op jit(solution)/shard_map/ppermute | solution.py:50
  154.5 2.6 %collective-permute-done.30.rest_7_ = f32[4,2,128,256]{3,2,1,0:T(8,128)S(1)} collective-permute-done((f32[4,2,128,256]{3,2,1,0:T(8,128)S(1)}, f32[4,2,128,256]{3,2,1,0:T(8,128)S(1)}, u32[]{:S(2)}, u32[]{:S(2)}) %collective-permute-start.30) | collective-permute-done | bytes 1048608 | tf_op jit(solution)/shard_map/ppermute | solution.py:50
  157.1 1.8 place.1
  159.0 1.4 copy-done.1
  161.6 1.4 copy-done.6
  164.3 7.5 %full_products.2.rest_0_ = f32[2,4,1,1024,128]{4,3,2,1,0:T(8,128)} custom-call(bf16[1024,1024]{1,0:T(8,128)(2,1)} %copy-done.6, bf16[1024,1024]{1,0:T(8,128)(2,1)} %copy-done.7, f32[8,4,128,128]{3,2,1,0:T(8,128)} %all-to-all-done.1.received), custom_call_target="tpu_custom_call" | custom-call | flops 3221225472 | bytes 12582912 | tf_op jit(solution)/shard_map/full_products/pallas_call | solution.py:243
  171.8 6.5 %all-to-all-done.received = f32[8,4,128,128]{3,2,1,0:T(8,128)} async-done(((f32[8,4,128,128]{3,2,1,0:T(8,128)}), f32[8,4,128,128]{3,2,1,0:T(8,128)}, u32[]{:S(2)}, u32[]{:S(2)}) %all-to-all-start) | async-done | bytes 2097184 | tf_op jit(solution)/shard_map/all_to_all | solution.py:281
  178.3 7.5 %full_products.3 = f32[2,4,1,1024,128]{4,3,2,1,0:T(8,128)} custom-call(bf16[1024,1024]{1,0:T(8,128)(2,1)} %copy-done.1, bf16[1024,1024]{1,0:T(8,128)(2,1)} %copy-done.2, f32[8,4,128,128]{3,2,1,0:T(8,128)} %all-to-all-done.received, f32[2,4,1,1024,128]{4,3,2,1,0:T(8,128)} %full_products.2.rest_0_), custom_call_target="tpu_custom_call", output_to_operand_aliasing={{}: (3, {})} | custom-call | flops 3221225472 | bytes 12582912 | tf_op jit(solution)/shard_map/full_products/pallas_call | solution.py:243
  (104 shorter events, 20.2 us)
Async XLA Ops:
  1.0 10.4 %collective-permute-start = (f32[1,128,256]{2,1,0:T(8,128)S(1)}, f32[1,128,256]{2,1,0:T(8,128)S(1)}, u32[]{:S(2)}, u32[]{:S(2)}) collective-permute-start(f32[1,128,256]{2,1,0:T(8,128)S(1)} %get-tuple-element.90), channel_id=1, source_target_pairs={{0,4},{1,5},{2,6},{3,7},{4,0},{5,1},{6,2},{7,3},{8,12},{9,13},{10,... | collective-permute-start | bytes 393224 | tf_op jit(solution)/shard_map/ppermute | solution.py:50
  11.4 8.8 %collective-permute-start.3 = (f32[1,128,256]{2,1,0:T(8,128)S(1)}, f32[1,128,256]{2,1,0:T(8,128)S(1)}, u32[]{:S(2)}, u32[]{:S(2)}) collective-permute-start(f32[1,128,256]{2,1,0:T(8,128)S(1)} %get-tuple-element.56), channel_id=1, source_target_pairs={{0,4},{1,5},{2,6},{3,7},{4,0},{5,1},{6,2},{7,3},{8,12},{9,13},{10,... | collective-permute-start | bytes 393224 | tf_op jit(solution)/shard_map/ppermute | solution.py:50
  11.5 9.1 %collective-permute-start.1 = (f32[2,64,256]{2,1,0:T(8,128)S(1)}, f32[2,64,256]{2,1,0:T(8,128)S(1)}, u32[]{:S(2)}, u32[]{:S(2)}) collective-permute-start(f32[2,64,256]{2,1,0:T(8,128)S(1)} %get-tuple-element.54), channel_id=1, source_target_pairs={{0,2},{1,3},{2,0},{3,1},{4,6},{5,7},{6,4},{7,5},{8,10},{9,11},{10,... | collective-permute-start | bytes 393224 | tf_op jit(solution)/shard_map/ppermute | solution.py:50
  15.6 5.0 %collective-permute-start.2 = (f32[2,64,256]{2,1,0:T(8,128)S(1)}, f32[2,64,256]{2,1,0:T(8,128)S(1)}, u32[]{:S(2)}, u32[]{:S(2)}) collective-permute-start(f32[2,64,256]{2,1,0:T(8,128)S(1)} %get-tuple-element.55), channel_id=1, source_target_pairs={{0,16},{1,17},{2,18},{3,19},{4,20},{5,21},{6,22},{7,23},{8,24},{9,... | collective-permute-start | bytes 393224 | tf_op jit(solution)/shard_map/ppermute | solution.py:50
  20.6 7.2 %collective-permute-start.6 = (f32[2,64,256]{2,1,0:T(8,128)S(1)}, f32[2,64,256]{2,1,0:T(8,128)S(1)}, u32[]{:S(2)}, u32[]{:S(2)}) collective-permute-start(f32[2,64,256]{2,1,0:T(8,128)S(1)} %get-tuple-element.59), channel_id=1, source_target_pairs={{0,2},{1,3},{2,0},{3,1},{4,6},{5,7},{6,4},{7,5},{8,10},{9,11},{10,... | collective-permute-start | bytes 393224 | tf_op jit(solution)/shard_map/ppermute | solution.py:50
  20.9 14.2 %collective-permute-start.8 = (f32[1,2,128,256]{3,2,1,0:T(8,128)S(1)}, f32[1,2,128,256]{3,2,1,0:T(8,128)S(1)}, u32[]{:S(2)}, u32[]{:S(2)}) collective-permute-start(f32[1,2,128,256]{3,2,1,0:T(8,128)S(1)} %bitcast.6), channel_id=1, source_target_pairs={{0,4},{1,5},{2,6},{3,7},{4,0},{5,1},{6,2},{7,3},{8,12},{9,13},{10,... | collective-permute-start | bytes 786440 | tf_op jit(solution)/shard_map/ppermute | solution.py:50
  24.0 5.0 %collective-permute-start.7 = (f32[2,64,256]{2,1,0:T(8,128)S(1)}, f32[2,64,256]{2,1,0:T(8,128)S(1)}, u32[]{:S(2)}, u32[]{:S(2)}) collective-permute-start(f32[2,64,256]{2,1,0:T(8,128)S(1)} %get-tuple-element.60), channel_id=1, source_target_pairs={{0,16},{1,17},{2,18},{3,19},{4,20},{5,21},{6,22},{7,23},{8,24},{9,... | collective-permute-start | bytes 393224 | tf_op jit(solution)/shard_map/ppermute | solution.py:50
  25.5 9.7 %collective-permute-start.4 = (f32[4,64,256]{2,1,0:T(8,128)S(1)}, f32[4,64,256]{2,1,0:T(8,128)S(1)}, u32[]{:S(2)}, u32[]{:S(2)}) collective-permute-start(f32[4,64,256]{2,1,0:T(8,128)S(1)} %pad_maximum_fusion.6), channel_id=1, source_target_pairs={{0,1},{1,0},{2,3},{3,2},{4,5},{5,4},{6,7},{7,6},{8,9},{9,8},{10,11... | collective-permute-start | bytes 786440 | tf_op jit(solution)/shard_map/ppermute | solution.py:50
  27.0 9.4 %collective-permute-start.5 = (f32[4,64,256]{2,1,0:T(8,128)S(1)}, f32[4,64,256]{2,1,0:T(8,128)S(1)}, u32[]{:S(2)}, u32[]{:S(2)}) collective-permute-start(f32[4,64,256]{2,1,0:T(8,128)S(1)} %pad_maximum_fusion.7), channel_id=1, source_target_pairs={{0,2},{1,3},{2,0},{3,1},{4,6},{5,7},{6,4},{7,5},{8,10},{9,11},{10,... | collective-permute-start | bytes 786440 | tf_op jit(solution)/shard_map/ppermute | solution.py:50
  36.5 20.5 %collective-permute-start.9 = (f32[8,64,256]{2,1,0:T(8,128)S(1)}, f32[8,64,256]{2,1,0:T(8,128)}, u32[]{:S(2)}, u32[]{:S(2)}) collective-permute-start(f32[8,64,256]{2,1,0:T(8,128)S(1)} %pad_maximum_fusion.1.rest_0_), channel_id=1, source_target_pairs={{0,16},{1,17},{2,18},{3,19},{4,20},{5,21},{6,22},{7,23},{8,24},{9,... | collective-permute-start | bytes 1572872 | tf_op jit(solution)/shard_map/ppermute | solution.py:50
  38.0 19.0 %collective-permute-start.10 = (f32[8,64,256]{2,1,0:T(8,128)S(1)}, f32[8,64,256]{2,1,0:T(8,128)}, u32[]{:S(2)}, u32[]{:S(2)}) collective-permute-start(f32[8,64,256]{2,1,0:T(8,128)S(1)} %pad_maximum_fusion.2.rest_4_), channel_id=1, source_target_pairs={{0,1},{1,0},{2,3},{3,2},{4,5},{5,4},{6,7},{7,6},{8,9},{9,8},{10,11... | collective-permute-start | bytes 1572872 | tf_op jit(solution)/shard_map/ppermute | solution.py:50
  39.5 16.5 %collective-permute-start.11 = (f32[4,64,256]{2,1,0:T(8,128)S(1)}, f32[4,64,256]{2,1,0:T(8,128)S(1)}, u32[]{:S(2)}, u32[]{:S(2)}) collective-permute-start(f32[4,64,256]{2,1,0:T(8,128)S(1)} %pad_maximum_fusion.8), channel_id=1, source_target_pairs={{0,1},{1,0},{2,3},{3,2},{4,5},{5,4},{6,7},{7,6},{8,9},{9,8},{10,11... | collective-permute-start | bytes 786440 | tf_op jit(solution)/shard_map/ppermute | solution.py:50
  40.0 16.9 %collective-permute-start.12 = (f32[4,64,256]{2,1,0:T(8,128)S(1)}, f32[4,64,256]{2,1,0:T(8,128)S(1)}, u32[]{:S(2)}, u32[]{:S(2)}) collective-permute-start(f32[4,64,256]{2,1,0:T(8,128)S(1)} %pad_maximum_fusion.9), channel_id=1, source_target_pairs={{0,2},{1,3},{2,0},{3,1},{4,6},{5,7},{6,4},{7,5},{8,10},{9,11},{10,... | collective-permute-start | bytes 786440 | tf_op jit(solution)/shard_map/ppermute | solution.py:50
  40.7 17.4 %collective-permute-start.17 = (f32[2,2,128,256]{3,2,1,0:T(8,128)S(1)}, f32[2,2,128,256]{3,2,1,0:T(8,128)S(1)}, u32[]{:S(2)}, u32[]{:S(2)}) collective-permute-start(f32[2,2,128,256]{3,2,1,0:T(8,128)S(1)} %pad_maximum_fusion.3), channel_id=1, source_target_pairs={{0,2},{1,3},{2,0},{3,1},{4,6},{5,7},{6,4},{7,5},{8,10},{9,11},{10,... | collective-permute-start | bytes 1572872 | tf_op jit(solution)/shard_map/ppermute | solution.py:50
  57.1 5.4 %collective-permute-start.14 = (f32[8,64,256]{2,1,0:T(8,128)}, f32[8,64,256]{2,1,0:T(8,128)}, u32[]{:S(2)}, u32[]{:S(2)}) collective-permute-start(f32[8,64,256]{2,1,0:T(8,128)} %collective-permute-done.9.rest_1_), channel_id=1, source_target_pairs={{0,8},{1,9},{2,10},{3,11},{4,12},{5,13},{6,14},{7,15},{8,0},{9,1},... | collective-permute-start | bytes 1572872 | tf_op jit(solution)/shard_map/ppermute | solution.py:50
  57.6 4.9 %collective-permute-start.15 = (f32[8,64,256]{2,1,0:T(8,128)S(1)}, f32[8,64,256]{2,1,0:T(8,128)}, u32[]{:S(2)}, u32[]{:S(2)}) collective-permute-start(f32[8,64,256]{2,1,0:T(8,128)S(1)} %pad_maximum_fusion.2.rest_4_), channel_id=1, source_target_pairs={{0,8},{1,9},{2,10},{3,11},{4,12},{5,13},{6,14},{7,15},{8,0},{9,1},... | collective-permute-start | bytes 1572872 | tf_op jit(solution)/shard_map/ppermute | solution.py:50
  57.7 4.9 %collective-permute-start.16 = (f32[8,64,256]{2,1,0:T(8,128)}, f32[8,64,256]{2,1,0:T(8,128)}, u32[]{:S(2)}, u32[]{:S(2)}) collective-permute-start(f32[8,64,256]{2,1,0:T(8,128)} %collective-permute-done.10.rest_5_), channel_id=1, source_target_pairs={{0,8},{1,9},{2,10},{3,11},{4,12},{5,13},{6,14},{7,15},{8,0},{9,1},... | collective-permute-start | bytes 1572872 | tf_op jit(solution)/shard_map/ppermute | solution.py:50
  58.1 14.1 %collective-permute-start.18 = (f32[8,64,256]{2,1,0:T(8,128)}, f32[8,64,256]{2,1,0:T(8,128)S(1)}, u32[]{:S(2)}, u32[]{:S(2)}) collective-permute-start(f32[8,64,256]{2,1,0:T(8,128)} %pad_maximum_fusion.4.rest_0_), channel_id=1, source_target_pairs={{0,16},{1,17},{2,18},{3,19},{4,20},{5,21},{6,22},{7,23},{8,24},{9,... | collective-permute-start | bytes 1572872 | tf_op jit(solution)/shard_map/ppermute | solution.py:50
  59.0 14.1 %collective-permute-start.19 = (f32[8,64,256]{2,1,0:T(8,128)S(1)}, f32[8,64,256]{2,1,0:T(8,128)}, u32[]{:S(2)}, u32[]{:S(2)}) collective-permute-start(f32[8,64,256]{2,1,0:T(8,128)S(1)} %pad_maximum_fusion.5.rest_4_), channel_id=1, source_target_pairs={{0,1},{1,0},{2,3},{3,2},{4,5},{5,4},{6,7},{7,6},{8,9},{9,8},{10,11... | collective-permute-start | bytes 1572872 | tf_op jit(solution)/shard_map/ppermute | solution.py:50
  73.1 52.9 %all-to-all-start.1 = ((f32[8,4,128,128]{3,2,1,0:T(8,128)}), f32[8,4,128,128]{3,2,1,0:T(8,128)}, u32[]{:S(2)}, u32[]{:S(2)}) async-start(f32[8,4,128,128]{3,2,1,0:T(8,128)} %half_products.2), calls=%async_computation.1 | async-start | bytes 4194304 | tf_op jit(solution)/shard_map/all_to_all | solution.py:281
  78.1 3.3 %collective-permute-start.20 = (f32[8,64,256]{2,1,0:T(8,128)}, f32[8,64,256]{2,1,0:T(8,128)S(1)}, u32[]{:S(2)}, u32[]{:S(2)}) collective-permute-start(f32[8,64,256]{2,1,0:T(8,128)} %pad_maximum_fusion.4.rest_0_), channel_id=1, source_target_pairs={{0,8},{1,9},{2,10},{3,11},{4,12},{5,13},{6,14},{7,15},{8,0},{9,1},... | collective-permute-start | bytes 1572872 | tf_op jit(solution)/shard_map/ppermute | solution.py:50
  78.1 46.8 %collective-permute-start.25 = (f32[4,2,128,256]{3,2,1,0:T(8,128)S(1)}, f32[4,2,128,256]{3,2,1,0:T(8,128)S(1)}, u32[]{:S(2)}, u32[]{:S(2)}) collective-permute-start(f32[4,2,128,256]{3,2,1,0:T(8,128)S(1)} %pad_maximum_fusion.rest_0_), channel_id=1, source_target_pairs={{0,1},{1,0},{2,3},{3,2},{4,5},{5,4},{6,7},{7,6},{8,9},{9,8},{10,11... | collective-permute-start | bytes 3145736 | tf_op jit(solution)/shard_map/ppermute | solution.py:50
  80.1 44.8 %collective-permute-start.24 = (f32[4,2,128,256]{3,2,1,0:T(8,128)S(1)}, f32[4,2,128,256]{3,2,1,0:T(8,128)S(1)}, u32[]{:S(2)}, u32[]{:S(2)}) collective-permute-start(f32[4,2,128,256]{3,2,1,0:T(8,128)S(1)} %pad_maximum_fusion.rest_0_), channel_id=1, source_target_pairs={{0,16},{1,17},{2,18},{3,19},{4,20},{5,21},{6,22},{7,23},{8,24},{9,... | collective-permute-start | bytes 3145736 | tf_op jit(solution)/shard_map/ppermute | solution.py:50
  80.9 2.1 %collective-permute-start.21 = (f32[8,64,256]{2,1,0:T(8,128)}, f32[8,64,256]{2,1,0:T(8,128)S(1)}, u32[]{:S(2)}, u32[]{:S(2)}) collective-permute-start(f32[8,64,256]{2,1,0:T(8,128)} %copy-done.17), channel_id=1, source_target_pairs={{0,8},{1,9},{2,10},{3,11},{4,12},{5,13},{6,14},{7,15},{8,0},{9,1},... | collective-permute-start | bytes 1572872 | tf_op jit(solution)/shard_map/ppermute | solution.py:50
  80.9 2.9 %collective-permute-start.22 = (f32[8,64,256]{2,1,0:T(8,128)}, f32[8,64,256]{2,1,0:T(8,128)S(1)}, u32[]{:S(2)}, u32[]{:S(2)}) collective-permute-start(f32[8,64,256]{2,1,0:T(8,128)} %copy-done.12), channel_id=1, source_target_pairs={{0,8},{1,9},{2,10},{3,11},{4,12},{5,13},{6,14},{7,15},{8,0},{9,1},... | collective-permute-start | bytes 1572872 | tf_op jit(solution)/shard_map/ppermute | solution.py:50
  81.4 3.1 %collective-permute-start.23 = (f32[8,64,256]{2,1,0:T(8,128)}, f32[8,64,256]{2,1,0:T(8,128)S(1)}, u32[]{:S(2)}, u32[]{:S(2)}) collective-permute-start(f32[8,64,256]{2,1,0:T(8,128)} %collective-permute-done.19.rest_5_), channel_id=1, source_target_pairs={{0,8},{1,9},{2,10},{3,11},{4,12},{5,13},{6,14},{7,15},{8,0},{9,1},... | collective-permute-start | bytes 1572872 | tf_op jit(solution)/shard_map/ppermute | solution.py:50
  126.0 52.3 %all-to-all-start = ((f32[8,4,128,128]{3,2,1,0:T(8,128)}), f32[8,4,128,128]{3,2,1,0:T(8,128)}, u32[]{:S(2)}, u32[]{:S(2)}) async-start(f32[8,4,128,128]{3,2,1,0:T(8,128)} %half_products.3), calls=%async_computation | async-start | bytes 4194304 | tf_op jit(solution)/shard_map/all_to_all | solution.py:281
  130.5 24.0 %collective-permute-start.26 = (f32[4,2,128,256]{3,2,1,0:T(8,128)S(1)}, f32[4,2,128,256]{3,2,1,0:T(8,128)S(1)}, u32[]{:S(2)}, u32[]{:S(2)}) collective-permute-start(f32[4,2,128,256]{3,2,1,0:T(8,128)S(1)} %collective-permute-done.25.rest_2_), channel_id=1, source_target_pairs={{0,16},{1,17},{2,18},{3,19},{4,20},{5,21},{6,22},{7,23},{8,24},{9,... | collective-permute-start | bytes 3145736 | tf_op jit(solution)/shard_map/ppermute | solution.py:50
  131.0 23.5 %collective-permute-start.29 = (f32[4,2,128,256]{3,2,1,0:T(8,128)S(1)}, f32[4,2,128,256]{3,2,1,0:T(8,128)S(1)}, u32[]{:S(2)}, u32[]{:S(2)}) collective-permute-start(f32[4,2,128,256]{3,2,1,0:T(8,128)S(1)} %collective-permute-done.25.rest_2_), channel_id=1, source_target_pairs={{0,8},{1,9},{2,10},{3,11},{4,12},{5,13},{6,14},{7,15},{8,0},{9,1},... | collective-permute-start | bytes 3145736 | tf_op jit(solution)/shard_map/ppermute | solution.py:50
  131.0 23.5 %collective-permute-start.27 = (f32[4,2,128,256]{3,2,1,0:T(8,128)S(1)}, f32[4,2,128,256]{3,2,1,0:T(8,128)S(1)}, u32[]{:S(2)}, u32[]{:S(2)}) collective-permute-start(f32[4,2,128,256]{3,2,1,0:T(8,128)S(1)} %pad_maximum_fusion.rest_0_), channel_id=1, source_target_pairs={{0,8},{1,9},{2,10},{3,11},{4,12},{5,13},{6,14},{7,15},{8,0},{9,1},... | collective-permute-start | bytes 3145736 | tf_op jit(solution)/shard_map/ppermute | solution.py:50
  131.5 23.0 %collective-permute-start.28 = (f32[4,2,128,256]{3,2,1,0:T(8,128)S(1)}, f32[4,2,128,256]{3,2,1,0:T(8,128)S(1)}, u32[]{:S(2)}, u32[]{:S(2)}) collective-permute-start(f32[4,2,128,256]{3,2,1,0:T(8,128)S(1)} %collective-permute-done.24.rest_1_), channel_id=1, source_target_pairs={{0,8},{1,9},{2,10},{3,11},{4,12},{5,13},{6,14},{7,15},{8,0},{9,1},... | collective-permute-start | bytes 3145736 | tf_op jit(solution)/shard_map/ppermute | solution.py:50
  154.5 2.7 %collective-permute-start.30 = (f32[4,2,128,256]{3,2,1,0:T(8,128)S(1)}, f32[4,2,128,256]{3,2,1,0:T(8,128)S(1)}, u32[]{:S(2)}, u32[]{:S(2)}) collective-permute-start(f32[4,2,128,256]{3,2,1,0:T(8,128)S(1)} %collective-permute-done.26.rest_3_), channel_id=1, source_target_pairs={{0,8},{1,9},{2,10},{3,11},{4,12},{5,13},{6,14},{7,15},{8,0},{9,1},... | collective-permute-start | bytes 3145736 | tf_op jit(solution)/shard_map/ppermute | solution.py:50
  (24 other events, 291.5 us)
